TPU v7x, 128 devices: a whole 4x4x4 slice. The times are simulated.
128 devices in a mesh: expert: 16 (over x, z_lo, core), tensor: 8 (over y, z_hi).
Axes of the slice: x: 4, y: 4, z: 4 (z_hi: 2, z_lo: 2; z = z_hi * 2 + z_lo), core: 2. Of those that a mesh axis runs over, the one named last changes fastest.
Arguments:
- tokens: bfloat16 [2048, 4096], P('expert', 'tensor'), may hold values from -6 to 6
- routes: int32 [2048, 8], P('expert'), may hold values from 0 to 63, all different within a row; in each aligned block of 128 rows (0 to 127, 128 to 255, ...) at most 32 rows name the same one
- gates: float32 [2048, 8], P('expert'), may hold values from 0.05 to 1
- w_gate: bfloat16 [64, 1536, 4096], P('expert', 'tensor'), may hold values from -0.09375 to 0.09375
- w_up: bfloat16 [64, 1536, 4096], P('expert', 'tensor'), may hold values from -0.09375 to 0.09375
- w_down: bfloat16 [64, 1536, 4096], P('expert', 'tensor'), may hold values from -0.15625 to 0.15625
Outputs:
- combined: bfloat16 [2048, 4096], P('expert', 'tensor')
Inputs may be any that keep to these rules, and one draw needn't show every extreme that they name: `routes`: each row names 8 different experts; within the rows of one device (aligned blocks of 128 rows) no expert is named by more than 32 rows, a bound that some block reaches.
All inputs are finite; a program needn't handle non-finite values.
Results may differ from a plain program's by a relative error of at most 0.018.
Values may be sent and summed in bfloat16 or wider, within the bound.
No kernel may reach another device: no remote copies, remote signals or barrier semaphores. Data moves between devices by JAX's collectives and lax.ppermute only.
A program may use at most 192 MiB of HBM per device.

v0:
```python
import jax
import jax.numpy as jnp
from jax import lax
from jax.sharding import PartitionSpec as P


def project_in(shard_piece, w_gate, w_up):
    gate_act = jnp.einsum("secd,efd->escf", shard_piece, w_gate, preferred_element_type=jnp.float32)
    up_act = jnp.einsum("secd,efd->escf", shard_piece, w_up, preferred_element_type=jnp.float32)
    return (gate_act, up_act)


def local(tokens, routes, gates, w_gate, w_up, w_down):
    tok_rows = tokens.shape[0]
    top_count = routes.shape[1]
    group_count = lax.axis_size("expert")
    tensor_count = lax.axis_size("tensor")
    local_experts = w_gate.shape[0]
    model_width = w_gate.shape[2]
    feature_share = model_width // tensor_count
    experts = local_experts * group_count
    capacity = 2 * tok_rows * top_count // experts
    flat_routes = routes.reshape(-1)
    onehot = (flat_routes[:, None] == jnp.arange(experts, dtype=jnp.int32)[None, :]).astype(
        jnp.int32
    )
    before = jnp.cumsum(onehot, axis=0) - onehot
    slot_index = jnp.sum(before * onehot, axis=1)
    target = flat_routes * capacity + slot_index
    owner_rows = lax.all_gather(tokens, "tensor", axis=1, tiled=True)
    buffer = (
        jnp.zeros((experts * capacity, model_width), jnp.bfloat16)
        .at[target]
        .set(jnp.repeat(owner_rows, top_count, axis=0))
    )
    received = lax.all_to_all(
        buffer.reshape(group_count, local_experts * capacity, model_width),
        "expert",
        split_axis=0,
        concat_axis=0,
        tiled=True,
    )
    received = received.reshape(group_count, local_experts, capacity, model_width)
    gate_act, up_act = project_in(received, w_gate, w_up)
    hidden = (jax.nn.silu(gate_act) * up_act).astype(jnp.bfloat16)
    partials = jnp.einsum(
        "escf,efd->secd", hidden, w_down, preferred_element_type=jnp.float32
    ).astype(jnp.bfloat16)
    returned = lax.all_to_all(
        partials.reshape(group_count, local_experts * capacity, model_width),
        "expert",
        split_axis=0,
        concat_axis=0,
        tiled=True,
    )
    picked = returned.reshape(experts * capacity, model_width)[target].astype(jnp.float32)
    summed = lax.psum_scatter(
        picked.astype(jnp.bfloat16), "tensor", scatter_dimension=1, tiled=True
    ).astype(jnp.float32)
    combined = jnp.sum(
        gates[:, :, None] * summed.reshape(tok_rows, top_count, feature_share), axis=1
    )
    return combined.astype(jnp.bfloat16)


def solution(mesh):
    placed = (
        P("expert", "tensor"),
        P("expert", None),
        P("expert", None),
        P("expert", "tensor", None),
        P("expert", "tensor", None),
        P("expert", "tensor", None),
    )
    return jax.shard_map(
        local, mesh=mesh, in_specs=placed, out_specs=P("expert", "tensor"), check_vma=False
    )
```

profile of v0, /device:TPU:32, one launch (start us, length us, event | category | flops | bytes accessed | tf_op | source)
XLA Modules:
  0.0 743.5 jit_solution(3039535908782076998)
XLA Ops:
  6.5 0.0 all-gather.2.cloned.1.call-start
  6.5 0.7 all-gather.2.cloned.1.call-update
  7.3 0.8 copy.10
  8.0 0.1 eq.29
  8.1 0.1 eq.25
  8.3 18.0 %reduce-window.6 = s32[64,8,128]{2,1,0:T(8,128)S(1)} reduce-window(s32[64,8,128]{2,1,0:T(8,128)S(1)} %fusion.24, s32[]{:T(128)} %constant.8.clone.1), window={size=1x1x128 pad=0_0x0_0x127_0}, to_apply=%region_0.0 | reduce-window | flops 8323072 | bytes 524292 | tf_op jit(solution)/shard_map/reduce-window
  26.3 0.1 slice.10
  26.4 0.1 copy.12
  26.6 0.1 copy.13
  26.7 0.7 broadcast_multiply_fusion
  27.4 0.1 copy.9
  27.5 0.1 mul.37
  27.6 0.1 broadcast_add_fusion
  27.7 0.1 fusion.23
  27.8 31.3 %all-gather.2.cloned.1.call-done = bf16[128,4096]{1,0:T(8,128)(2,1)} async-done(((bf16[128,512]{1,0:T(8,128)(2,1)}), bf16[128,4096]{1,0:T(8,128)(2,1)}) %all-gather.2.cloned.1.call-update) | async-done | bytes 1048592 | tf_op jit(solution)/shard_map/all_gather | solution.py:30
  59.1 20.8 %scatter_custom_fusion = bf16[2048,4096]{1,0:T(8,128)(2,1)} fusion(s32[1024]{0:T(1024)S(1)} %bitcast.58, bf16[]{:T(256)} %constant.6.clone.1, bf16[128,4096]{1,0:T(8,128)(2,1)} %all-gather.2.cloned.1.call-done), kind=kCustom, calls=%fused_computation.7 | custom fusion | bytes 17825794 | tf_op jit(solution)/shard_map/scatter | solution.py:34
  79.9 190.6 %all_to_all.10 = bf16[16,128,4096]{2,1,0:T(8,128)(2,1)} all-to-all(bf16[16,128,4096]{2,1,0:T(8,128)(2,1)} %bitcast.51), channel_id=1, replica_groups=mesh['expert'=16,'tensor'=8] {'expert'}, dimensions={0} | all-to-all | bytes 33554432 | tf_op jit(solution)/shard_map/all_to_all | solution.py:36
  270.5 9.9 %fusion = f32[4,16,32,192]{3,2,1,0:T(8,128)S(1)} fusion(bf16[16,4,32,4096]{3,2,1,0:T(8,128)(2,1)} %bitcast.53, bf16[4,192,4096]{2,1,0:T(8,128)(2,1)} %param.10), kind=kOutput, calls=%fused_computation.3 | convolution fusion | flops 3221225472 | bytes 24641536 | tf_op jit(solution)/shard_map/secd,efd->escf/dot_general | solution.py:9
  280.5 25.2 %convert_bitcast_fusion = bf16[16,4,32,4096]{3,2,0,1:T(8,128)(2,1)} fusion(bf16[4,192,4096]{2,1,0:T(8,128)(2,1)} %param.11, f32[4,16,32,192]{3,2,1,0:T(8,128)S(1)} %fusion, bf16[4,192,4096]{2,1,0:T(8,128)(2,1)} %param.9, bf16[16,4,32,4096]{3,2,1,0:T(8,128)(2,1)} %bitcast.54), kind=kOutput, calls=%fused_computation.2 | convolution fusion | flops 6453198848 | bytes 47710208 | tf_op jit(solution)/shard_map/escf,efd->secd/dot_general | solution.py:46
  305.7 14.0 %copy.15 = bf16[16,4,32,4096]{3,2,1,0:T(8,128)(2,1)} copy(bf16[16,4,32,4096]{3,2,0,1:T(8,128)(2,1)} %convert_bitcast_fusion) | data formatting | bytes 33554432 | tf_op jit(solution)/shard_map/convert_element_type | solution.py:48
  319.7 6.6 all-to-all-start.1
  326.3 0.3 reduce-scatter.2.cloned.1.call-start
  326.5 248.6 %all-to-all-done.1 = bf16[16,128,4096]{2,1,0:T(8,128)(2,1)} async-done(((bf16[16,128,4096]{2,1,0:T(8,128)(2,1)}), bf16[16,128,4096]{2,1,0:T(8,128)(2,1)}, u32[]{:S(2)}, u32[]{:S(2)}) %all-to-all-start.1) | async-done | bytes 16777248 | tf_op jit(solution)/shard_map/all_to_all | solution.py:49
  575.1 23.0 %gather_fusion = bf16[1024,4096]{1,0:T(8,128)(2,1)} fusion(bf16[2048,4096]{1,0:T(8,128)(2,1)} %bitcast.15, s32[1024]{0:T(1024)S(1)} %broadcast_clamp_fusion), kind=kCustom, calls=%fused_computation | custom fusion | bytes 16781312 | tf_op jit(solution)/shard_map/gather | solution.py:56
  598.1 0.0 copy-start
  598.1 0.0 reduce-scatter.2.cloned.1.call-update
  598.2 0.7 copy-done
  598.8 0.1 copy.8
  598.9 135.2 %reduce-scatter.2.cloned.1.call-done = bf16[1024,512]{1,0:T(8,128)(2,1)} async-done(((bf16[1024,4096]{1,0:T(8,128)(2,1)}), bf16[1024,512]{1,0:T(8,128)(2,1)}) %reduce-scatter.2.cloned.1.call-update) | async-done | bytes 1048592 | tf_op jit(solution)/shard_map/reduce_scatter | solution.py:57
  734.1 2.6 fusion.11
  (5 shorter events, 0.1 us)
Async XLA Ops:
  6.5 52.5 %all-gather.2.cloned.1.call-start = ((), (), s32[]{:S(2)}) async-start(), calls=%async_computation.3 | async-start | bytes 1179648 | tf_op jit(solution)/shard_map/all_gather | solution.py:30
  319.7 255.5 %all-to-all-start.1 = ((bf16[16,128,4096]{2,1,0:T(8,128)(2,1)}), bf16[16,128,4096]{2,1,0:T(8,128)(2,1)}, u32[]{:S(2)}, u32[]{:S(2)}) async-start(bf16[16,128,4096]{2,1,0:T(8,128)(2,1)} %bitcast.52), calls=%async_computation.1 | async-start | bytes 33554432 | tf_op jit(solution)/shard_map/all_to_all | solution.py:49
  326.3 407.8 %reduce-scatter.2.cloned.1.call-start = ((), (), s32[]{:S(2)}) async-start(), calls=%async_computation.4 | async-start | bytes 9437184 | tf_op jit(solution)/shard_map/reduce_scatter | solution.py:57
  598.1 0.7 copy-start
Sparse Core Ops, SparseCore 0:
  9.5 49.4 all-gather.1
  598.3 135.7 reduce-scatter.1
where the time goes:
time: 746 us; the launch traced here: 744 us
  waiting for transfers between devices  416 us (56%)
  blocking collectives  191 us (26%)
  local copies, waits for them, and re-layouts  60.1 us (8%)
  matrix products  35.2 us (5%)
  other arithmetic  21.6 us (3%)
  between operations  13.5 us (2%)
    all_to_all x1, waiting for transfers between devices, local(): lax.all_to_all(partials.reshape(group_count, local_experts * capacity, mo...  249 us
    all_to_all x1, blocking collectives, local(): lax.all_to_all(buffer.reshape(group_count, local_experts * capacity, mode...  191 us
    reduce_scatter x1, waiting for transfers between devices, local(): lax.psum_scatter(picked.astype(jnp.bfloat16), 'tensor', scatter_dimension...  135 us
    all_gather x1, waiting for transfers between devices, local(): owner_rows = lax.all_gather(tokens, 'tensor', axis=1, tiled=True)  31.3 us
    dot_general x1, matrix products, local(): jnp.einsum('escf,efd->secd', hidden, w_down, preferred_element_type=jnp.f...  25.2 us
    gather x1, local copies, waits for them, and re-layouts, local(): returned.reshape(experts * capacity, model_width)[target]  23 us
    scatter x1, local copies, waits for them, and re-layouts, local(): buffer = jnp.zeros((experts * capacity, model_width), jnp.bfloat16).at[ta...  20.8 us
    another operation x3, other arithmetic  18.2 us
  transfers between devices with their start and end apart: 3, of which 3 were waited for; matrix products, arithmetic and copies ran while one was open for 3% of the time, Pallas kernels for 0%

commit v1 on v0

v1 whole, which is shorter than its diff:
```python
import functools

import jax
import jax.numpy as jnp
from jax import lax
from jax.experimental import pallas as pl
from jax.experimental.pallas import tpu as pltpu
from jax.sharding import PartitionSpec as P

AXES = ("expert", "tensor")
ROWS = (48, 48, 32)
FIRST = (0, 48, 96)
BF16 = jnp.bfloat16
F32 = jnp.float32


def device_number(x, y, z, core):
    return (x * 4 + (z % 2) * 2 + core) * 8 + y * 2 + z // 2


def places():
    return [(x, y, z, c) for x in range(4) for y in range(4) for z in range(4) for c in range(2)]


def ring_pairs(dim, sub):
    pairs = []
    for place in places():
        other = list(place)
        other[dim] ^= 1 if sub == place[3] else 3
        pairs.append((device_number(*place), device_number(*other)))
    return pairs


def core_pairs():
    return [(device_number(x, y, z, c), device_number(x, y, z, 1 - c)) for x, y, z, c in places()]


def swap(value, dim, sub):
    return lax.ppermute(value, AXES, ring_pairs(dim, sub))


def gather_tokens(tokens):
    parts = [tokens[first : first + rows][None] for first, rows in zip(FIRST, ROWS)]
    for phase in (0, 1):
        for sub in (0, 1):
            got = [swap(part, (i + phase) % 3, sub) for i, part in enumerate(parts)]
            parts = [jnp.concatenate([part, new], 0) for part, new in zip(parts, got)]
    one = [swap(part, (i + 2) % 3, 0) for i, part in enumerate(parts)]
    two = [swap(part, (i + 2) % 3, 1) for i, part in enumerate(parts)]
    three = [swap(part, (i + 2) % 3, 1) for i, part in enumerate(one)]
    return [list(pieces) for pieces in zip(parts, one, two, three)]


def scatter_sums(parts):
    far = [swap(p[2], (i + 2) % 3, 1) for i, p in enumerate(parts)]
    side = [swap(p[3], (i + 2) % 3, 1) for i, p in enumerate(parts)]
    near = [p[1] + s for p, s in zip(parts, side)]
    got = [swap(p, (i + 2) % 3, 0) for i, p in enumerate(near)]
    held = [p[0] + s + r for p, s, r in zip(parts, far, got)]
    for phase in (1, 0):
        for sub in (1, 0):
            half = held[0].shape[0] // 2
            got = [swap(p[half:], (i + phase) % 3, sub) for i, p in enumerate(held)]
            held = [p[:half] + r for p, r in zip(held, got)]
    return jnp.concatenate([p[0] for p in held], 0)


def z_place(low, high, core):
    if low == 0:
        return 3 * high
    return 1 + (high ^ core)


def x_copies(sc_ref, x_refs, x_all, sem):
    core = sc_ref[8]
    copies = []

    def column(ky, kz):
        if kz == 0 or kz == 3:
            f = sc_ref[ky * 2 + kz // 3]
        else:
            f = sc_ref[ky * 2 + ((kz - 1) ^ core)]
        return pl.ds(pl.multiple_of(f * 512, 512), 512)

    for i in range(3):
        rows = pl.ds(FIRST[i], ROWS[i])
        for k3 in range(4):
            src = x_refs[i * 4 + k3]
            for k in range(4):
                if i == 0:
                    kz, ky = k3, k
                    low = (0, 1, 1, 0)[kz]
                    copies.append((src.at[ky], x_all.at[:, low, rows, column(ky, kz)]))
                elif i == 1:
                    kx, kz = k3, k
                    low = (0, 1, 1, 0)[kz]
                    for ky in range(4):
                        copies.append((src.at[kz, ky], x_all.at[kx, low, rows, column(ky, kz)]))
                else:
                    ky, kz = k3, k
                    low = (0, 1, 1, 0)[kz]
                    copies.append((src.at[:, kz], x_all.at[:, low, rows, column(ky, kz)]))
    return [pltpu.make_async_copy(a, b, sem.at[n]) for n, (a, b) in enumerate(copies)]


N_X_COPIES = 96


def hidden_kernel(sc_ref, p_ref, q_ref, gs_ref, wg, wu, wg2, wu2, *rest):
    x_refs = rest[:12]
    hd_ref, x_all, xd, wbuf, hp, x_sem, w_sem = rest[12:]

    def fetch(pair, j, gate, up):
        e = lax.rem(pair, 2) * 2 + j
        return [
            pltpu.make_async_copy(gate.at[e], wbuf.at[j, pl.ds(0, 192)], w_sem.at[j, 0]),
            pltpu.make_async_copy(up.at[e], wbuf.at[j, pl.ds(192, 192)], w_sem.at[j, 1]),
        ]

    x_in = x_copies(sc_ref, x_refs, x_all, x_sem)
    for copy in x_in:
        copy.start()
    for j in range(2):
        for copy in fetch(0, j, wg, wu):
            copy.start()
    hp[...] = jnp.zeros_like(hp)
    for copy in x_in:
        copy.wait()

    def dispatch(n, carry):
        b = n // 8
        col = pl.ds(pl.multiple_of(lax.rem(n, 8) * 512, 512), 512)
        rows = jnp.dot(p_ref[b], x_all[b // 2, lax.rem(b, 2), :, col], preferred_element_type=F32)
        xd[:, pl.ds(pl.multiple_of(b * 32, 32), 32), col] = rows.astype(BF16).reshape(8, 32, 512)
        return carry

    lax.fori_loop(0, 64, dispatch, 0)

    def experts(pair, carry):
        for j in range(2):
            e = pair * 2 + j
            for copy in fetch(pair, j, wg, wu):
                copy.wait()
            act = lax.dot_general(
                wbuf[j], xd[e], (((1,), (1,)), ((), ())), preferred_element_type=F32
            )
            gate, up = act[:192], act[192:]
            hidden = gate / (1.0 + jnp.exp(-gate)) * up * gs_ref[e]
            hp[pl.ds(j * 192, 192), pl.ds(j * 256, 256)] = hidden.astype(BF16)

            @pl.when(pair == 0)
            def _():
                for copy in fetch(pair + 1, j, wg, wu):
                    copy.start()

            @pl.when((pair == 1) | (pair == 2))
            def _():
                for copy in fetch(pair + 1, j, wg2, wu2):
                    copy.start()

        def spread(r, c2):
            rows = pl.ds(pl.multiple_of(r * 256, 256), 256)
            out = lax.dot_general(
                q_ref[rows, pl.ds(pl.multiple_of(pair * 512, 512), 512)],
                hp[...],
                (((1,), (1,)), ((), ())),
                preferred_element_type=F32,
            )
            hd_ref[rows, pl.ds(pl.multiple_of(pair * 384, 128), 384)] = out.astype(BF16)
            return c2

        lax.fori_loop(0, 4, spread, 0)
        return carry

    lax.fori_loop(0, 4, experts, 0)


def down_kernel(sc_ref, hd_ref, wd, wd2, *rest):
    outs = rest[:12]
    wbuf, ybuf, w_sem, y_sem = rest[12:]
    core = sc_ref[8]

    def fetch(f):
        slot = f % 2
        col = pl.ds(pl.multiple_of(sc_ref[f] * 512, 512), 512)
        return [
            pltpu.make_async_copy(wd.at[:, :, col], wbuf.at[slot, pl.ds(0, 4)], w_sem.at[slot, 0]),
            pltpu.make_async_copy(wd2.at[:, :, col], wbuf.at[slot, pl.ds(4, 4)], w_sem.at[slot, 1]),
        ]

    def stores(f, turn):
        slot, ky, high = f % 2, f // 2, f % 2
        y = ybuf.at[slot]
        copies = []
        for low in range(2):
            kz = z_place(low, high, turn if turn is not None else core)
            rows = [pl.ds(FIRST[i], ROWS[i]) for i in range(3)]
            if turn is not None and low == 1:
                copies.append((y.at[:, low, rows[0]], outs[kz].at[ky]))
            if turn is None:
                if low == 0:
                    copies.append((y.at[:, low, rows[0]], outs[kz].at[ky]))
                for kx in range(4):
                    copies.append((y.at[kx, low, rows[1]], outs[4 + kx].at[kz, ky]))
                copies.append((y.at[:, low, rows[2]], outs[8 + ky].at[:, kz]))
        first = 0 if turn is None else 11
        return [
            pltpu.make_async_copy(a, b, y_sem.at[slot, first + n]) for n, (a, b) in enumerate(copies)
        ]

    for copy in fetch(0) + fetch(1):
        copy.start()
    for f in range(8):
        slot = f % 2
        for copy in fetch(f):
            copy.wait()
        if f >= 2:
            for copy in stores(f - 2, None) + stores(f - 2, 0):
                copy.wait()

        def rows_step(kx, carry):
            rows = pl.ds(pl.multiple_of(kx * 256, 256), 256)
            out = jnp.dot(
                hd_ref[rows], wbuf[slot].reshape(1536, 512), preferred_element_type=F32
            )
            ybuf[slot, kx] = out.astype(BF16).reshape(2, 128, 512)
            return carry

        lax.fori_loop(0, 4, rows_step, 0)
        if f < 6:
            for copy in fetch(f + 2):
                copy.start()
        for copy in stores(f, None):
            copy.start()
        for turn in range(2):

            @pl.when(core == turn)
            def _():
                for copy in stores(f, turn):
                    copy.start()

    for f in (6, 7):
        for copy in stores(f, None) + stores(f, 0):
            copy.wait()


def local(tokens, routes, gates, w_gate, w_up, w_down):
    e, t = lax.axis_index("expert"), lax.axis_index("tensor")
    x, zlo, core, y, zhi = e // 4, e // 2 % 2, e % 2, t // 2, t % 2
    offs = [0, jnp.where(core == 0, 1, 3), jnp.where(core == 0, 3, 1), 2]

    wg2, wu2, wd2 = [lax.ppermute(w, AXES, core_pairs()) for w in (w_gate, w_up, w_down)]

    packed = jnp.concatenate([routes.astype(F32), gates], axis=1)
    spread = lax.all_gather(packed, "expert")
    blocks = jnp.stack(
        [(x ^ offs[kx]) * 4 + (zlo ^ low) * 2 + core for kx in range(4) for low in range(2)]
    )
    mine = jnp.take(spread, blocks, axis=0)
    ids = jnp.concatenate([e * 4 + jnp.arange(4), (e ^ 1) * 4 + jnp.arange(4)]).astype(F32)
    hit = mine[:, :, None, :8] == ids[None, None, :, None]
    named = jnp.any(hit, axis=3).astype(BF16)
    weight = jnp.sum(jnp.where(hit, mine[:, :, None, 8:], 0.0), axis=3)
    earlier = (jnp.arange(128)[:, None] < jnp.arange(128)[None, :]).astype(BF16)
    slot = jnp.einsum("bte,ts->bse", named, earlier, preferred_element_type=F32)
    slot = jnp.where(named > 0, slot, -1.0)
    slots = jnp.arange(32, dtype=F32)
    chosen = jnp.swapaxes(slot, 1, 2)[:, :, None, :] == slots[None, None, :, None]
    p_mat = chosen.astype(BF16).reshape(8, 256, 128)
    gslot = jnp.sum(jnp.where(chosen, jnp.swapaxes(weight, 1, 2)[:, :, None, :], 0.0), axis=3)
    gslot = jnp.swapaxes(gslot, 0, 1).reshape(8, 1, 256)
    wide = jnp.arange(256)
    q_mat = (slot[..., None] == (wide % 32).astype(F32)) & (
        wide // 32 == jnp.arange(8)[:, None, None, None]
    )
    q_mat = q_mat.astype(BF16).reshape(1024, 2048)

    scalars = jnp.stack(
        [(y ^ offs[ky]) * 2 + (zhi ^ high) for ky in range(4) for high in range(2)] + [core]
    ).astype(jnp.int32)

    parts = gather_tokens(tokens)
    pieces = [
        piece.reshape(4, 4, ROWS[i], 512) for i, part in enumerate(parts) for piece in part
    ]
    smem = pl.BlockSpec(memory_space=pltpu.SMEM)
    vmem = pl.BlockSpec(memory_space=pltpu.VMEM)
    hbm = pl.BlockSpec(memory_space=pl.ANY)
    hidden = pl.pallas_call(
        hidden_kernel,
        out_shape=jax.ShapeDtypeStruct((1024, 1536), BF16),
        in_specs=[smem, vmem, vmem, vmem] + [hbm] * 16,
        out_specs=vmem,
        scratch_shapes=[
            pltpu.VMEM((4, 2, 128, 4096), BF16),
            pltpu.VMEM((8, 256, 4096), BF16),
            pltpu.VMEM((2, 384, 4096), BF16),
            pltpu.VMEM((384, 512), BF16),
            pltpu.SemaphoreType.DMA((N_X_COPIES,)),
            pltpu.SemaphoreType.DMA((2, 2)),
        ],
        compiler_params=pltpu.CompilerParams(vmem_limit_bytes=56 * 2**20),
        name="hidden",
    )(scalars, p_mat, q_mat, gslot, w_gate, w_up, wg2, wu2, *pieces)

    sums = pl.pallas_call(
        down_kernel,
        out_shape=[
            jax.ShapeDtypeStruct((4, 4, ROWS[i], 512), BF16) for i in range(3) for _ in range(4)
        ],
        in_specs=[smem, vmem, hbm, hbm],
        out_specs=[hbm] * 12,
        scratch_shapes=[
            pltpu.VMEM((2, 8, 192, 512), BF16),
            pltpu.VMEM((2, 4, 2, 128, 512), BF16),
            pltpu.SemaphoreType.DMA((2, 2)),
            pltpu.SemaphoreType.DMA((2, 12)),
        ],
        compiler_params=pltpu.CompilerParams(vmem_limit_bytes=56 * 2**20),
        name="down",
    )(scalars, hidden, w_down, wd2)
    parts = [
        [sums[i * 4 + k].reshape(16, ROWS[i], 512) for k in range(4)] for i in range(3)
    ]
    return scatter_sums(parts)


def solution(mesh):
    placed = (
        P("expert", "tensor"),
        P("expert", None),
        P("expert", None),
        P("expert", "tensor", None),
        P("expert", "tensor", None),
        P("expert", "tensor", None),
    )
    return jax.shard_map(
        local, mesh=mesh, in_specs=placed, out_specs=P("expert", "tensor"), check_vma=False
    )
```

time: 746 us -> 315 us (0.42)
  waiting for transfers between devices: 416 us -> 119 us
  blocking collectives: 191 us -> 30.5 us
  Pallas kernels: 0 us -> 65.2 us
  starting transfers between devices: 6.84 us -> 65.4 us
  local copies, waits for them, and re-layouts: 60.1 us -> 18 us
  matrix products: 35.2 us -> 0.14 us
  between operations: 13.5 us -> 0.61 us
    all_to_all x1 -> x0, waiting for transfers between devices: 249 us -> none  [local(): lax.all_to_all(partials.reshape(group_count, local_experts * capacity, mo...]
    all_to_all x1 -> x0, blocking collectives: 191 us -> none  [local(): lax.all_to_all(buffer.reshape(group_count, local_experts * capacity, mode...]
    reduce_scatter x1 -> x0, waiting for transfers between devices: 135 us -> none  [local(): lax.psum_scatter(picked.astype(jnp.bfloat16), 'tensor', scatter_dimension...]
    ppermute x0 -> x45, waiting for transfers between devices: none -> 119 us  [the longest x42 119 us: swap(): return lax.ppermute(value, AXES, ring_pairs(dim, sub))]
    ppermute x0 -> x45, starting transfers between devices: none -> 65.4 us  [the longest x42 62.5 us: swap(): return lax.ppermute(value, AXES, ring_pairs(dim, sub))]
    pallas_call x0 -> x2, Pallas kernels: none -> 65.2 us  [the longest x1 42.2 us: local(): pl.pallas_call(hidden_kernel, out_shape=jax.ShapeDtypeStruct((1024, 1536)...]
    dot_general x2 -> x0, matrix products: 35.2 us -> none  [the longest x1 25.2 us: local(): jnp.einsum('escf,efd->secd', hidden, w_down, preferred_element_type=jnp.f...]
    all_gather x1 -> x0, waiting for transfers between devices: 31.3 us -> none  [local(): owner_rows = lax.all_gather(tokens, 'tensor', axis=1, tiled=True)]
  transfers between devices with their start and end apart: 3 -> 45, of which waited for: 3 -> 26; matrix products, arithmetic and copies ran while one was open for 3% -> 10% of each run, Pallas kernels for 0% -> 13%
where the time goes in v1:
time: 315 us
  waiting for transfers between devices  119 us (38%)
  starting transfers between devices  65.4 us (21%)
  Pallas kernels  65.2 us (21%)
  blocking collectives  30.5 us (10%)
  local copies, waits for them, and re-layouts  18 us (6%)
  other arithmetic  15.3 us (5%)
    ppermute x42, waiting for transfers between devices, swap(): return lax.ppermute(value, AXES, ring_pairs(dim, sub))  119 us
    ppermute x42, starting transfers between devices, swap(): return lax.ppermute(value, AXES, ring_pairs(dim, sub))  62.5 us
    pallas_call x1, Pallas kernels, local(): pl.pallas_call(hidden_kernel, out_shape=jax.ShapeDtypeStruct((1024, 1536)...  42.2 us
    all_gather x1, blocking collectives, local(): spread = lax.all_gather(packed, 'expert')  30.5 us
    pallas_call x1, Pallas kernels, local(): pl.pallas_call(down_kernel, out_shape=[jax.ShapeDtypeStruct((4, 4, ROWS[i...  23 us
    unnamed x41, local copies, waits for them, and re-layouts  11.4 us
    convert_element_type x1, other arithmetic, local(): q_mat = q_mat.astype(BF16).reshape(1024, 2048)  7.09 us
  transfers between devices with their start and end apart: 45, of which 26 were waited for; matrix products, arithmetic and copies ran while one was open for 10% of the time, Pallas kernels for 13%

profile of v1, /device:TPU:32, one launch (start us, length us, event | category | flops | bytes accessed | tf_op | source)
XLA Modules:
  0.0 314.5 jit_solution(11298379862074415659)
XLA Ops:
  7.5 30.5 %all-gather = f32[2048,16]{0,1:T(8,128)S(1)} all-gather(f32[128,16]{0,1:T(8,128)S(1)} %pad_maximum_fusion.10), channel_id=2, replica_groups=mesh['expert'=16,'tensor'=8] {'expert'}, dimensions={0}, use_global_device_ids=true | all-gather | bytes 139264 | tf_op jit(solution)/shard_map/all_gather | solution.py:255
  44.1 3.0 collective-permute-done.17
  47.9 5.8 %collective-permute-done.3 = bf16[2,48,512]{2,1,0:T(8,128)(2,1)S(1)} collective-permute-done((bf16[2,48,512]{2,1,0:T(8,128)(2,1)S(1)}, bf16[2,48,512]{2,1,0:T(8,128)(2,1)S(1)}, u32[]{:S(2)}, u32[]{:S(2)}) %collective-permute-start.3) | collective-permute-done | bytes 98336 | tf_op jit(solution)/shard_map/ppermute | solution.py:39
  55.5 4.3 %collective-permute-done.4 = bf16[4,48,512]{2,1,0:T(8,128)(2,1)S(1)} collective-permute-done((bf16[4,48,512]{2,1,0:T(8,128)(2,1)S(1)}, bf16[4,48,512]{2,1,0:T(8,128)(2,1)S(1)}, u32[]{:S(2)}, u32[]{:S(2)}) %collective-permute-start.4) | collective-permute-done | bytes 196640 | tf_op jit(solution)/shard_map/ppermute | solution.py:39
  61.8 3.8 %collective-permute-done.10 = bf16[2,48,512]{2,1,0:T(8,128)(2,1)S(1)} collective-permute-done((bf16[2,48,512]{2,1,0:T(8,128)(2,1)S(1)}, bf16[2,48,512]{2,1,0:T(8,128)(2,1)S(1)}, u32[]{:S(2)}, u32[]{:S(2)}) %collective-permute-start.10) | collective-permute-done | bytes 98336 | tf_op jit(solution)/shard_map/ppermute | solution.py:39
  68.8 6.7 %collective-permute-done.11 = bf16[4,48,512]{2,1,0:T(8,128)(2,1)S(1)} collective-permute-done((bf16[4,48,512]{2,1,0:T(8,128)(2,1)S(1)}, bf16[4,48,512]{2,1,0:T(8,128)(2,1)S(1)}, u32[]{:S(2)}, u32[]{:S(2)}) %collective-permute-start.11) | collective-permute-done | bytes 196640 | tf_op jit(solution)/shard_map/ppermute | solution.py:39
  75.6 3.2 %collective-permute-done.5 = bf16[8,48,512]{2,1,0:T(8,128)(2,1)S(1)} collective-permute-done((bf16[8,48,512]{2,1,0:T(8,128)(2,1)S(1)}, bf16[8,48,512]{2,1,0:T(8,128)(2,1)S(1)}, u32[]{:S(2)}, u32[]{:S(2)}) %collective-permute-start.5) | collective-permute-done | bytes 393248 | tf_op jit(solution)/shard_map/ppermute | solution.py:39
  80.1 10.5 %collective-permute-done.12 = bf16[8,48,512]{2,1,0:T(8,128)(2,1)S(1)} collective-permute-done((bf16[8,48,512]{2,1,0:T(8,128)(2,1)S(1)}, bf16[8,48,512]{2,1,0:T(8,128)(2,1)S(1)}, u32[]{:S(2)}, u32[]{:S(2)}) %collective-permute-start.12) | collective-permute-done | bytes 393248 | tf_op jit(solution)/shard_map/ppermute | solution.py:39
  95.1 5.9 %collective-permute-done.21 = bf16[16,32,512]{2,1,0:T(8,128)(2,1)S(1)} collective-permute-done((bf16[16,32,512]{2,1,0:T(8,128)(2,1)S(1)}, bf16[16,32,512]{2,1,0:T(8,128)(2,1)S(1)}, u32[]{:S(2)}, u32[]{:S(2)}) %collective-permute-start.21) | collective-permute-done | bytes 524320 | tf_op jit(solution)/shard_map/ppermute | solution.py:39
  101.3 10.3 %collective-permute-done.6 = bf16[16,48,512]{2,1,0:T(8,128)(2,1)S(1)} collective-permute-done((bf16[16,48,512]{2,1,0:T(8,128)(2,1)S(1)}, bf16[16,48,512]{2,1,0:T(8,128)(2,1)S(1)}, u32[]{:S(2)}, u32[]{:S(2)}) %collective-permute-start.6) | collective-permute-done | bytes 786464 | tf_op jit(solution)/shard_map/ppermute | solution.py:39
  111.6 2.9 collective-permute-start.7
  114.6 6.6 %collective-permute-done.13 = bf16[16,48,512]{2,1,0:T(8,128)(2,1)S(1)} collective-permute-done((bf16[16,48,512]{2,1,0:T(8,128)(2,1)S(1)}, bf16[16,48,512]{2,1,0:T(8,128)(2,1)S(1)}, u32[]{:S(2)}, u32[]{:S(2)}) %collective-permute-start.13) | collective-permute-done | bytes 786464 | tf_op jit(solution)/shard_map/ppermute | solution.py:39
  127.8 7.4 %copy.26 = f32[128,8,8,256]{3,1,2,0:T(8,128)} copy(f32[128,8,8,256]{3,2,1,0:T(8,128)S(1)} %bitcast.118) | data formatting | bytes 16777216
  141.1 3.6 %collective-permute-start.15 = (bf16[16,48,512]{2,1,0:T(8,128)(2,1)}, bf16[16,48,512]{2,1,0:T(8,128)(2,1)S(1)}, u32[]{:S(2)}, u32[]{:S(2)}) collective-permute-start(bf16[16,48,512]{2,1,0:T(8,128)(2,1)} %copy-done.6), channel_id=1, source_target_pairs={{0,96},{8,40},{16,112},{24,56},{1,97},{9,41},{17,113},{25,57},{2,9... | collective-permute-start | bytes 2359304 | tf_op jit(solution)/shard_map/ppermute | solution.py:39
  144.8 7.1 %and_convert_fusion.q_ref = bf16[1024,2048]{1,0:T(8,128)(2,1)} fusion(pred[1024,2048]{1,0:T(8,128)(4,1)S(1)} %bitcast.119, f32[1024,2048]{1,0:T(8,128)} %bitcast.117, f32[2048]{0:T(1024)S(1)} %bitcast.132), kind=kLoop, calls=%fused_computation.1 | loop fusion | flops 6291456 | bytes 14688256 | tf_op jit(solution)/shard_map/convert_element_type | solution.py:276
  152.2 2.7 collective-permute-done.15
  155.9 42.2 %hidden.1.hd_ref = bf16[1024,1536]{1,0:T(8,128)(2,1)} custom-call(s32[9]{0:T(128)} %stack.84.sc_ref, bf16[8,256,128]{2,1,0:T(8,128)(2,1)} %fusion.p_ref, bf16[1024,2048]{1,0:T(8,128)(2,1)} %and_convert_fusion.q_ref, f32[8,1,256]{2,1,0:T(1,128)} %reshape.494.gs_ref, bf16[4,192,4096]{2,1,0:T(8,128)(2,1)} %wg.1, bf16[4,192,4096]{2,1,0:T(8,128)(2,1)} %wu.1, ...), custom_call_target="tpu_custom_call" | custom-call | tf_op jit(solution)/shard_map/hidden/pallas_call | solution.py:289
  198.1 23.0 %down.1 = (bf16[4,4,48,512]{3,2,1,0:T(8,128)(2,1)}, bf16[4,4,48,512]{3,2,1,0:T(8,128)(2,1)}, bf16[4,4,48,512]{3,2,1,0:T(8,128)(2,1)}, bf16[4,4,48,512]{3,2,1,0:T...) custom-call(s32[9]{0:T(128)} %stack.84.sc_ref, ...), custom_call_target="tpu_custom_call" | custom-call | tf_op jit(solution)/shard_map/down/pallas_call | solution.py:306
  224.5 7.4 %collective-permute-done.39 = bf16[16,32,512]{2,1,0:T(8,128)(2,1)S(1)} collective-permute-done((bf16[16,32,512]{2,1,0:T(8,128)(2,1)}, bf16[16,32,512]{2,1,0:T(8,128)(2,1)S(1)}, u32[]{:S(2)}, u32[]{:S(2)}) %collective-permute-start.39) | collective-permute-done | bytes 524320 | tf_op jit(solution)/shard_map/ppermute | solution.py:39
  235.1 3.2 %collective-permute-start.32 = (bf16[16,48,512]{2,1,0:T(8,128)(2,1)}, bf16[16,48,512]{2,1,0:T(8,128)(2,1)S(1)}, u32[]{:S(2)}, u32[]{:S(2)}) collective-permute-start(bf16[16,48,512]{2,1,0:T(8,128)(2,1)} %bitcast.135), channel_id=1, source_target_pairs={{0,96},{8,40},{16,112},{24,56},{1,97},{9,41},{17,113},{25,57},{2,9... | collective-permute-start | bytes 2359304 | tf_op jit(solution)/shard_map/ppermute | solution.py:39
  243.4 3.3 %collective-permute-start.41 = (bf16[8,32,512]{2,1,0:T(8,128)(2,1)S(1)}, bf16[8,32,512]{2,1,0:T(8,128)(2,1)S(1)}, u32[]{:S(2)}, u32[]{:S(2)}) collective-permute-start(bf16[8,32,512]{2,1,0:T(8,128)(2,1)S(1)} %slice.137), channel_id=1, source_target_pairs={{0,96},{8,40},{16,112},{24,56},{1,97},{9,41},{17,113},{25,57},{2,9... | collective-permute-start | bytes 786440 | tf_op jit(solution)/shard_map/ppermute | solution.py:39
  246.7 4.6 %collective-permute-done.25 = bf16[16,48,512]{2,1,0:T(8,128)(2,1)S(1)} collective-permute-done((bf16[16,48,512]{2,1,0:T(8,128)(2,1)}, bf16[16,48,512]{2,1,0:T(8,128)(2,1)S(1)}, u32[]{:S(2)}, u32[]{:S(2)}) %collective-permute-start.25) | collective-permute-done | bytes 786464 | tf_op jit(solution)/shard_map/ppermute | solution.py:39
  252.9 16.7 %collective-permute-done.41 = bf16[8,32,512]{2,1,0:T(8,128)(2,1)S(1)} collective-permute-done((bf16[8,32,512]{2,1,0:T(8,128)(2,1)S(1)}, bf16[8,32,512]{2,1,0:T(8,128)(2,1)S(1)}, u32[]{:S(2)}, u32[]{:S(2)}) %collective-permute-start.41) | collective-permute-done | bytes 262176 | tf_op jit(solution)/shard_map/ppermute | solution.py:39
  272.0 2.7 collective-permute-done.42
  276.3 2.8 collective-permute-done.43
  279.1 6.5 %collective-permute-start.44 = (bf16[1,32,512]{2,1,0:T(8,128)(2,1)S(1)}, bf16[1,32,512]{2,1,0:T(8,128)(2,1)S(1)}, u32[]{:S(2)}, u32[]{:S(2)}) collective-permute-start(bf16[1,32,512]{2,1,0:T(8,128)(2,1)S(1)} %slice.143), channel_id=1, source_target_pairs={{0,16},{8,25},{16,0},{24,9},{1,17},{9,24},{17,1},{25,8},{2,18},{10... | collective-permute-start | bytes 98312 | tf_op jit(solution)/shard_map/ppermute | solution.py:39
  285.8 2.5 collective-permute-start.27
  289.0 5.9 %collective-permute-done.27 = bf16[8,48,512]{2,1,0:T(8,128)(2,1)S(1)} collective-permute-done((bf16[8,48,512]{2,1,0:T(8,128)(2,1)S(1)}, bf16[8,48,512]{2,1,0:T(8,128)(2,1)S(1)}, u32[]{:S(2)}, u32[]{:S(2)}) %collective-permute-start.27) | collective-permute-done | bytes 393248 | tf_op jit(solution)/shard_map/ppermute | solution.py:39
  297.8 2.9 collective-permute-done.28
  300.8 2.9 collective-permute-start.29
  306.8 2.9 collective-permute-done.36
  310.9 3.0 collective-permute-done.37
  (178 shorter events, 67.1 us)
Async XLA Ops:
  0.8 41.9 %collective-permute-start.2 = (bf16[1,48,512]{2,1,0:T(8,128)(2,1)S(1)}, bf16[1,48,512]{2,1,0:T(8,128)(2,1)S(1)}, u32[]{:S(2)}, u32[]{:S(2)}) collective-permute-start(bf16[1,48,512]{2,1,0:T(8,128)(2,1)S(1)} %get-tuple-element.30), channel_id=1, source_target_pairs={{0,32},{8,104},{16,48},{24,120},{1,33},{9,105},{17,49},{25,121},{2... | collective-permute-start | bytes 147464 | tf_op jit(solution)/shard_map/ppermute | solution.py:39
  3.1 38.0 %collective-permute-start.16 = (bf16[1,32,512]{2,1,0:T(8,128)(2,1)S(1)}, bf16[1,32,512]{2,1,0:T(8,128)(2,1)S(1)}, u32[]{:S(2)}, u32[]{:S(2)}) collective-permute-start(bf16[1,32,512]{2,1,0:T(8,128)(2,1)S(1)} %slice_bitcast_fusion.2), channel_id=1, source_target_pairs={{0,16},{8,25},{16,0},{24,9},{1,17},{9,24},{17,1},{25,8},{2,18},{10... | collective-permute-start | bytes 98312 | tf_op jit(solution)/shard_map/ppermute | solution.py:39
  3.3 151.7 %collective-permute-start = (bf16[4,192,4096]{2,1,0:T(8,128)(2,1)}, bf16[4,192,4096]{2,1,0:T(8,128)(2,1)}, u32[]{:S(2)}, u32[]{:S(2)}) collective-permute-start(bf16[4,192,4096]{2,1,0:T(8,128)(2,1)} %wg.1), channel_id=1, source_target_pairs={{0,8},{8,0},{16,24},{24,16},{1,9},{9,1},{17,25},{25,17},{2,10},{10... | collective-permute-start | bytes 18874376 | tf_op jit(solution)/shard_map/ppermute | solution.py:252
  5.6 149.3 %collective-permute-start.1 = (bf16[4,192,4096]{2,1,0:T(8,128)(2,1)}, bf16[4,192,4096]{2,1,0:T(8,128)(2,1)}, u32[]{:S(2)}, u32[]{:S(2)}) collective-permute-start(bf16[4,192,4096]{2,1,0:T(8,128)(2,1)} %wu.1), channel_id=1, source_target_pairs={{0,8},{8,0},{16,24},{24,16},{1,9},{9,1},{17,25},{25,17},{2,10},{10... | collective-permute-start | bytes 18874376 | tf_op jit(solution)/shard_map/ppermute | solution.py:252
  5.6 192.5 %collective-permute-start.23 = (bf16[4,192,4096]{2,1,0:T(8,128)(2,1)}, bf16[4,192,4096]{2,1,0:T(8,128)(2,1)}, u32[]{:S(2)}, u32[]{:S(2)}) collective-permute-start(bf16[4,192,4096]{2,1,0:T(8,128)(2,1)} %wd.1), channel_id=1, source_target_pairs={{0,8},{8,0},{16,24},{24,16},{1,9},{9,1},{17,25},{25,17},{2,10},{10... | collective-permute-start | bytes 18874376 | tf_op jit(solution)/shard_map/ppermute | solution.py:252
  54.1 13.5 %collective-permute-start.19 = (bf16[8,32,512]{2,1,0:T(8,128)(2,1)S(1)}, bf16[8,32,512]{2,1,0:T(8,128)(2,1)S(1)}, u32[]{:S(2)}, u32[]{:S(2)}) collective-permute-start(bf16[8,32,512]{2,1,0:T(8,128)(2,1)S(1)} %pad_maximum_fusion.2), channel_id=1, source_target_pairs={{0,96},{8,40},{16,112},{24,56},{1,97},{9,41},{17,113},{25,57},{2,9... | collective-permute-start | bytes 786440 | tf_op jit(solution)/shard_map/ppermute | solution.py:39
  65.6 13.2 %collective-permute-start.5 = (bf16[8,48,512]{2,1,0:T(8,128)(2,1)S(1)}, bf16[8,48,512]{2,1,0:T(8,128)(2,1)S(1)}, u32[]{:S(2)}, u32[]{:S(2)}) collective-permute-start(bf16[8,48,512]{2,1,0:T(8,128)(2,1)S(1)} %pad_maximum_fusion), channel_id=1, source_target_pairs={{0,6},{8,10},{16,22},{24,26},{1,7},{9,11},{17,23},{25,27},{2,4},{1... | collective-permute-start | bytes 1179656 | tf_op jit(solution)/shard_map/ppermute | solution.py:39
  67.6 7.9 %collective-permute-start.11 = (bf16[4,48,512]{2,1,0:T(8,128)(2,1)S(1)}, bf16[4,48,512]{2,1,0:T(8,128)(2,1)S(1)}, u32[]{:S(2)}, u32[]{:S(2)}) collective-permute-start(bf16[4,48,512]{2,1,0:T(8,128)(2,1)S(1)} %pad_maximum_fusion.4), channel_id=1, source_target_pairs={{0,16},{8,25},{16,0},{24,9},{1,17},{9,24},{17,1},{25,8},{2,18},{10... | collective-permute-start | bytes 589832 | tf_op jit(solution)/shard_map/ppermute | solution.py:39
  75.5 17.2 %collective-permute-start.20 = (bf16[16,32,512]{2,1,0:T(8,128)(2,1)S(1)}, bf16[16,32,512]{2,1,0:T(8,128)(2,1)}, u32[]{:S(2)}, u32[]{:S(2)}) collective-permute-start(bf16[16,32,512]{2,1,0:T(8,128)(2,1)S(1)} %constant_dynamic-update-slice_fusion.10), channel_id=1, source_target_pairs={{0,2},{8,14},{16,18},{24,30},{1,3},{9,15},{17,19},{25,31},{2,0},{1... | collective-permute-start | bytes 1572872 | tf_op jit(solution)/shard_map/ppermute | solution.py:39
  78.7 11.9 %collective-permute-start.12 = (bf16[8,48,512]{2,1,0:T(8,128)(2,1)S(1)}, bf16[8,48,512]{2,1,0:T(8,128)(2,1)S(1)}, u32[]{:S(2)}, u32[]{:S(2)}) collective-permute-start(bf16[8,48,512]{2,1,0:T(8,128)(2,1)S(1)} %pad_maximum_fusion.1), channel_id=1, source_target_pairs={{0,17},{8,24},{16,1},{24,8},{1,16},{9,25},{17,0},{25,9},{2,19},{10... | collective-permute-start | bytes 1179656 | tf_op jit(solution)/shard_map/ppermute | solution.py:39
  90.7 10.4 %collective-permute-start.21 = (bf16[16,32,512]{2,1,0:T(8,128)(2,1)S(1)}, bf16[16,32,512]{2,1,0:T(8,128)(2,1)S(1)}, u32[]{:S(2)}, u32[]{:S(2)}) collective-permute-start(bf16[16,32,512]{2,1,0:T(8,128)(2,1)S(1)} %constant_dynamic-update-slice_fusion.10), channel_id=1, source_target_pairs={{0,6},{8,10},{16,22},{24,26},{1,7},{9,11},{17,23},{25,27},{2,4},{1... | collective-permute-start | bytes 1572872 | tf_op jit(solution)/shard_map/ppermute | solution.py:39
  92.7 18.9 %collective-permute-start.6 = (bf16[16,48,512]{2,1,0:T(8,128)(2,1)S(1)}, bf16[16,48,512]{2,1,0:T(8,128)(2,1)S(1)}, u32[]{:S(2)}, u32[]{:S(2)}) collective-permute-start(bf16[16,48,512]{2,1,0:T(8,128)(2,1)S(1)} %constant_dynamic-update-slice_fusion), channel_id=1, source_target_pairs={{0,16},{8,25},{16,0},{24,9},{1,17},{9,24},{17,1},{25,8},{2,18},{10... | collective-permute-start | bytes 2359304 | tf_op jit(solution)/shard_map/ppermute | solution.py:39
  101.1 20.1 %collective-permute-start.13 = (bf16[16,48,512]{2,1,0:T(8,128)(2,1)S(1)}, bf16[16,48,512]{2,1,0:T(8,128)(2,1)S(1)}, u32[]{:S(2)}, u32[]{:S(2)}) collective-permute-start(bf16[16,48,512]{2,1,0:T(8,128)(2,1)S(1)} %constant_dynamic-update-slice_fusion.5), channel_id=1, source_target_pairs={{0,32},{8,104},{16,48},{24,120},{1,33},{9,105},{17,49},{25,121},{2... | collective-permute-start | bytes 2359304 | tf_op jit(solution)/shard_map/ppermute | solution.py:39
  111.6 12.9 %collective-permute-start.7 = (bf16[16,48,512]{2,1,0:T(8,128)(2,1)S(1)}, bf16[16,48,512]{2,1,0:T(8,128)(2,1)S(1)}, u32[]{:S(2)}, u32[]{:S(2)}) collective-permute-start(bf16[16,48,512]{2,1,0:T(8,128)(2,1)S(1)} %constant_dynamic-update-slice_fusion), channel_id=1, source_target_pairs={{0,17},{8,24},{16,1},{24,8},{1,16},{9,25},{17,0},{25,9},{2,19},{10... | collective-permute-start | bytes 2359304 | tf_op jit(solution)/shard_map/ppermute | solution.py:39
  121.2 18.8 %collective-permute-start.14 = (bf16[16,48,512]{2,1,0:T(8,128)(2,1)S(1)}, bf16[16,48,512]{2,1,0:T(8,128)(2,1)}, u32[]{:S(2)}, u32[]{:S(2)}) collective-permute-start(bf16[16,48,512]{2,1,0:T(8,128)(2,1)S(1)} %constant_dynamic-update-slice_fusion.5), channel_id=1, source_target_pairs={{0,96},{8,40},{16,112},{24,56},{1,97},{9,41},{17,113},{25,57},{2,9... | collective-permute-start | bytes 2359304 | tf_op jit(solution)/shard_map/ppermute | solution.py:39
  124.5 16.7 %collective-permute-start.22 = (bf16[16,32,512]{2,1,0:T(8,128)(2,1)}, bf16[16,32,512]{2,1,0:T(8,128)(2,1)}, u32[]{:S(2)}, u32[]{:S(2)}) collective-permute-start(bf16[16,32,512]{2,1,0:T(8,128)(2,1)} %collective-permute-done.20), channel_id=1, source_target_pairs={{0,6},{8,10},{16,22},{24,26},{1,7},{9,11},{17,23},{25,27},{2,4},{1... | collective-permute-start | bytes 1572872 | tf_op jit(solution)/shard_map/ppermute | solution.py:39
  140.0 12.2 %collective-permute-start.8 = (bf16[16,48,512]{2,1,0:T(8,128)(2,1)}, bf16[16,48,512]{2,1,0:T(8,128)(2,1)S(1)}, u32[]{:S(2)}, u32[]{:S(2)}) collective-permute-start(bf16[16,48,512]{2,1,0:T(8,128)(2,1)} %copy-done.5), channel_id=1, source_target_pairs={{0,17},{8,24},{16,1},{24,8},{1,16},{9,25},{17,0},{25,9},{2,19},{10... | collective-permute-start | bytes 2359304 | tf_op jit(solution)/shard_map/ppermute | solution.py:39
  141.1 13.8 %collective-permute-start.15 = (bf16[16,48,512]{2,1,0:T(8,128)(2,1)}, bf16[16,48,512]{2,1,0:T(8,128)(2,1)S(1)}, u32[]{:S(2)}, u32[]{:S(2)}) collective-permute-start(bf16[16,48,512]{2,1,0:T(8,128)(2,1)} %copy-done.6), channel_id=1, source_target_pairs={{0,96},{8,40},{16,112},{24,56},{1,97},{9,41},{17,113},{25,57},{2,9... | collective-permute-start | bytes 2359304 | tf_op jit(solution)/shard_map/ppermute | solution.py:39
  221.1 10.7 %collective-permute-start.39 = (bf16[16,32,512]{2,1,0:T(8,128)(2,1)}, bf16[16,32,512]{2,1,0:T(8,128)(2,1)S(1)}, u32[]{:S(2)}, u32[]{:S(2)}) collective-permute-start(bf16[16,32,512]{2,1,0:T(8,128)(2,1)} %bitcast.138), channel_id=1, source_target_pairs={{0,6},{8,10},{16,22},{24,26},{1,7},{9,11},{17,23},{25,27},{2,4},{1... | collective-permute-start | bytes 1572872 | tf_op jit(solution)/shard_map/ppermute | solution.py:39
  223.2 15.2 %collective-permute-start.38 = (bf16[16,32,512]{2,1,0:T(8,128)(2,1)}, bf16[16,32,512]{2,1,0:T(8,128)(2,1)S(1)}, u32[]{:S(2)}, u32[]{:S(2)}) collective-permute-start(bf16[16,32,512]{2,1,0:T(8,128)(2,1)} %bitcast.137), channel_id=1, source_target_pairs={{0,6},{8,10},{16,22},{24,26},{1,7},{9,11},{17,23},{25,27},{2,4},{1... | collective-permute-start | bytes 1572872 | tf_op jit(solution)/shard_map/ppermute | solution.py:39
  232.9 9.3 %collective-permute-start.40 = (bf16[16,32,512]{2,1,0:T(8,128)(2,1)S(1)}, bf16[16,32,512]{2,1,0:T(8,128)(2,1)S(1)}, u32[]{:S(2)}, u32[]{:S(2)}) collective-permute-start(bf16[16,32,512]{2,1,0:T(8,128)(2,1)S(1)} %bitcast_add_fusion.4), channel_id=1, source_target_pairs={{0,2},{8,14},{16,18},{24,30},{1,3},{9,15},{17,19},{25,31},{2,0},{1... | collective-permute-start | bytes 1572872 | tf_op jit(solution)/shard_map/ppermute | solution.py:39
  233.0 18.3 %collective-permute-start.25 = (bf16[16,48,512]{2,1,0:T(8,128)(2,1)}, bf16[16,48,512]{2,1,0:T(8,128)(2,1)S(1)}, u32[]{:S(2)}, u32[]{:S(2)}) collective-permute-start(bf16[16,48,512]{2,1,0:T(8,128)(2,1)} %bitcast.136), channel_id=1, source_target_pairs={{0,17},{8,24},{16,1},{24,8},{1,16},{9,25},{17,0},{25,9},{2,19},{10... | collective-permute-start | bytes 2359304 | tf_op jit(solution)/shard_map/ppermute | solution.py:39
  234.6 51.0 %collective-permute-start.24 = (bf16[16,48,512]{2,1,0:T(8,128)(2,1)}, bf16[16,48,512]{2,1,0:T(8,128)(2,1)S(1)}, u32[]{:S(2)}, u32[]{:S(2)}) collective-permute-start(bf16[16,48,512]{2,1,0:T(8,128)(2,1)} %bitcast.134), channel_id=1, source_target_pairs={{0,17},{8,24},{16,1},{24,8},{1,16},{9,25},{17,0},{25,9},{2,19},{10... | collective-permute-start | bytes 2359304 | tf_op jit(solution)/shard_map/ppermute | solution.py:39
  235.1 34.6 %collective-permute-start.32 = (bf16[16,48,512]{2,1,0:T(8,128)(2,1)}, bf16[16,48,512]{2,1,0:T(8,128)(2,1)S(1)}, u32[]{:S(2)}, u32[]{:S(2)}) collective-permute-start(bf16[16,48,512]{2,1,0:T(8,128)(2,1)} %bitcast.135), channel_id=1, source_target_pairs={{0,96},{8,40},{16,112},{24,56},{1,97},{9,41},{17,113},{25,57},{2,9... | collective-permute-start | bytes 2359304 | tf_op jit(solution)/shard_map/ppermute | solution.py:39
  238.3 50.0 %collective-permute-start.31 = (bf16[16,48,512]{2,1,0:T(8,128)(2,1)}, bf16[16,48,512]{2,1,0:T(8,128)(2,1)S(1)}, u32[]{:S(2)}, u32[]{:S(2)}) collective-permute-start(bf16[16,48,512]{2,1,0:T(8,128)(2,1)} %bitcast.133), channel_id=1, source_target_pairs={{0,96},{8,40},{16,112},{24,56},{1,97},{9,41},{17,113},{25,57},{2,9... | collective-permute-start | bytes 2359304 | tf_op jit(solution)/shard_map/ppermute | solution.py:39
  243.4 26.2 %collective-permute-start.41 = (bf16[8,32,512]{2,1,0:T(8,128)(2,1)S(1)}, bf16[8,32,512]{2,1,0:T(8,128)(2,1)S(1)}, u32[]{:S(2)}, u32[]{:S(2)}) collective-permute-start(bf16[8,32,512]{2,1,0:T(8,128)(2,1)S(1)} %slice.137), channel_id=1, source_target_pairs={{0,96},{8,40},{16,112},{24,56},{1,97},{9,41},{17,113},{25,57},{2,9... | collective-permute-start | bytes 786440 | tf_op jit(solution)/shard_map/ppermute | solution.py:39
  252.5 33.1 %collective-permute-start.26 = (bf16[16,48,512]{2,1,0:T(8,128)(2,1)S(1)}, bf16[16,48,512]{2,1,0:T(8,128)(2,1)S(1)}, u32[]{:S(2)}, u32[]{:S(2)}) collective-permute-start(bf16[16,48,512]{2,1,0:T(8,128)(2,1)S(1)} %bitcast_add_fusion.2), channel_id=1, source_target_pairs={{0,16},{8,25},{16,0},{24,9},{1,17},{9,24},{17,1},{25,8},{2,18},{10... | collective-permute-start | bytes 2359304 | tf_op jit(solution)/shard_map/ppermute | solution.py:39
  269.9 18.5 %collective-permute-start.33 = (bf16[16,48,512]{2,1,0:T(8,128)(2,1)S(1)}, bf16[16,48,512]{2,1,0:T(8,128)(2,1)S(1)}, u32[]{:S(2)}, u32[]{:S(2)}) collective-permute-start(bf16[16,48,512]{2,1,0:T(8,128)(2,1)S(1)} %bitcast_add_fusion), channel_id=1, source_target_pairs={{0,32},{8,104},{16,48},{24,120},{1,33},{9,105},{17,49},{25,121},{2... | collective-permute-start | bytes 2359304 | tf_op jit(solution)/shard_map/ppermute | solution.py:39
  279.1 9.9 %collective-permute-start.44 = (bf16[1,32,512]{2,1,0:T(8,128)(2,1)S(1)}, bf16[1,32,512]{2,1,0:T(8,128)(2,1)S(1)}, u32[]{:S(2)}, u32[]{:S(2)}) collective-permute-start(bf16[1,32,512]{2,1,0:T(8,128)(2,1)S(1)} %slice.143), channel_id=1, source_target_pairs={{0,16},{8,25},{16,0},{24,9},{1,17},{9,24},{17,1},{25,8},{2,18},{10... | collective-permute-start | bytes 98312 | tf_op jit(solution)/shard_map/ppermute | solution.py:39
  285.8 9.1 %collective-permute-start.27 = (bf16[8,48,512]{2,1,0:T(8,128)(2,1)S(1)}, bf16[8,48,512]{2,1,0:T(8,128)(2,1)S(1)}, u32[]{:S(2)}, u32[]{:S(2)}) collective-permute-start(bf16[8,48,512]{2,1,0:T(8,128)(2,1)S(1)} %slice.121), channel_id=1, source_target_pairs={{0,6},{8,10},{16,22},{24,26},{1,7},{9,11},{17,23},{25,27},{2,4},{1... | collective-permute-start | bytes 1179656 | tf_op jit(solution)/shard_map/ppermute | solution.py:39
  288.6 7.9 %collective-permute-start.34 = (bf16[8,48,512]{2,1,0:T(8,128)(2,1)S(1)}, bf16[8,48,512]{2,1,0:T(8,128)(2,1)S(1)}, u32[]{:S(2)}, u32[]{:S(2)}) collective-permute-start(bf16[8,48,512]{2,1,0:T(8,128)(2,1)S(1)} %slice.129), channel_id=1, source_target_pairs={{0,17},{8,24},{16,1},{24,8},{1,16},{9,25},{17,0},{25,9},{2,19},{10... | collective-permute-start | bytes 1179656 | tf_op jit(solution)/shard_map/ppermute | solution.py:39
  296.5 7.2 %collective-permute-start.35 = (bf16[4,48,512]{2,1,0:T(8,128)(2,1)S(1)}, bf16[4,48,512]{2,1,0:T(8,128)(2,1)S(1)}, u32[]{:S(2)}, u32[]{:S(2)}) collective-permute-start(bf16[4,48,512]{2,1,0:T(8,128)(2,1)S(1)} %slice.131), channel_id=1, source_target_pairs={{0,16},{8,25},{16,0},{24,9},{1,17},{9,24},{17,1},{25,8},{2,18},{10... | collective-permute-start | bytes 589832 | tf_op jit(solution)/shard_map/ppermute | solution.py:39
  (26 other events, 435.7 us)

commit v2 on v0

v2 whole, which is shorter than its diff:
```python
import jax
import jax.numpy as jnp
from jax import lax
from jax.experimental import pallas as pl
from jax.experimental.pallas import tpu as pltpu
from jax.sharding import PartitionSpec as P

AXES = ("expert", "tensor")
OFF = (0, 1, 3, 2)
LOW = (0, 1, 1, 0)
HIGH = (0, 0, 1, 1)
ROWS = (48, 48, 32)
FIRST = (0, 48, 96)
BF16 = jnp.bfloat16
F32 = jnp.float32


def device_number(x, y, z, core):
    return (x * 4 + (z % 2) * 2 + core) * 8 + y * 2 + z // 2


def places():
    return [(x, y, z, c) for x in range(4) for y in range(4) for z in range(4) for c in range(2)]


def swap(value, dim, mask):
    pairs = []
    for place in places():
        other = list(place)
        other[dim] ^= mask
        pairs.append((device_number(*place), device_number(*other)))
    return lax.ppermute(value, AXES, pairs)


def from_other_core(value):
    pairs = [(device_number(x, y, z, c), device_number(x, y, z, 1 - c)) for x, y, z, c in places()]
    return lax.ppermute(value, AXES, pairs)


def swap_each(parts, phase, mask):
    return [swap(part, (i + phase) % 3, mask) for i, part in enumerate(parts)]


def double(parts, phase, mask):
    got = swap_each(parts, phase, mask)
    return [jnp.concatenate([part, new], 0) for part, new in zip(parts, got)]


def gather_last(parts):
    one = swap_each(parts, 2, 1)
    three = swap_each(parts, 2, 3)
    two_a = swap_each([p[:8] for p in one], 2, 3)
    two_b = swap_each([p[8:] for p in three], 2, 1)
    return list(zip(parts, one, three, two_a, two_b))


def scatter_sums(parts):
    own, one, three, two_a, two_b = (list(p) for p in zip(*parts))
    got_a = swap_each(two_a, 2, 3)
    got_b = swap_each(two_b, 2, 1)
    one = [jnp.concatenate([p[:8] + g, p[8:]], 0) for p, g in zip(one, got_a)]
    three = [jnp.concatenate([p[:8], p[8:] + g], 0) for p, g in zip(three, got_b)]
    got_a = swap_each(one, 2, 1)
    got_b = swap_each(three, 2, 3)
    held = [
        (p.astype(F32) + a.astype(F32) + b.astype(F32)).astype(BF16)
        for p, a, b in zip(own, got_a, got_b)
    ]
    for phase in (1, 0):
        for mask in (3, 1):
            half = held[0].shape[0] // 2
            got = swap_each([p[half:] for p in held], phase, mask)
            held = [p[:half] + r for p, r in zip(held, got)]
    return jnp.concatenate([p[0] for p in held], 0)


def piece(refs, i, k3, k2, k1):
    group = refs[i * 5 : i * 5 + 5]
    if k3 < 3:
        return [group[k3].at[slice(None) if k2 is None else k2, slice(None) if k1 is None else k1]]
    if k2 is None:
        return [half.at[:, k1] for half in group[3:]]
    return [group[3 + k2 // 2].at[k2 % 2, slice(None) if k1 is None else k1]]


def place_of(low, high):
    return [k for k in range(4) if (LOW[k], HIGH[k]) == (low, high)][0]


def block_pieces(refs, tile, column):
    def pairs(ky, kz):
        found = []
        low, cols = LOW[kz], column(ky, kz)
        rows = [pl.ds(first, count) for first, count in zip(FIRST, ROWS)]
        (hbm,) = piece(refs, 0, kz, ky, None)
        found.append((hbm, tile.at[:, low, rows[0], cols]))
        for kx in range(4):
            (hbm,) = piece(refs, 1, kx, kz, ky)
            found.append((hbm, tile.at[kx, low, rows[1], cols]))
        halves = piece(refs, 2, ky, None, kz)
        for n, hbm in enumerate(halves):
            step = 4 // len(halves)
            found.append((hbm, tile.at[pl.ds(n * step, step), low, rows[2], cols]))
        return found

    return pairs


def route(ids_ref, mine_ref, slot_ref, gate_col, pick):
    before = lax.broadcasted_iota(jnp.int32, (128, 128), 0)
    before = (before < lax.broadcasted_iota(jnp.int32, (128, 128), 1)).astype(BF16)
    number = lax.broadcasted_iota(jnp.int32, (8, 32, 128), 1).astype(F32)
    line = lax.broadcasted_iota(jnp.int32, (8, 128), 0)

    def block(b, carry):
        named = jnp.zeros((8, 128), F32)
        weight = jnp.zeros((8, 128), F32)
        for e in range(8):
            hit = mine_ref[b, 0:8] == ids_ref[e]
            any_hit = jnp.max(jnp.where(hit, 1.0, 0.0), axis=0, keepdims=True)
            gate = jnp.sum(jnp.where(hit, mine_ref[b, 8:16], 0.0), axis=0, keepdims=True)
            named = jnp.where(line == e, any_hit, named)
            weight = jnp.where(line == e, gate, weight)
        slot = jnp.dot(named.astype(BF16), before, preferred_element_type=F32)
        slot = jnp.where(named > 0, slot, -1.0)
        slot_ref[b] = slot
        chosen = slot[:, None, :] == number
        pick[b] = jnp.where(chosen, 1.0, 0.0).astype(BF16).reshape(256, 128)
        rows = pl.ds(pl.multiple_of(b * 32, 32), 32)
        gate_col[:, rows, :] = jnp.sum(
            jnp.where(chosen, weight[:, None, :], 0.0), axis=2, keepdims=True
        )
        return carry

    lax.fori_loop(0, 8, block, 0)


N_TOKEN_COPIES = 100


def hidden_kernel(ids_ref, cols_ref, mine_ref, wg, wu, wg2, wu2, *rest):
    token_refs = rest[:15]
    h_ref, slot_ref, tokens, sorted_rows, wbuf, gate_col, pick, t_sem, w_sem = rest[15:]

    def fetch(e, j, gate, up):
        return [
            pltpu.make_async_copy(gate.at[e], wbuf.at[j, pl.ds(0, 192)], w_sem.at[j, 0]),
            pltpu.make_async_copy(up.at[e], wbuf.at[j, pl.ds(192, 192)], w_sem.at[j, 1]),
        ]

    def column(ky, kz):
        return pl.ds(pl.multiple_of(cols_ref[ky * 2 + HIGH[kz]] * 512, 512), 512)

    pairs = block_pieces(token_refs, tokens, column)
    loads = [pair for ky in range(4) for kz in range(4) for pair in pairs(ky, kz)]
    loads = [pltpu.make_async_copy(a, b, t_sem.at[n]) for n, (a, b) in enumerate(loads)]
    for copy in loads:
        copy.start()
    route(ids_ref, mine_ref, slot_ref, gate_col, pick)
    for copy in loads:
        copy.wait()
    for j in range(4):
        for copy in fetch(j, j, wg, wu):
            copy.start()

    def dispatch(b, carry):
        rows = jnp.dot(pick[b], tokens[b // 2, lax.rem(b, 2)], preferred_element_type=F32)
        sorted_rows[:, pl.ds(pl.multiple_of(b * 32, 32), 32)] = rows.astype(BF16).reshape(
            8, 32, 4096
        )
        return carry

    lax.fori_loop(0, 8, dispatch, 0)

    def experts(turn, carry):
        for j in range(4):
            e = turn * 4 + j
            for copy in fetch(j, j, wg, wu):
                copy.wait()
            act = lax.dot_general(
                sorted_rows[e], wbuf[j], (((1,), (1,)), ((), ())), preferred_element_type=F32
            )
            gate, up = act[:, :192], act[:, 192:]
            hidden = gate / (1.0 + jnp.exp(-gate)) * up * gate_col[e]
            h_ref[e] = hidden.astype(BF16)

            @pl.when(turn == 0)
            def _():
                for copy in fetch(j, j, wg2, wu2):
                    copy.start()

        return carry

    lax.fori_loop(0, 2, experts, 0)


def down_kernel(cols_ref, h_ref, slot_ref, wd, wd2, *rest):
    outs = rest[:15]
    wbuf, expert_rows, ybuf, put, w_sem, y_sem = rest[15:]

    def fetch(ky):
        slot = ky % 2
        col = pl.ds(pl.multiple_of(cols_ref[ky * 2] // 2 * 1024, 1024), 1024)
        return [
            pltpu.make_async_copy(wd.at[:, :, col], wbuf.at[slot, pl.ds(0, 4)], w_sem.at[slot, 0]),
            pltpu.make_async_copy(wd2.at[:, :, col], wbuf.at[slot, pl.ds(4, 4)], w_sem.at[slot, 1]),
        ]

    def stores(ky):
        def column(ky, kz):
            side = lax.rem(cols_ref[ky * 2 + HIGH[kz]], 2)
            return pl.ds(pl.multiple_of(side * 512, 512), 512)

        pairs = block_pieces(outs, ybuf.at[ky % 2], column)
        found = [pair for kz in range(4) for pair in pairs(ky, kz)]
        return [
            pltpu.make_async_copy(b, a, y_sem.at[ky % 2, n]) for n, (a, b) in enumerate(found)
        ]

    for copy in fetch(0) + fetch(1):
        copy.start()
    number = lax.broadcasted_iota(jnp.int32, (8, 32, 128), 1).astype(F32)
    for b in range(8):
        chosen = jnp.where(slot_ref[b][:, None, :] == number, 1.0, 0.0).reshape(256, 128)
        put[b] = chosen.T.astype(BF16)
    for ky in range(4):
        slot = ky % 2
        for copy in fetch(ky):
            copy.wait()

        def project(e, carry):
            out = jnp.dot(h_ref[e], wbuf[slot, e], preferred_element_type=F32)
            rows = pl.ds(pl.multiple_of(e * 32, 32), 32)
            expert_rows[:, rows] = out.astype(BF16).reshape(8, 32, 1024)
            return carry

        lax.fori_loop(0, 8, project, 0, unroll=2)
        if ky < 2:
            for copy in fetch(ky + 2):
                copy.start()
        if ky >= 2:
            for copy in stores(ky - 2):
                copy.wait()

        def combine(b, carry):
            out = jnp.dot(put[b], expert_rows[b], preferred_element_type=F32)
            ybuf[slot, b // 2, lax.rem(b, 2)] = out.astype(BF16)
            return carry

        lax.fori_loop(0, 8, combine, 0, unroll=2)
        for copy in stores(ky):
            copy.start()
    for ky in (2, 3):
        for copy in stores(ky):
            copy.wait()


def local(tokens, routes, gates, w_gate, w_up, w_down):
    e, t = lax.axis_index("expert"), lax.axis_index("tensor")
    y, zhi = t // 2, t % 2
    ids = jnp.concatenate([e * 4 + jnp.arange(4), (e ^ 1) * 4 + jnp.arange(4)]).astype(F32)
    cols = jnp.stack([(y ^ OFF[ky]) * 2 + (zhi ^ high) for ky in range(4) for high in range(2)])
    cols = cols.astype(jnp.int32)

    packed = jnp.concatenate([routes.astype(F32), gates], axis=1).T[None]
    parts = [tokens[first : first + rows][None] for first, rows in zip(FIRST, ROWS)]

    wg2 = from_other_core(w_gate)
    for mask in (1, 3):
        parts = double(parts, 0, mask)
        packed = jnp.concatenate([packed, swap(packed, 0, mask)], 0)
    parts, wg2, w_up = lax.optimization_barrier((parts, wg2, w_up))
    wu2 = from_other_core(w_up)
    mine = jnp.stack([packed, swap(packed, 2, 1)], 1).reshape(8, 16, 128)
    for mask in (1, 3):
        parts = double(parts, 1, mask)
    parts, wu2, mine = lax.optimization_barrier((parts, wu2, mine))
    parts = gather_last(parts)
    parts, w_down = lax.optimization_barrier((parts, w_down))
    wd2 = from_other_core(w_down)
    pieces = [
        p.reshape(p.shape[0] // 4, 4, ROWS[i], 512) for i, part in enumerate(parts) for p in part
    ]
    smem = pl.BlockSpec(memory_space=pltpu.SMEM)
    vmem = pl.BlockSpec(memory_space=pltpu.VMEM)
    hbm = pl.BlockSpec(memory_space=pl.ANY)
    hidden, slots = pl.pallas_call(
        hidden_kernel,
        out_shape=[
            jax.ShapeDtypeStruct((8, 256, 192), BF16),
            jax.ShapeDtypeStruct((8, 8, 128), F32),
        ],
        in_specs=[smem, smem, vmem] + [hbm] * 19,
        out_specs=[vmem, vmem],
        scratch_shapes=[
            pltpu.VMEM((4, 2, 128, 4096), BF16),
            pltpu.VMEM((8, 256, 4096), BF16),
            pltpu.VMEM((4, 384, 4096), BF16),
            pltpu.VMEM((8, 256, 1), F32),
            pltpu.VMEM((8, 256, 128), BF16),
            pltpu.SemaphoreType.DMA((N_TOKEN_COPIES,)),
            pltpu.SemaphoreType.DMA((4, 2)),
        ],
        compiler_params=pltpu.CompilerParams(vmem_limit_bytes=56 * 2**20),
        name="hidden",
    )(ids, cols, mine, w_gate, w_up, wg2, wu2, *pieces)

    sums = pl.pallas_call(
        down_kernel,
        out_shape=[
            jax.ShapeDtypeStruct((4 if k < 3 else 2, 4, ROWS[i], 512), BF16)
            for i in range(3)
            for k in range(5)
        ],
        in_specs=[smem, vmem, vmem, hbm, hbm],
        out_specs=[hbm] * 15,
        scratch_shapes=[
            pltpu.VMEM((2, 8, 192, 1024), BF16),
            pltpu.VMEM((8, 256, 1024), BF16),
            pltpu.VMEM((2, 4, 2, 128, 1024), BF16),
            pltpu.VMEM((8, 128, 256), BF16),
            pltpu.SemaphoreType.DMA((2, 2)),
            pltpu.SemaphoreType.DMA((2, 28)),
        ],
        compiler_params=pltpu.CompilerParams(vmem_limit_bytes=56 * 2**20),
        name="down",
    )(cols, hidden, slots, w_down, wd2)
    parts = [
        [p.reshape(-1, ROWS[i], 512) for p in sums[i * 5 : i * 5 + 5]] for i in range(3)
    ]
    return scatter_sums(parts)


def solution(mesh):
    placed = (
        P("expert", "tensor"),
        P("expert", None),
        P("expert", None),
        P("expert", "tensor", None),
        P("expert", "tensor", None),
        P("expert", "tensor", None),
    )
    return jax.shard_map(
        local, mesh=mesh, in_specs=placed, out_specs=P("expert", "tensor"), check_vma=False
    )
```

time: 746 us -> 211 us (0.28)
  waiting for transfers between devices: 416 us -> 95.5 us
  blocking collectives: 191 us -> 0 us
  starting transfers between devices: 6.84 us -> 63.1 us
  local copies, waits for them, and re-layouts: 60.1 us -> 6.88 us
  Pallas kernels: 0 us -> 39.9 us
  matrix products: 35.2 us -> 0 us
  other arithmetic: 21.6 us -> 3.83 us
  between operations: 13.5 us -> 0.83 us
    all_to_all x1 -> x0, waiting for transfers between devices: 249 us -> none  [local(): lax.all_to_all(partials.reshape(group_count, local_experts * capacity, mo...]
    all_to_all x1 -> x0, blocking collectives: 191 us -> none  [local(): lax.all_to_all(buffer.reshape(group_count, local_experts * capacity, mode...]
    reduce_scatter x1 -> x0, waiting for transfers between devices: 135 us -> none  [local(): lax.psum_scatter(picked.astype(jnp.bfloat16), 'tensor', scatter_dimension...]
    ppermute x0 -> x54, waiting for transfers between devices: none -> 95.5 us  [the longest x51 95.5 us: swap(): return lax.ppermute(value, AXES, pairs)]
    ppermute x0 -> x54, starting transfers between devices: none -> 63.1 us  [the longest x51 62.7 us: swap(): return lax.ppermute(value, AXES, pairs)]
    pallas_call x0 -> x2, Pallas kernels: none -> 39.9 us  [the longest x1 22.6 us: local(): pl.pallas_call(hidden_kernel, out_shape=[jax.ShapeDtypeStruct((8, 256, 19...]
    dot_general x2 -> x0, matrix products: 35.2 us -> none  [the longest x1 25.2 us: local(): jnp.einsum('escf,efd->secd', hidden, w_down, preferred_element_type=jnp.f...]
    all_gather x1 -> x0, waiting for transfers between devices: 31.3 us -> none  [local(): owner_rows = lax.all_gather(tokens, 'tensor', axis=1, tiled=True)]
  transfers between devices with their start and end apart: 3 -> 54, of which waited for: 3 -> 25; matrix products, arithmetic and copies ran while one was open for 3% -> 4% of each run, Pallas kernels for 0% -> 11%
where the time goes in v2:
time: 211 us; the launch traced here: 210 us
  waiting for transfers between devices  95.5 us (45%)
  starting transfers between devices  63.1 us (30%)
  Pallas kernels  39.9 us (19%)
  local copies, waits for them, and re-layouts  6.88 us (3%)
  other arithmetic  3.83 us (2%)
    ppermute x51, waiting for transfers between devices, swap(): return lax.ppermute(value, AXES, pairs)  95.5 us
    ppermute x51, starting transfers between devices, swap(): return lax.ppermute(value, AXES, pairs)  62.7 us
    pallas_call x1, Pallas kernels, local(): pl.pallas_call(hidden_kernel, out_shape=[jax.ShapeDtypeStruct((8, 256, 19...  22.6 us
    pallas_call x1, Pallas kernels, local(): pl.pallas_call(down_kernel, out_shape=[jax.ShapeDtypeStruct((4 if k < 3 e...  17.3 us
  transfers between devices with their start and end apart: 54, of which 25 were waited for; matrix products, arithmetic and copies ran while one was open for 4% of the time, Pallas kernels for 11%

profile of v2, /device:TPU:32, one launch (start us, length us, event | category | flops | bytes accessed | tf_op | source)
XLA Modules:
  0.0 210.0 jit_solution(2467112808740208172)
XLA Ops:
  4.9 3.5 %collective-permute-start.5 = (bf16[2,32,512]{2,1,0:T(8,128)(2,1)S(1)}, bf16[2,32,512]{2,1,0:T(8,128)(2,1)S(1)}, u32[]{:S(2)}, u32[]{:S(2)}) collective-permute-start(bf16[2,32,512]{2,1,0:T(8,128)(2,1)S(1)} %pad_maximum_fusion.18), channel_id=1, source_target_pairs={{0,17},{8,25},{16,1},{24,9},{1,16},{9,24},{17,0},{25,8},{2,19},{10... | collective-permute-start | bytes 196616 | tf_op jit(solution)/shard_map/ppermute | solution.py:32
  8.4 2.3 %collective-permute-start.3 = (bf16[2,48,512]{2,1,0:T(8,128)(2,1)S(1)}, bf16[2,48,512]{2,1,0:T(8,128)(2,1)S(1)}, u32[]{:S(2)}, u32[]{:S(2)}) collective-permute-start(bf16[2,48,512]{2,1,0:T(8,128)(2,1)S(1)} %pad_maximum_fusion.17), channel_id=1, source_target_pairs={{0,6},{8,14},{16,22},{24,30},{1,7},{9,15},{17,23},{25,31},{2,4},{1... | collective-permute-start | bytes 294920 | tf_op jit(solution)/shard_map/ppermute | solution.py:32
  10.7 2.2 %collective-permute-start.1 = (bf16[2,48,512]{2,1,0:T(8,128)(2,1)S(1)}, bf16[2,48,512]{2,1,0:T(8,128)(2,1)S(1)}, u32[]{:S(2)}, u32[]{:S(2)}) collective-permute-start(bf16[2,48,512]{2,1,0:T(8,128)(2,1)S(1)} %pad_maximum_fusion.16), channel_id=1, source_target_pairs={{0,96},{8,104},{16,112},{24,120},{1,97},{9,105},{17,113},{25,121},... | collective-permute-start | bytes 294920 | tf_op jit(solution)/shard_map/ppermute | solution.py:32
  14.3 2.3 %collective-permute-done.1 = bf16[2,48,512]{2,1,0:T(8,128)(2,1)S(1)} collective-permute-done((bf16[2,48,512]{2,1,0:T(8,128)(2,1)S(1)}, bf16[2,48,512]{2,1,0:T(8,128)(2,1)S(1)}, u32[]{:S(2)}, u32[]{:S(2)}) %collective-permute-start.1) | collective-permute-done | bytes 98336 | tf_op jit(solution)/shard_map/ppermute | solution.py:32
  19.5 3.3 %collective-permute-done.14 = f32[1,16,128]{2,1,0:T(8,128)S(1)} collective-permute-done((f32[1,16,128]{2,1,0:T(8,128)S(1)}, f32[1,16,128]{2,1,0:T(8,128)S(1)}, u32[]{:S(2)}, u32[]{:S(2)}) %collective-permute-start.14) | collective-permute-done | bytes 8224 | tf_op jit(solution)/shard_map/ppermute | solution.py:32
  22.8 2.1 collective-permute-start.15
  24.9 2.1 collective-permute-start.9
  29.5 2.3 %collective-permute-done.9 = bf16[4,48,512]{2,1,0:T(8,128)(2,1)S(1)} collective-permute-done((bf16[4,48,512]{2,1,0:T(8,128)(2,1)S(1)}, bf16[4,48,512]{2,1,0:T(8,128)(2,1)S(1)}, u32[]{:S(2)}, u32[]{:S(2)}) %collective-permute-start.9) | collective-permute-done | bytes 196640 | tf_op jit(solution)/shard_map/ppermute | solution.py:32
  31.8 2.2 %collective-permute-start.10 = (bf16[8,48,512]{2,1,0:T(8,128)(2,1)S(1)}, bf16[8,48,512]{2,1,0:T(8,128)(2,1)S(1)}, u32[]{:S(2)}, u32[]{:S(2)}) collective-permute-start(bf16[8,48,512]{2,1,0:T(8,128)(2,1)S(1)} %pad_maximum_fusion.10), channel_id=1, source_target_pairs={{0,17},{8,25},{16,1},{24,9},{1,16},{9,24},{17,0},{25,8},{2,19},{10... | collective-permute-start | bytes 1179656 | tf_op jit(solution)/shard_map/ppermute | solution.py:32
  35.7 3.1 %collective-permute-done.8 = bf16[8,48,512]{2,1,0:T(8,128)(2,1)S(1)} collective-permute-done((bf16[8,48,512]{2,1,0:T(8,128)(2,1)S(1)}, bf16[8,48,512]{2,1,0:T(8,128)(2,1)S(1)}, u32[]{:S(2)}, u32[]{:S(2)}) %collective-permute-start.8) | collective-permute-done | bytes 393248 | tf_op jit(solution)/shard_map/ppermute | solution.py:32
  38.8 2.5 %collective-permute-done.10 = bf16[8,48,512]{2,1,0:T(8,128)(2,1)S(1)} collective-permute-done((bf16[8,48,512]{2,1,0:T(8,128)(2,1)S(1)}, bf16[8,48,512]{2,1,0:T(8,128)(2,1)S(1)}, u32[]{:S(2)}, u32[]{:S(2)}) %collective-permute-start.10) | collective-permute-done | bytes 393248 | tf_op jit(solution)/shard_map/ppermute | solution.py:32
  43.9 2.2 %collective-permute-start.17 = (bf16[16,48,512]{2,1,0:T(8,128)(2,1)S(1)}, bf16[16,48,512]{2,1,0:T(8,128)(2,1)S(1)}, u32[]{:S(2)}, u32[]{:S(2)}) collective-permute-start(bf16[16,48,512]{2,1,0:T(8,128)(2,1)S(1)} %pad_maximum_fusion), channel_id=1, source_target_pairs={{0,16},{8,24},{16,0},{24,8},{1,17},{9,25},{17,1},{25,9},{2,18},{10... | collective-permute-start | bytes 2359304 | tf_op jit(solution)/shard_map/ppermute | solution.py:32
  48.0 6.1 %collective-permute-done.26 = bf16[16,32,512]{2,1,0:T(8,128)(2,1)S(1)} collective-permute-done((bf16[16,32,512]{2,1,0:T(8,128)(2,1)S(1)}, bf16[16,32,512]{2,1,0:T(8,128)(2,1)S(1)}, u32[]{:S(2)}, u32[]{:S(2)}) %collective-permute-start.26) | collective-permute-done | bytes 524320 | tf_op jit(solution)/shard_map/ppermute | solution.py:32
  54.1 4.7 %collective-permute-done.18 = bf16[16,48,512]{2,1,0:T(8,128)(2,1)S(1)} collective-permute-done((bf16[16,48,512]{2,1,0:T(8,128)(2,1)S(1)}, bf16[16,48,512]{2,1,0:T(8,128)(2,1)S(1)}, u32[]{:S(2)}, u32[]{:S(2)}) %collective-permute-start.18) | collective-permute-done | bytes 786464 | tf_op jit(solution)/shard_map/ppermute | solution.py:32
  59.5 2.3 %collective-permute-done.17 = bf16[16,48,512]{2,1,0:T(8,128)(2,1)S(1)} collective-permute-done((bf16[16,48,512]{2,1,0:T(8,128)(2,1)S(1)}, bf16[16,48,512]{2,1,0:T(8,128)(2,1)S(1)}, u32[]{:S(2)}, u32[]{:S(2)}) %collective-permute-start.17) | collective-permute-done | bytes 786464 | tf_op jit(solution)/shard_map/ppermute | solution.py:32
  61.8 2.0 collective-permute-start.20
  70.6 6.9 %collective-permute-done.27 = bf16[8,32,512]{2,1,0:T(8,128)(2,1)S(1)} collective-permute-done((bf16[8,32,512]{2,1,0:T(8,128)(2,1)S(1)}, bf16[8,32,512]{2,1,0:T(8,128)(2,1)S(1)}, u32[]{:S(2)}, u32[]{:S(2)}) %collective-permute-start.27) | collective-permute-done | bytes 262176 | tf_op jit(solution)/shard_map/ppermute | solution.py:32
  79.3 22.6 %hidden.1 = (bf16[8,256,192]{2,1,0:T(8,128)(2,1)}, f32[8,8,128]{2,1,0:T(8,128)}) custom-call(f32[8]{0:T(128)} %add_convert_fusion.ids_ref, s32[8]{0:T(128)} %stack.44.cols_ref, f32[8,16,128]{2,1,0:T(8,128)} %bitcast.96, bf16[4,192,4096]{2,1,0:T(8,128)(2,1)} %wg.1, bf16[4,192,4096]{2,1,0:T(8,128)(2,1)} %wu, bf16[4,192,4096]{2,1,0:T(8,128)(2,1)} %collective-permute-done.6.wg2, ...), custom_call_target="tpu_custom_call" | custom-call | tf_op jit(solution)/shard_map/hidden/pallas_call | solution.py:287
  101.9 17.3 %down.1 = (bf16[4,4,48,512]{3,2,1,0:T(8,128)(2,1)}, bf16[4,4,48,512]{3,2,1,0:T(8,128)(2,1)}, bf16[4,4,48,512]{3,2,1,0:T(8,128)(2,1)}, bf16[2,4,48,512]{3,2,1,0:T...) custom-call(s32[8]{0:T(128)} %stack.44.cols_ref, ...), custom_call_target="tpu_custom_call" | custom-call | tf_op jit(solution)/shard_map/down/pallas_call | solution.py:308
  121.1 2.9 %collective-permute-start.32 = (bf16[8,48,512]{2,1,0:T(8,128)(2,1)}, bf16[8,48,512]{2,1,0:T(8,128)(2,1)S(1)}, u32[]{:S(2)}, u32[]{:S(2)}) collective-permute-start(bf16[8,48,512]{2,1,0:T(8,128)(2,1)} %bitcast.99), channel_id=1, source_target_pairs={{0,16},{8,24},{16,0},{24,8},{1,17},{9,25},{17,1},{25,9},{2,18},{10... | collective-permute-start | bytes 1179656 | tf_op jit(solution)/shard_map/ppermute | solution.py:32
  129.5 2.2 %collective-permute-start.49 = (bf16[16,32,512]{2,1,0:T(8,128)(2,1)S(1)}, bf16[16,32,512]{2,1,0:T(8,128)(2,1)S(1)}, u32[]{:S(2)}, u32[]{:S(2)}) collective-permute-start(bf16[16,32,512]{2,1,0:T(8,128)(2,1)S(1)} %pad_maximum_fusion.8), channel_id=1, source_target_pairs={{0,6},{8,14},{16,22},{24,30},{1,7},{9,15},{17,23},{25,31},{2,4},{1... | collective-permute-start | bytes 1572872 | tf_op jit(solution)/shard_map/ppermute | solution.py:32
  131.8 7.8 %collective-permute-done.40 = bf16[8,48,512]{2,1,0:T(8,128)(2,1)S(1)} collective-permute-done((bf16[8,48,512]{2,1,0:T(8,128)(2,1)S(1)}, bf16[8,48,512]{2,1,0:T(8,128)(2,1)S(1)}, u32[]{:S(2)}, u32[]{:S(2)}) %collective-permute-start.40) | collective-permute-done | bytes 393248 | tf_op jit(solution)/shard_map/ppermute | solution.py:32
  144.1 7.8 %collective-permute-done.47 = bf16[16,32,512]{2,1,0:T(8,128)(2,1)S(1)} collective-permute-done((bf16[16,32,512]{2,1,0:T(8,128)(2,1)S(1)}, bf16[16,32,512]{2,1,0:T(8,128)(2,1)S(1)}, u32[]{:S(2)}, u32[]{:S(2)}) %collective-permute-start.47) | collective-permute-done | bytes 524320 | tf_op jit(solution)/shard_map/ppermute | solution.py:32
  155.1 10.7 %collective-permute-done.50 = bf16[8,32,512]{2,1,0:T(8,128)(2,1)S(1)} collective-permute-done((bf16[8,32,512]{2,1,0:T(8,128)(2,1)S(1)}, bf16[8,32,512]{2,1,0:T(8,128)(2,1)S(1)}, u32[]{:S(2)}, u32[]{:S(2)}) %collective-permute-start.50) | collective-permute-done | bytes 262176 | tf_op jit(solution)/shard_map/ppermute | solution.py:32
  166.6 4.2 %collective-permute-done.51 = bf16[4,32,512]{2,1,0:T(8,128)(2,1)S(1)} collective-permute-done((bf16[4,32,512]{2,1,0:T(8,128)(2,1)S(1)}, bf16[4,32,512]{2,1,0:T(8,128)(2,1)S(1)}, u32[]{:S(2)}, u32[]{:S(2)}) %collective-permute-start.51) | collective-permute-done | bytes 131104 | tf_op jit(solution)/shard_map/ppermute | solution.py:32
  173.5 2.4 %collective-permute-done.52 = bf16[2,32,512]{2,1,0:T(8,128)(2,1)S(1)} collective-permute-done((bf16[2,32,512]{2,1,0:T(8,128)(2,1)S(1)}, bf16[2,32,512]{2,1,0:T(8,128)(2,1)S(1)}, u32[]{:S(2)}, u32[]{:S(2)}) %collective-permute-start.52) | collective-permute-done | bytes 65568 | tf_op jit(solution)/shard_map/ppermute | solution.py:32
  177.9 4.9 %collective-permute-done.31 = bf16[16,48,512]{2,1,0:T(8,128)(2,1)S(1)} collective-permute-done((bf16[16,48,512]{2,1,0:T(8,128)(2,1)S(1)}, bf16[16,48,512]{2,1,0:T(8,128)(2,1)S(1)}, u32[]{:S(2)}, u32[]{:S(2)}) %collective-permute-start.31) | collective-permute-done | bytes 786464 | tf_op jit(solution)/shard_map/ppermute | solution.py:32
  183.2 2.3 %collective-permute-start.34 = (bf16[8,48,512]{2,1,0:T(8,128)(2,1)S(1)}, bf16[8,48,512]{2,1,0:T(8,128)(2,1)S(1)}, u32[]{:S(2)}, u32[]{:S(2)}) collective-permute-start(bf16[8,48,512]{2,1,0:T(8,128)(2,1)S(1)} %slice.235), channel_id=1, source_target_pairs={{0,6},{8,14},{16,22},{24,30},{1,7},{9,15},{17,23},{25,31},{2,4},{1... | collective-permute-start | bytes 1179656 | tf_op jit(solution)/shard_map/ppermute | solution.py:32
  187.7 5.7 %collective-permute-done.34 = bf16[8,48,512]{2,1,0:T(8,128)(2,1)S(1)} collective-permute-done((bf16[8,48,512]{2,1,0:T(8,128)(2,1)S(1)}, bf16[8,48,512]{2,1,0:T(8,128)(2,1)S(1)}, u32[]{:S(2)}, u32[]{:S(2)}) %collective-permute-start.34) | collective-permute-done | bytes 393248 | tf_op jit(solution)/shard_map/ppermute | solution.py:32
  195.4 3.8 %collective-permute-done.35 = bf16[4,48,512]{2,1,0:T(8,128)(2,1)S(1)} collective-permute-done((bf16[4,48,512]{2,1,0:T(8,128)(2,1)S(1)}, bf16[4,48,512]{2,1,0:T(8,128)(2,1)S(1)}, u32[]{:S(2)}, u32[]{:S(2)}) %collective-permute-start.35) | collective-permute-done | bytes 196640 | tf_op jit(solution)/shard_map/ppermute | solution.py:32
  201.2 3.9 %collective-permute-done.36 = bf16[2,48,512]{2,1,0:T(8,128)(2,1)S(1)} collective-permute-done((bf16[2,48,512]{2,1,0:T(8,128)(2,1)S(1)}, bf16[2,48,512]{2,1,0:T(8,128)(2,1)S(1)}, u32[]{:S(2)}, u32[]{:S(2)}) %collective-permute-start.36) | collective-permute-done | bytes 98336 | tf_op jit(solution)/shard_map/ppermute | solution.py:32
  205.8 3.6 %collective-permute-done.37 = bf16[1,48,512]{2,1,0:T(8,128)(2,1)S(1)} collective-permute-done((bf16[1,48,512]{2,1,0:T(8,128)(2,1)S(1)}, bf16[1,48,512]{2,1,0:T(8,128)(2,1)S(1)}, u32[]{:S(2)}, u32[]{:S(2)}) %collective-permute-start.37) | collective-permute-done | bytes 49184 | tf_op jit(solution)/shard_map/ppermute | solution.py:32
  (201 shorter events, 55.0 us)
Async XLA Ops:
  0.0 16.6 %collective-permute-start.6 = (bf16[4,192,4096]{2,1,0:T(8,128)(2,1)}, bf16[4,192,4096]{2,1,0:T(8,128)(2,1)}, u32[]{:S(2)}, u32[]{:S(2)}) collective-permute-start(bf16[4,192,4096]{2,1,0:T(8,128)(2,1)} %wg.1), channel_id=1, source_target_pairs={{0,8},{8,0},{16,24},{24,16},{1,9},{9,1},{17,25},{25,17},{2,10},{10... | collective-permute-start | bytes 18874376 | tf_op jit(solution)/shard_map/ppermute | solution.py:37
  16.6 24.8 %collective-permute-start.13 = (bf16[4,192,4096]{2,1,0:T(8,128)(2,1)}, bf16[4,192,4096]{2,1,0:T(8,128)(2,1)}, u32[]{:S(2)}, u32[]{:S(2)}) collective-permute-start(bf16[4,192,4096]{2,1,0:T(8,128)(2,1)} %wu), channel_id=1, source_target_pairs={{0,8},{8,0},{16,24},{24,16},{1,9},{9,1},{17,25},{25,17},{2,10},{10... | collective-permute-start | bytes 18874376 | tf_op jit(solution)/shard_map/ppermute | solution.py:37
  16.7 10.2 %collective-permute-start.11 = (bf16[4,32,512]{2,1,0:T(8,128)(2,1)S(1)}, bf16[4,32,512]{2,1,0:T(8,128)(2,1)S(1)}, u32[]{:S(2)}, u32[]{:S(2)}) collective-permute-start(bf16[4,32,512]{2,1,0:T(8,128)(2,1)S(1)} %pad_maximum_fusion.14), channel_id=1, source_target_pairs={{0,32},{8,40},{16,48},{24,56},{1,33},{9,41},{17,49},{25,57},{2,34}... | collective-permute-start | bytes 393224 | tf_op jit(solution)/shard_map/ppermute | solution.py:32
  27.6 11.1 %collective-permute-start.8 = (bf16[8,48,512]{2,1,0:T(8,128)(2,1)S(1)}, bf16[8,48,512]{2,1,0:T(8,128)(2,1)S(1)}, u32[]{:S(2)}, u32[]{:S(2)}) collective-permute-start(bf16[8,48,512]{2,1,0:T(8,128)(2,1)S(1)} %pad_maximum_fusion.9), channel_id=1, source_target_pairs={{0,6},{8,14},{16,22},{24,30},{1,7},{9,15},{17,23},{25,31},{2,4},{1... | collective-permute-start | bytes 1179656 | tf_op jit(solution)/shard_map/ppermute | solution.py:32
  31.8 9.6 %collective-permute-start.10 = (bf16[8,48,512]{2,1,0:T(8,128)(2,1)S(1)}, bf16[8,48,512]{2,1,0:T(8,128)(2,1)S(1)}, u32[]{:S(2)}, u32[]{:S(2)}) collective-permute-start(bf16[8,48,512]{2,1,0:T(8,128)(2,1)S(1)} %pad_maximum_fusion.10), channel_id=1, source_target_pairs={{0,17},{8,25},{16,1},{24,9},{1,16},{9,24},{17,0},{25,8},{2,19},{10... | collective-permute-start | bytes 1179656 | tf_op jit(solution)/shard_map/ppermute | solution.py:32
  41.5 12.6 %collective-permute-start.26 = (bf16[16,32,512]{2,1,0:T(8,128)(2,1)S(1)}, bf16[16,32,512]{2,1,0:T(8,128)(2,1)S(1)}, u32[]{:S(2)}, u32[]{:S(2)}) collective-permute-start(bf16[16,32,512]{2,1,0:T(8,128)(2,1)S(1)} %pad_maximum_fusion.6), channel_id=1, source_target_pairs={{0,6},{8,14},{16,22},{24,30},{1,7},{9,15},{17,23},{25,31},{2,4},{1... | collective-permute-start | bytes 1572872 | tf_op jit(solution)/shard_map/ppermute | solution.py:32
  42.2 16.6 %collective-permute-start.18 = (bf16[16,48,512]{2,1,0:T(8,128)(2,1)S(1)}, bf16[16,48,512]{2,1,0:T(8,128)(2,1)S(1)}, u32[]{:S(2)}, u32[]{:S(2)}) collective-permute-start(bf16[16,48,512]{2,1,0:T(8,128)(2,1)S(1)} %pad_maximum_fusion), channel_id=1, source_target_pairs={{0,17},{8,25},{16,1},{24,9},{1,16},{9,24},{17,0},{25,8},{2,19},{10... | collective-permute-start | bytes 2359304 | tf_op jit(solution)/shard_map/ppermute | solution.py:32
  43.9 17.9 %collective-permute-start.17 = (bf16[16,48,512]{2,1,0:T(8,128)(2,1)S(1)}, bf16[16,48,512]{2,1,0:T(8,128)(2,1)S(1)}, u32[]{:S(2)}, u32[]{:S(2)}) collective-permute-start(bf16[16,48,512]{2,1,0:T(8,128)(2,1)S(1)} %pad_maximum_fusion), channel_id=1, source_target_pairs={{0,16},{8,24},{16,0},{24,8},{1,17},{9,25},{17,1},{25,9},{2,18},{10... | collective-permute-start | bytes 2359304 | tf_op jit(solution)/shard_map/ppermute | solution.py:32
  46.1 17.7 %collective-permute-start.22 = (bf16[16,48,512]{2,1,0:T(8,128)(2,1)S(1)}, bf16[16,48,512]{2,1,0:T(8,128)(2,1)S(1)}, u32[]{:S(2)}, u32[]{:S(2)}) collective-permute-start(bf16[16,48,512]{2,1,0:T(8,128)(2,1)S(1)} %pad_maximum_fusion.1), channel_id=1, source_target_pairs={{0,96},{8,104},{16,112},{24,120},{1,97},{9,105},{17,113},{25,121},... | collective-permute-start | bytes 2359304 | tf_op jit(solution)/shard_map/ppermute | solution.py:32
  48.0 17.0 %collective-permute-start.21 = (bf16[16,48,512]{2,1,0:T(8,128)(2,1)S(1)}, bf16[16,48,512]{2,1,0:T(8,128)(2,1)S(1)}, u32[]{:S(2)}, u32[]{:S(2)}) collective-permute-start(bf16[16,48,512]{2,1,0:T(8,128)(2,1)S(1)} %pad_maximum_fusion.1), channel_id=1, source_target_pairs={{0,32},{8,40},{16,48},{24,56},{1,33},{9,41},{17,49},{25,57},{2,34}... | collective-permute-start | bytes 2359304 | tf_op jit(solution)/shard_map/ppermute | solution.py:32
  54.0 13.2 %collective-permute-start.25 = (bf16[16,32,512]{2,1,0:T(8,128)(2,1)S(1)}, bf16[16,32,512]{2,1,0:T(8,128)(2,1)S(1)}, u32[]{:S(2)}, u32[]{:S(2)}) collective-permute-start(bf16[16,32,512]{2,1,0:T(8,128)(2,1)S(1)} %pad_maximum_fusion.6), channel_id=1, source_target_pairs={{0,2},{8,10},{16,18},{24,26},{1,3},{9,11},{17,19},{25,27},{2,0},{1... | collective-permute-start | bytes 1572872 | tf_op jit(solution)/shard_map/ppermute | solution.py:32
  58.8 11.2 %collective-permute-start.28 = (bf16[8,32,512]{2,1,0:T(8,128)(2,1)S(1)}, bf16[8,32,512]{2,1,0:T(8,128)(2,1)S(1)}, u32[]{:S(2)}, u32[]{:S(2)}) collective-permute-start(bf16[8,32,512]{2,1,0:T(8,128)(2,1)S(1)} %slice.233), channel_id=1, source_target_pairs={{0,2},{8,10},{16,18},{24,26},{1,3},{9,11},{17,19},{25,27},{2,0},{1... | collective-permute-start | bytes 786440 | tf_op jit(solution)/shard_map/ppermute | solution.py:32
  61.8 15.8 %collective-permute-start.20 = (bf16[8,48,512]{2,1,0:T(8,128)(2,1)S(1)}, bf16[8,48,512]{2,1,0:T(8,128)(2,1)}, u32[]{:S(2)}, u32[]{:S(2)}) collective-permute-start(bf16[8,48,512]{2,1,0:T(8,128)(2,1)S(1)} %slice.229), channel_id=1, source_target_pairs={{0,16},{8,24},{16,0},{24,8},{1,17},{9,25},{17,1},{25,9},{2,18},{10... | collective-permute-start | bytes 1179656 | tf_op jit(solution)/shard_map/ppermute | solution.py:32
  63.9 13.7 %collective-permute-start.19 = (bf16[8,48,512]{2,1,0:T(8,128)(2,1)S(1)}, bf16[8,48,512]{2,1,0:T(8,128)(2,1)S(1)}, u32[]{:S(2)}, u32[]{:S(2)}) collective-permute-start(bf16[8,48,512]{2,1,0:T(8,128)(2,1)S(1)} %slice.228), channel_id=1, source_target_pairs={{0,17},{8,25},{16,1},{24,9},{1,16},{9,24},{17,0},{25,8},{2,19},{10... | collective-permute-start | bytes 1179656 | tf_op jit(solution)/shard_map/ppermute | solution.py:32
  65.0 12.6 %collective-permute-start.24 = (bf16[8,48,512]{2,1,0:T(8,128)(2,1)S(1)}, bf16[8,48,512]{2,1,0:T(8,128)(2,1)S(1)}, u32[]{:S(2)}, u32[]{:S(2)}) collective-permute-start(bf16[8,48,512]{2,1,0:T(8,128)(2,1)S(1)} %slice.231), channel_id=1, source_target_pairs={{0,32},{8,40},{16,48},{24,56},{1,33},{9,41},{17,49},{25,57},{2,34}... | collective-permute-start | bytes 1179656 | tf_op jit(solution)/shard_map/ppermute | solution.py:32
  67.2 10.4 %collective-permute-start.23 = (bf16[8,48,512]{2,1,0:T(8,128)(2,1)S(1)}, bf16[8,48,512]{2,1,0:T(8,128)(2,1)S(1)}, u32[]{:S(2)}, u32[]{:S(2)}) collective-permute-start(bf16[8,48,512]{2,1,0:T(8,128)(2,1)S(1)} %slice.230), channel_id=1, source_target_pairs={{0,96},{8,104},{16,112},{24,120},{1,97},{9,105},{17,113},{25,121},... | collective-permute-start | bytes 1179656 | tf_op jit(solution)/shard_map/ppermute | solution.py:32
  77.7 24.2 %collective-permute-start.29 = (bf16[4,192,4096]{2,1,0:T(8,128)(2,1)}, bf16[4,192,4096]{2,1,0:T(8,128)(2,1)}, u32[]{:S(2)}, u32[]{:S(2)}) collective-permute-start(bf16[4,192,4096]{2,1,0:T(8,128)(2,1)} %wd), channel_id=1, source_target_pairs={{0,8},{8,0},{16,24},{24,16},{1,9},{9,1},{17,25},{25,17},{2,10},{10... | collective-permute-start | bytes 18874376 | tf_op jit(solution)/shard_map/ppermute | solution.py:37
  119.2 10.3 %collective-permute-start.46 = (bf16[8,32,512]{2,1,0:T(8,128)(2,1)}, bf16[8,32,512]{2,1,0:T(8,128)(2,1)S(1)}, u32[]{:S(2)}, u32[]{:S(2)}) collective-permute-start(bf16[8,32,512]{2,1,0:T(8,128)(2,1)} %bitcast.102), channel_id=1, source_target_pairs={{0,6},{8,14},{16,22},{24,30},{1,7},{9,15},{17,23},{25,31},{2,4},{1... | collective-permute-start | bytes 786440 | tf_op jit(solution)/shard_map/ppermute | solution.py:32
  119.9 35.1 %collective-permute-start.30 = (bf16[8,48,512]{2,1,0:T(8,128)(2,1)}, bf16[8,48,512]{2,1,0:T(8,128)(2,1)S(1)}, u32[]{:S(2)}, u32[]{:S(2)}) collective-permute-start(bf16[8,48,512]{2,1,0:T(8,128)(2,1)} %bitcast.98), channel_id=1, source_target_pairs={{0,17},{8,25},{16,1},{24,9},{1,16},{9,24},{17,0},{25,8},{2,19},{10... | collective-permute-start | bytes 1179656 | tf_op jit(solution)/shard_map/ppermute | solution.py:32
  121.1 22.5 %collective-permute-start.32 = (bf16[8,48,512]{2,1,0:T(8,128)(2,1)}, bf16[8,48,512]{2,1,0:T(8,128)(2,1)S(1)}, u32[]{:S(2)}, u32[]{:S(2)}) collective-permute-start(bf16[8,48,512]{2,1,0:T(8,128)(2,1)} %bitcast.99), channel_id=1, source_target_pairs={{0,16},{8,24},{16,0},{24,8},{1,17},{9,25},{17,1},{25,9},{2,18},{10... | collective-permute-start | bytes 1179656 | tf_op jit(solution)/shard_map/ppermute | solution.py:32
  124.0 17.5 %collective-permute-start.38 = (bf16[8,48,512]{2,1,0:T(8,128)(2,1)}, bf16[8,48,512]{2,1,0:T(8,128)(2,1)S(1)}, u32[]{:S(2)}, u32[]{:S(2)}) collective-permute-start(bf16[8,48,512]{2,1,0:T(8,128)(2,1)} %bitcast.100), channel_id=1, source_target_pairs={{0,96},{8,104},{16,112},{24,120},{1,97},{9,105},{17,113},{25,121},... | collective-permute-start | bytes 1179656 | tf_op jit(solution)/shard_map/ppermute | solution.py:32
  129.2 10.4 %collective-permute-start.40 = (bf16[8,48,512]{2,1,0:T(8,128)(2,1)S(1)}, bf16[8,48,512]{2,1,0:T(8,128)(2,1)S(1)}, u32[]{:S(2)}, u32[]{:S(2)}) collective-permute-start(bf16[8,48,512]{2,1,0:T(8,128)(2,1)S(1)} %bitcast.101), channel_id=1, source_target_pairs={{0,32},{8,40},{16,48},{24,56},{1,33},{9,41},{17,49},{25,57},{2,34}... | collective-permute-start | bytes 1179656 | tf_op jit(solution)/shard_map/ppermute | solution.py:32
  129.5 14.6 %collective-permute-start.49 = (bf16[16,32,512]{2,1,0:T(8,128)(2,1)S(1)}, bf16[16,32,512]{2,1,0:T(8,128)(2,1)S(1)}, u32[]{:S(2)}, u32[]{:S(2)}) collective-permute-start(bf16[16,32,512]{2,1,0:T(8,128)(2,1)S(1)} %pad_maximum_fusion.8), channel_id=1, source_target_pairs={{0,6},{8,14},{16,22},{24,30},{1,7},{9,15},{17,23},{25,31},{2,4},{1... | collective-permute-start | bytes 1572872 | tf_op jit(solution)/shard_map/ppermute | solution.py:32
  139.6 12.2 %collective-permute-start.47 = (bf16[16,32,512]{2,1,0:T(8,128)(2,1)S(1)}, bf16[16,32,512]{2,1,0:T(8,128)(2,1)S(1)}, u32[]{:S(2)}, u32[]{:S(2)}) collective-permute-start(bf16[16,32,512]{2,1,0:T(8,128)(2,1)S(1)} %pad_maximum_fusion.7), channel_id=1, source_target_pairs={{0,2},{8,10},{16,18},{24,26},{1,3},{9,11},{17,19},{25,27},{2,0},{1... | collective-permute-start | bytes 1572872 | tf_op jit(solution)/shard_map/ppermute | solution.py:32
  141.5 30.7 %collective-permute-start.41 = (bf16[16,48,512]{2,1,0:T(8,128)(2,1)S(1)}, bf16[16,48,512]{2,1,0:T(8,128)(2,1)S(1)}, u32[]{:S(2)}, u32[]{:S(2)}) collective-permute-start(bf16[16,48,512]{2,1,0:T(8,128)(2,1)S(1)} %pad_maximum_fusion.5), channel_id=1, source_target_pairs={{0,96},{8,104},{16,112},{24,120},{1,97},{9,105},{17,113},{25,121},... | collective-permute-start | bytes 2359304 | tf_op jit(solution)/shard_map/ppermute | solution.py:32
  143.6 28.6 %collective-permute-start.39 = (bf16[16,48,512]{2,1,0:T(8,128)(2,1)S(1)}, bf16[16,48,512]{2,1,0:T(8,128)(2,1)S(1)}, u32[]{:S(2)}, u32[]{:S(2)}) collective-permute-start(bf16[16,48,512]{2,1,0:T(8,128)(2,1)S(1)} %pad_maximum_fusion.4), channel_id=1, source_target_pairs={{0,32},{8,40},{16,48},{24,56},{1,33},{9,41},{17,49},{25,57},{2,34}... | collective-permute-start | bytes 2359304 | tf_op jit(solution)/shard_map/ppermute | solution.py:32
  152.2 13.6 %collective-permute-start.50 = (bf16[8,32,512]{2,1,0:T(8,128)(2,1)S(1)}, bf16[8,32,512]{2,1,0:T(8,128)(2,1)S(1)}, u32[]{:S(2)}, u32[]{:S(2)}) collective-permute-start(bf16[8,32,512]{2,1,0:T(8,128)(2,1)S(1)} %slice.251), channel_id=1, source_target_pairs={{0,96},{8,104},{16,112},{24,120},{1,97},{9,105},{17,113},{25,121},... | collective-permute-start | bytes 786440 | tf_op jit(solution)/shard_map/ppermute | solution.py:32
  154.1 23.7 %collective-permute-start.33 = (bf16[16,48,512]{2,1,0:T(8,128)(2,1)S(1)}, bf16[16,48,512]{2,1,0:T(8,128)(2,1)S(1)}, u32[]{:S(2)}, u32[]{:S(2)}) collective-permute-start(bf16[16,48,512]{2,1,0:T(8,128)(2,1)S(1)} %pad_maximum_fusion.3), channel_id=1, source_target_pairs={{0,17},{8,25},{16,1},{24,9},{1,16},{9,24},{17,0},{25,8},{2,19},{10... | collective-permute-start | bytes 2359304 | tf_op jit(solution)/shard_map/ppermute | solution.py:32
  166.0 16.8 %collective-permute-start.31 = (bf16[16,48,512]{2,1,0:T(8,128)(2,1)S(1)}, bf16[16,48,512]{2,1,0:T(8,128)(2,1)S(1)}, u32[]{:S(2)}, u32[]{:S(2)}) collective-permute-start(bf16[16,48,512]{2,1,0:T(8,128)(2,1)S(1)} %pad_maximum_fusion.2), channel_id=1, source_target_pairs={{0,16},{8,24},{16,0},{24,8},{1,17},{9,25},{17,1},{25,9},{2,18},{10... | collective-permute-start | bytes 2359304 | tf_op jit(solution)/shard_map/ppermute | solution.py:32
  172.7 12.9 %collective-permute-start.42 = (bf16[8,48,512]{2,1,0:T(8,128)(2,1)S(1)}, bf16[8,48,512]{2,1,0:T(8,128)(2,1)S(1)}, u32[]{:S(2)}, u32[]{:S(2)}) collective-permute-start(bf16[8,48,512]{2,1,0:T(8,128)(2,1)S(1)} %slice.243), channel_id=1, source_target_pairs={{0,17},{8,25},{16,1},{24,9},{1,16},{9,24},{17,0},{25,8},{2,19},{10... | collective-permute-start | bytes 1179656 | tf_op jit(solution)/shard_map/ppermute | solution.py:32
  176.0 9.6 %collective-permute-start.53 = (bf16[1,32,512]{2,1,0:T(8,128)(2,1)S(1)}, bf16[1,32,512]{2,1,0:T(8,128)(2,1)S(1)}, u32[]{:S(2)}, u32[]{:S(2)}) collective-permute-start(bf16[1,32,512]{2,1,0:T(8,128)(2,1)S(1)} %slice.257), channel_id=1, source_target_pairs={{0,16},{8,24},{16,0},{24,8},{1,17},{9,25},{17,1},{25,9},{2,18},{10... | collective-permute-start | bytes 98312 | tf_op jit(solution)/shard_map/ppermute | solution.py:32
  183.2 10.1 %collective-permute-start.34 = (bf16[8,48,512]{2,1,0:T(8,128)(2,1)S(1)}, bf16[8,48,512]{2,1,0:T(8,128)(2,1)S(1)}, u32[]{:S(2)}, u32[]{:S(2)}) collective-permute-start(bf16[8,48,512]{2,1,0:T(8,128)(2,1)S(1)} %slice.235), channel_id=1, source_target_pairs={{0,6},{8,14},{16,22},{24,30},{1,7},{9,15},{17,23},{25,31},{2,4},{1... | collective-permute-start | bytes 1179656 | tf_op jit(solution)/shard_map/ppermute | solution.py:32
  (46 other events, 353.7 us)

commit v3 on v0

v3 whole, which is shorter than its diff:
```python
import functools

import jax
import jax.numpy as jnp
from jax import lax
from jax.experimental import pallas as pl
from jax.experimental.pallas import tpu as pltpu
from jax.sharding import PartitionSpec as P

AXES = ("expert", "tensor")
OFF = (0, 1, 3, 2)
Z_OFF = (OFF, (0, 3, 1, 2), OFF)
LAST = (2, 0, 1)
MIDDLE = (1, 2, 2)
MASKS = ((1, 3), (3, 1), (1, 3))
ROWS = (48, 48, 32)
VMEM_EXPERTS = 46 * 2**20
FIRST = (0, 48, 96)
BF16 = jnp.bfloat16
F32 = jnp.float32


def device_number(x, y, z, core):
    return (x * 4 + (z % 2) * 2 + core) * 8 + y * 2 + z // 2


def places():
    return [(x, y, z, c) for x in range(4) for y in range(4) for z in range(4) for c in range(2)]


def swap(value, dim, mask):
    pairs = []
    for place in places():
        other = list(place)
        other[dim] ^= mask
        pairs.append((device_number(*place), device_number(*other)))
    return lax.ppermute(value, AXES, pairs)


def from_other_core(value):
    pairs = [(device_number(x, y, z, c), device_number(x, y, z, 1 - c)) for x, y, z, c in places()]
    return lax.ppermute(value, AXES, pairs)


def join(*arrays):
    return jnp.concatenate(arrays, 0)


def gather_last(parts):
    a, b, c = parts
    one_c = swap(c, LAST[2], 1)
    one_a, one_b = swap(a, LAST[0], 1), swap(b, LAST[1], 1)
    three_a, three_b = swap(a, LAST[0], 3), swap(b, LAST[1], 3)
    two_c = swap(one_c, LAST[2], 3)
    c, one_a = lax.optimization_barrier((c, one_a))
    three_c = swap(c, LAST[2], 3)
    two_a = swap(one_a[:8], LAST[0], 3), swap(three_a[8:], LAST[0], 1)
    two_b = swap(one_b[:8], LAST[1], 3), swap(three_b[8:], LAST[1], 1)
    return [a, one_a, three_a, *two_a, b, one_b, three_b, *two_b, c, one_c, three_c, two_c]


def total(own, *others):
    out = own.astype(F32)
    for other in others:
        out = out + other.astype(F32)
    return out.astype(BF16)


def scatter_sums(first, second):
    z_f, x_f, (y_three, y_two) = first[0:4], first[4:8], first[8:]
    z_s, x_s, (y_own, y_one) = second[0:4], second[4:8], second[8:]
    z, x, y = 2, 0, 1
    z_a, x_a = swap(z_f[3], z, 3), swap(x_f[3], x, 3)
    y_a = swap(y_two, y, 3)
    z_b, x_b = swap(z_s[3], z, 1), swap(x_s[3], x, 1)
    y_three = swap(y_three, y, 3)
    y_one = swap(y_one + y_a, y, 1)
    z_one = swap(join(z_f[1] + z_a, z_s[1]), z, 1)
    x_one = swap(join(x_f[1] + x_a, x_s[1]), x, 1)
    z_three = swap(join(z_f[2], z_s[2] + z_b), z, 3)
    x_three = swap(join(x_f[2], x_s[2] + x_b), x, 3)
    x_t = [
        total(x_s[0], x_one[4:], x_three[4:]),
        total(x_f[0], x_one[:4], x_three[:4]),
    ]
    x_t = jnp.concatenate(x_t, 1)
    y_t = total(y_own, y_one, y_three)
    keep = [total(z_s[0], z_one[2:], z_three[2:]), x_t[:2], y_t[:2]]
    send = [total(z_f[0], z_one[:2], z_three[:2]), x_t[2:], y_t[2:]]
    held = [keep[i] + swap(send[i], MIDDLE[i], MASKS[i][1]) for i in range(3)]
    held = [held[i][0] + swap(held[i][1], MIDDLE[i], MASKS[i][0]) for i in range(3)]
    pair = [jnp.concatenate([held[0], held[2]], 1), held[1]]
    for mask, half in ((3, 2), (1, 1)):
        got = [swap(p[half:], dim, mask) for dim, p in enumerate(pair)]
        pair = [p[:half] + g for p, g in zip(pair, got)]
    return join(pair[0][0, :48], pair[1][0], pair[0][0, 48:])


def gathered(refs, i, k3, k2, k1):
    k1 = slice(None) if k1 is None else k1
    group = refs[i * 5 : i * 5 + 5]
    if k3 < 3 or i == 2:
        return group[k3].at[k2, k1]
    return group[3 + k2 // 2].at[k2 % 2, k1]


def spread_out(kys):
    def find(refs, i, k3, k2, k1):
        if i == 0:
            return refs[k3].at[kys.index(k2)]
        if i == 1:
            return refs[4 + k3].at[k2, kys.index(k1)]
        return refs[8 + kys.index(k3)].at[k2]

    return find


def block_pieces(refs, piece, tile, column, ky, bits):
    low, high = bits
    rows = [pl.ds(first, count) for first, count in zip(FIRST, ROWS)]
    kz = [off.index(high * 2 + low) for off in Z_OFF]
    cols = column(ky, high)
    found = [(piece(refs, 0, kz[0], ky, None), tile.at[:, low, rows[0], cols])]
    for kx in range(4):
        found.append((piece(refs, 1, kx, kz[1], ky), tile.at[kx, low, rows[1], cols]))
    found.append((piece(refs, 2, ky, kz[2], None), tile.at[:, low, rows[2], cols]))
    return found


BITS = [(low, high) for low in range(2) for high in range(2)]


def route(ids_ref, mine_ref, gate_col, pick, put):
    before = lax.broadcasted_iota(jnp.int32, (128, 128), 0)
    before = (before < lax.broadcasted_iota(jnp.int32, (128, 128), 1)).astype(BF16)
    number = lax.broadcasted_iota(jnp.int32, (8, 32, 128), 1).astype(F32)
    line = lax.broadcasted_iota(jnp.int32, (8, 128), 0)

    def block(b, carry):
        mine = mine_ref[b].astype(F32)[0:8]
        routes = mine[:, 0:128]
        gates = mine[:, 128:256] + mine[:, 256:384] + mine[:, 384:512]
        named = jnp.zeros((8, 128), F32)
        weight = jnp.zeros((8, 128), F32)
        for e in range(8):
            hit = routes == ids_ref[e]
            any_hit = jnp.max(jnp.where(hit, 1.0, 0.0), axis=0, keepdims=True)
            gate = jnp.sum(jnp.where(hit, gates, 0.0), axis=0, keepdims=True)
            named = jnp.where(line == e, any_hit, named)
            weight = jnp.where(line == e, gate, weight)
        slot = jnp.dot(named.astype(BF16), before, preferred_element_type=F32)
        slot = jnp.where(named > 0, slot, -1.0)
        chosen = slot[:, None, :] == number
        one_hot = jnp.where(chosen, 1.0, 0.0).reshape(256, 128)
        pick[b] = one_hot.astype(BF16)
        put[b] = one_hot.T.astype(BF16)
        rows = pl.ds(pl.multiple_of(b * 32, 32), 32)
        gate_col[:, rows, :] = jnp.sum(
            jnp.where(chosen, weight[:, None, :], 0.0), axis=2, keepdims=True
        )
        return carry

    lax.fori_loop(0, 8, block, 0)


def y_pairs(outs, kys, n, cols_ref, tile):
    def column(ky, high):
        side = lax.rem(cols_ref[ky * 2 + high], 2)
        return pl.ds(pl.multiple_of(side * 512, 512), 512)

    find = spread_out(kys)
    return [
        pair for bits in BITS for pair in block_pieces(outs, find, tile, column, kys[n], bits)
    ]


def columns_of(cols_ref, ky):
    return pl.ds(pl.multiple_of(cols_ref[ky * 2] // 2 * 1024, 1024), 1024)


def expert_kernel(kys, ids_ref, cols_ref, mine_ref, wg, wu, wg2, wu2, wd, wd2, *rest):
    token_refs, rest = rest[:14], rest[14:]
    (h_ref, put), outs = rest[:2], rest[2:-7]
    tokens, sorted_rows, wbuf, gate_col, pick, t_sem, w_sem = rest[-7:]
    d_sem = t_sem.at[0]

    def fetch(e, j, gate, up):
        return [
            pltpu.make_async_copy(gate.at[e], wbuf.at[j, pl.ds(0, 192)], w_sem.at[j, 0]),
            pltpu.make_async_copy(up.at[e], wbuf.at[j, pl.ds(192, 192)], w_sem.at[j, 1]),
        ]

    def load(ky):
        def column(ky, high):
            return pl.ds(pl.multiple_of(cols_ref[ky * 2 + high] * 512, 512), 512)

        pairs = [
            pair
            for bits in BITS
            for pair in block_pieces(token_refs, gathered, tokens, column, ky, bits)
        ]
        return [pltpu.make_async_copy(a, b, t_sem.at[ky, m]) for m, (a, b) in enumerate(pairs)]

    def down_tile(slot, e):
        return wbuf.at[slot, pl.ds(e // 4 * 192, 192), pl.ds(e % 4 * 1024, 1024)]

    def fetch_down(n):
        col = columns_of(cols_ref, kys[n])
        return [
            pltpu.make_async_copy(
                (wd if e < 4 else wd2).at[e % 4, :, col], down_tile(n, e), d_sem.at[n * 8 + e]
            )
            for e in range(8)
        ]

    loads = [load(ky) for ky in range(4)]
    for ky in range(4):
        for copy in loads[ky]:
            copy.start()
    for j in range(2):
        for copy in fetch(j, j, wg, wu):
            copy.start()
    route(ids_ref, mine_ref, gate_col, pick, put)
    for ky in range(4):
        for copy in loads[ky]:
            copy.wait()
        if ky < 2:
            for copy in fetch(ky + 2, ky + 2, wg, wu):
                copy.start()
        col = columns_of(cols_ref, ky)

        def dispatch(b, carry):
            rows = jnp.dot(
                pick[b], tokens[b // 2, lax.rem(b, 2), :, col], preferred_element_type=F32
            )
            rows = rows.astype(BF16).reshape(4, 2, 32, 1024)
            sorted_rows[:, :, pl.ds(pl.multiple_of(b * 32, 32), 32), col] = rows
            return carry

        lax.fori_loop(0, 8, dispatch, 0, unroll=2)

    def experts(turn, carry):
        for j in range(4):
            e = turn * 4 + j
            for copy in fetch(j, j, wg, wu):
                copy.wait()
            act = lax.dot_general(
                sorted_rows[turn * 2 + j // 2, j % 2],
                wbuf[j],
                (((1,), (1,)), ((), ())),
                preferred_element_type=F32,
            )
            gate, up = act[:, :192], act[:, 192:]
            hidden = gate / (1.0 + jnp.exp(-gate)) * up * gate_col[e]
            h_ref[e] = hidden.astype(BF16)

            @pl.when(turn == 0)
            def _():
                for copy in fetch(j, j, wg2, wu2):
                    copy.start()

            if j < 2:

                @pl.when(turn == 1)
                def _():
                    for copy in fetch_down(j):
                        copy.start()

        return carry

    lax.fori_loop(0, 2, experts, 0)
    for n in range(2):
        for copy in fetch_down(n):
            copy.wait()
        for e in range(8):
            out = jnp.dot(h_ref[e], down_tile(n, e)[...], preferred_element_type=F32)
            sorted_rows[:, :, pl.ds(e * 32, 32), pl.ds(0, 1024)] = out.astype(BF16).reshape(
                4, 2, 32, 1024
            )
        col = pl.ds(1024 * (n + 1), 1024)

        def combine(b, carry):
            at = b // 2, lax.rem(b, 2)
            out = jnp.dot(
                put[b], sorted_rows[at[0], at[1], :, pl.ds(0, 1024)], preferred_element_type=F32
            )
            sorted_rows[at[0], at[1], pl.ds(0, 128), col] = out.astype(BF16)
            return carry

        lax.fori_loop(0, 8, combine, 0, unroll=2)
        tile = sorted_rows.at[:, :, pl.ds(0, 128), col]
        stores = [
            pltpu.make_async_copy(b, a, t_sem.at[2 + n, m])
            for m, (a, b) in enumerate(y_pairs(outs, kys, n, cols_ref, tile))
        ]
        for copy in stores:
            copy.start()
        if n == 0:
            first_stores = stores
    for copy in first_stores + stores:
        copy.wait()


def down_kernel(kys, cols_ref, h_ref, put_ref, wd, wd2, *rest):
    outs = rest[:-7]
    h, put, wbuf, expert_rows, ybuf, w_sem, y_sem = rest[-7:]

    def fetch(n):
        col = columns_of(cols_ref, kys[n])
        return [
            pltpu.make_async_copy(wd.at[:, :, col], wbuf.at[n, pl.ds(0, 4)], w_sem.at[n, 0]),
            pltpu.make_async_copy(wd2.at[:, :, col], wbuf.at[n, pl.ds(4, 4)], w_sem.at[n, 1]),
        ]

    def stores(n):
        pairs = y_pairs(outs, kys, n, cols_ref, ybuf.at[n])
        return [pltpu.make_async_copy(b, a, y_sem.at[n, m]) for m, (a, b) in enumerate(pairs)]

    inputs = [
        pltpu.make_async_copy(h_ref, h, w_sem.at[2, 0]),
        pltpu.make_async_copy(put_ref, put, w_sem.at[2, 1]),
    ]
    for copy in inputs + fetch(0) + fetch(1):
        copy.start()
    for copy in inputs:
        copy.wait()
    for n in range(2):
        for copy in fetch(n):
            copy.wait()

        def project(e, carry):
            out = jnp.dot(h[e], wbuf[n, e], preferred_element_type=F32)
            rows = pl.ds(pl.multiple_of(e * 32, 32), 32)
            expert_rows[:, rows] = out.astype(BF16).reshape(8, 32, 1024)
            return carry

        lax.fori_loop(0, 8, project, 0, unroll=2)

        def combine(b, carry):
            out = jnp.dot(put[b], expert_rows[b], preferred_element_type=F32)
            ybuf[n, b // 2, lax.rem(b, 2)] = out.astype(BF16)
            return carry

        lax.fori_loop(0, 8, combine, 0, unroll=2)
        for copy in stores(n):
            copy.start()
    for n in range(2):
        for copy in stores(n):
            copy.wait()


def local(tokens, routes, gates, w_gate, w_up, w_down):
    e, t = lax.axis_index("expert"), lax.axis_index("tensor")
    y, zhi = t // 2, t % 2
    ids = jnp.concatenate([e * 4 + jnp.arange(4), (e ^ 1) * 4 + jnp.arange(4)]).astype(F32)
    cols = jnp.stack([(y ^ OFF[ky]) * 2 + (zhi ^ high) for ky in range(4) for high in range(2)])
    cols = cols.astype(jnp.int32)

    top = lax.reduce_precision(gates, 8, 7)
    rest = gates - top
    middle = lax.reduce_precision(rest, 8, 7)
    packed = jnp.concatenate([part.T for part in (routes.astype(F32), top, middle, rest - middle)], 1)
    packed = jnp.pad(packed.astype(BF16), ((0, 8), (0, 0)))

    wg2 = from_other_core(w_gate)
    along_x = join(tokens[:48], tokens[96:], packed)[None]
    along_y = tokens[48:96][None]
    for mask in (1, 3):
        got = swap(along_x, 0, mask), swap(along_y, 1, mask)
        along_x, along_y = join(along_x, got[0]), join(along_y, got[1])
    along_x, along_y, wg2, w_up = lax.optimization_barrier((along_x, along_y, wg2, w_up))
    wu2 = from_other_core(w_up)
    parts = [along_x[:, :48], along_y, along_x[:, 48:]]
    parts = [join(p, swap(p, MIDDLE[i], MASKS[i][0])) for i, p in enumerate(parts)]
    mine = parts[2][:, 32:].reshape(2, 4, 16, 512)
    mine = jnp.swapaxes(mine, 0, 1).reshape(8, 16, 512)
    parts[2] = parts[2][:, :32]
    parts, wu2, w_down, mine, ids, cols = lax.optimization_barrier(
        (parts, wu2, w_down, mine, ids, cols)
    )
    wd2 = from_other_core(w_down)
    parts = [join(p, swap(p, MIDDLE[i], MASKS[i][1])) for i, p in enumerate(parts)]
    parts, wd2 = lax.optimization_barrier((parts, wd2))
    parts = gather_last(parts)
    pieces = [p.reshape(p.shape[0] // 4, 4, p.shape[1], 512) for p in parts]
    smem = pl.BlockSpec(memory_space=pltpu.SMEM)
    vmem = pl.BlockSpec(memory_space=pltpu.VMEM)
    hbm = pl.BlockSpec(memory_space=pl.ANY)
    shapes = [(2, 4, ROWS[0], 512)] * 4 + [(4, 2, ROWS[1], 512)] * 4
    shapes = [
        jax.ShapeDtypeStruct(shape, BF16) for shape in shapes + [(4, 4, ROWS[2], 512)] * 2
    ]
    hidden, put, *first = pl.pallas_call(
        functools.partial(expert_kernel, (2, 3)),
        out_shape=[
            jax.ShapeDtypeStruct((8, 256, 192), BF16),
            jax.ShapeDtypeStruct((8, 128, 256), BF16),
        ]
        + shapes,
        in_specs=[smem, smem, vmem] + [hbm] * 20,
        out_specs=[vmem, vmem] + [hbm] * 10,
        scratch_shapes=[
            pltpu.VMEM((4, 2, 128, 4096), BF16),
            pltpu.VMEM((4, 2, 256, 4096), BF16),
            pltpu.VMEM((4, 384, 4096), BF16),
            pltpu.VMEM((8, 256, 1), F32),
            pltpu.VMEM((8, 256, 128), BF16),
            pltpu.SemaphoreType.DMA((4, 24)),
            pltpu.SemaphoreType.DMA((4, 2)),
        ],
        compiler_params=pltpu.CompilerParams(vmem_limit_bytes=VMEM_EXPERTS),
        cost_estimate=pl.CostEstimate(
            flops=20 * 10**9, bytes_accessed=50 * 10**6, transcendentals=0
        ),
        name="experts",
    )(ids, cols, mine, w_gate, w_up, wg2, wu2, w_down, wd2, *pieces)

    second = pl.pallas_call(
        functools.partial(down_kernel, (0, 1)),
        out_shape=shapes,
        in_specs=[smem] + [hbm] * 4,
        out_specs=[hbm] * 10,
        scratch_shapes=[
            pltpu.VMEM((8, 256, 192), BF16),
            pltpu.VMEM((8, 128, 256), BF16),
            pltpu.VMEM((2, 8, 192, 1024), BF16),
            pltpu.VMEM((8, 256, 1024), BF16),
            pltpu.VMEM((2, 4, 2, 128, 1024), BF16),
            pltpu.SemaphoreType.DMA((3, 2)),
            pltpu.SemaphoreType.DMA((2, 24)),
        ],
        compiler_params=pltpu.CompilerParams(vmem_limit_bytes=50 * 2**20),
        cost_estimate=pl.CostEstimate(
            flops=6 * 10**9, bytes_accessed=12 * 10**6, transcendentals=0
        ),
        name="down",
    )(cols, hidden, put, w_down, wd2)
    return scatter_sums(first, second)


def solution(mesh):
    placed = (
        P("expert", "tensor"),
        P("expert", None),
        P("expert", None),
        P("expert", "tensor", None),
        P("expert", "tensor", None),
        P("expert", "tensor", None),
    )
    return jax.shard_map(
        local, mesh=mesh, in_specs=placed, out_specs=P("expert", "tensor"), check_vma=False
    )
```

time: 746 us -> 196 us (0.26)
  waiting for transfers between devices: 416 us -> 93.6 us
  blocking collectives: 191 us -> 0 us
  local copies, waits for them, and re-layouts: 60.1 us -> 5.37 us
  starting transfers between devices: 6.84 us -> 49 us
  Pallas kernels: 0 us -> 41.1 us
  matrix products: 35.2 us -> 0 us
  other arithmetic: 21.6 us -> 5.68 us
  between operations: 13.5 us -> 0.59 us
    all_to_all x1 -> x0, waiting for transfers between devices: 249 us -> none  [local(): lax.all_to_all(partials.reshape(group_count, local_experts * capacity, mo...]
    all_to_all x1 -> x0, blocking collectives: 191 us -> none  [local(): lax.all_to_all(buffer.reshape(group_count, local_experts * capacity, mode...]
    reduce_scatter x1 -> x0, waiting for transfers between devices: 135 us -> none  [local(): lax.psum_scatter(picked.astype(jnp.bfloat16), 'tensor', scatter_dimension...]
    ppermute x0 -> x45, waiting for transfers between devices: none -> 93.6 us  [the longest x42 92.4 us: swap(): return lax.ppermute(value, AXES, pairs)]
    ppermute x0 -> x45, starting transfers between devices: none -> 49 us  [the longest x42 48.8 us: swap(): return lax.ppermute(value, AXES, pairs)]
    pallas_call x0 -> x2, Pallas kernels: none -> 41.1 us  [the longest x1 30.4 us: local(): pl.pallas_call(functools.partial(expert_kernel, (2, 3)), out_shape=[jax.S...]
    dot_general x2 -> x0, matrix products: 35.2 us -> none  [the longest x1 25.2 us: local(): jnp.einsum('escf,efd->secd', hidden, w_down, preferred_element_type=jnp.f...]
    all_gather x1 -> x0, waiting for transfers between devices: 31.3 us -> none  [local(): owner_rows = lax.all_gather(tokens, 'tensor', axis=1, tiled=True)]
  transfers between devices with their start and end apart: 3 -> 45, of which waited for: 3 -> 23; matrix products, arithmetic and copies ran while one was open for 3% -> 4% of each run, Pallas kernels for 0% -> 5%
where the time goes in v3:
time: 196 us; the launch traced here: 195 us
  waiting for transfers between devices  93.6 us (48%)
  starting transfers between devices  49 us (25%)
  Pallas kernels  41.1 us (21%)
  other arithmetic  5.68 us (3%)
  local copies, waits for them, and re-layouts  5.37 us (3%)
    ppermute x42, waiting for transfers between devices, swap(): return lax.ppermute(value, AXES, pairs)  92.4 us
    ppermute x42, starting transfers between devices, swap(): return lax.ppermute(value, AXES, pairs)  48.8 us
    pallas_call x1, Pallas kernels, local(): pl.pallas_call(functools.partial(expert_kernel, (2, 3)), out_shape=[jax.S...  30.4 us
    pallas_call x1, Pallas kernels, local(): pl.pallas_call(functools.partial(down_kernel, (0, 1)), out_shape=shapes,...  10.6 us
  transfers between devices with their start and end apart: 45, of which 23 were waited for; matrix products, arithmetic and copies ran while one was open for 4% of the time, Pallas kernels for 5%

profile of v3, /device:TPU:32, one launch (start us, length us, event | category | flops | bytes accessed | tf_op | source)
XLA Modules:
  0.0 195.3 jit_solution(5430330189601154783)
XLA Ops:
  6.2 2.3 %collective-permute-start.3 = (bf16[2,48,512]{2,1,0:T(8,128)(2,1)S(1)}, bf16[2,48,512]{2,1,0:T(8,128)(2,1)S(1)}, u32[]{:S(2)}, u32[]{:S(2)}) collective-permute-start(bf16[2,48,512]{2,1,0:T(8,128)(2,1)S(1)} %pad_maximum_fusion.16), channel_id=1, source_target_pairs={{0,6},{8,14},{16,22},{24,30},{1,7},{9,15},{17,23},{25,31},{2,4},{1... | collective-permute-start | bytes 294920 | tf_op jit(solution)/shard_map/ppermute | solution.py:37
  9.7 2.8 %collective-permute-start.1 = (bf16[2,96,512]{2,1,0:T(8,128)(2,1)S(1)}, bf16[2,96,512]{2,1,0:T(8,128)(2,1)S(1)}, u32[]{:S(2)}, u32[]{:S(2)}) collective-permute-start(bf16[2,96,512]{2,1,0:T(8,128)(2,1)S(1)} %pad_maximum_fusion.11), channel_id=1, source_target_pairs={{0,96},{8,104},{16,112},{24,120},{1,97},{9,105},{17,113},{25,121},... | collective-permute-start | bytes 589832 | tf_op jit(solution)/shard_map/ppermute | solution.py:37
  12.5 4.6 %collective-permute-done.1 = bf16[2,96,512]{2,1,0:T(8,128)(2,1)S(1)} collective-permute-done((bf16[2,96,512]{2,1,0:T(8,128)(2,1)S(1)}, bf16[2,96,512]{2,1,0:T(8,128)(2,1)S(1)}, u32[]{:S(2)}, u32[]{:S(2)}) %collective-permute-start.1) | collective-permute-done | bytes 196640 | tf_op jit(solution)/shard_map/ppermute | solution.py:37
  18.1 3.5 %collective-permute-start.6 = (bf16[4,48,512]{2,1,0:T(8,128)(2,1)S(1)}, bf16[4,48,512]{2,1,0:T(8,128)(2,1)S(1)}, u32[]{:S(2)}, u32[]{:S(2)}) collective-permute-start(bf16[4,48,512]{2,1,0:T(8,128)(2,1)S(1)} %pad_maximum_fusion.12), channel_id=1, source_target_pairs={{0,17},{8,25},{16,1},{24,9},{1,16},{9,24},{17,0},{25,8},{2,19},{10... | collective-permute-start | bytes 589832 | tf_op jit(solution)/shard_map/ppermute | solution.py:37
  21.6 3.2 %collective-permute-done.7 = bf16[4,48,512]{2,1,0:T(8,128)(2,1)S(1)} collective-permute-done((bf16[4,48,512]{2,1,0:T(8,128)(2,1)S(1)}, bf16[4,48,512]{2,1,0:T(8,128)(2,1)S(1)}, u32[]{:S(2)}, u32[]{:S(2)}) %collective-permute-start.7) | collective-permute-done | bytes 196640 | tf_op jit(solution)/shard_map/ppermute | solution.py:37
  27.9 2.2 %collective-permute-start.9 = (bf16[8,48,512]{2,1,0:T(8,128)(2,1)S(1)}, bf16[8,48,512]{2,1,0:T(8,128)(2,1)S(1)}, u32[]{:S(2)}, u32[]{:S(2)}) collective-permute-start(bf16[8,48,512]{2,1,0:T(8,128)(2,1)S(1)} %pad_maximum_fusion.9), channel_id=1, source_target_pairs={{0,6},{8,14},{16,22},{24,30},{1,7},{9,15},{17,23},{25,31},{2,4},{1... | collective-permute-start | bytes 1179656 | tf_op jit(solution)/shard_map/ppermute | solution.py:37
  30.1 1.9 collective-permute-start.11
  32.1 2.2 %collective-permute-start.10 = (bf16[8,48,512]{2,1,0:T(8,128)(2,1)S(1)}, bf16[8,48,512]{2,1,0:T(8,128)(2,1)S(1)}, u32[]{:S(2)}, u32[]{:S(2)}) collective-permute-start(bf16[8,48,512]{2,1,0:T(8,128)(2,1)S(1)} %pad_maximum_fusion.10), channel_id=1, source_target_pairs={{0,16},{8,24},{16,0},{24,8},{1,17},{9,25},{17,1},{25,9},{2,18},{10... | collective-permute-start | bytes 1179656 | tf_op jit(solution)/shard_map/ppermute | solution.py:37
  34.3 4.3 %collective-permute-done.11 = bf16[8,32,512]{2,1,0:T(8,128)(2,1)S(1)} collective-permute-done((bf16[8,32,512]{2,1,0:T(8,128)(2,1)S(1)}, bf16[8,32,512]{2,1,0:T(8,128)(2,1)S(1)}, u32[]{:S(2)}, u32[]{:S(2)}) %collective-permute-start.11) | collective-permute-done | bytes 262176 | tf_op jit(solution)/shard_map/ppermute | solution.py:37
  38.7 1.9 collective-permute-done.9
  40.6 2.7 %collective-permute-done.10 = bf16[8,48,512]{2,1,0:T(8,128)(2,1)S(1)} collective-permute-done((bf16[8,48,512]{2,1,0:T(8,128)(2,1)S(1)}, bf16[8,48,512]{2,1,0:T(8,128)(2,1)S(1)}, u32[]{:S(2)}, u32[]{:S(2)}) %collective-permute-start.10) | collective-permute-done | bytes 393248 | tf_op jit(solution)/shard_map/ppermute | solution.py:37
  43.5 2.6 %copy-done.7 = bf16[4,192,4096]{2,1,0:T(8,128)(2,1)} copy-done((bf16[4,192,4096]{2,1,0:T(8,128)(2,1)}, bf16[4,192,4096]{2,1,0:T(8,128)(2,1)S(1)}, u32[]{:S(2)}) %copy-start.7) | copy-done | bytes 6291480
  48.5 2.8 %collective-permute-start.18 = (bf16[16,48,512]{2,1,0:T(8,128)(2,1)S(1)}, bf16[16,48,512]{2,1,0:T(8,128)(2,1)S(1)}, u32[]{:S(2)}, u32[]{:S(2)}) collective-permute-start(bf16[16,48,512]{2,1,0:T(8,128)(2,1)S(1)} %pad_maximum_fusion.1), channel_id=1, source_target_pairs={{0,96},{8,104},{16,112},{24,120},{1,97},{9,105},{17,113},{25,121},... | collective-permute-start | bytes 2359304 | tf_op jit(solution)/shard_map/ppermute | solution.py:37
  51.3 7.9 %collective-permute-done.21 = bf16[16,32,512]{2,1,0:T(8,128)(2,1)S(1)} collective-permute-done((bf16[16,32,512]{2,1,0:T(8,128)(2,1)S(1)}, bf16[16,32,512]{2,1,0:T(8,128)(2,1)S(1)}, u32[]{:S(2)}, u32[]{:S(2)}) %collective-permute-start.21) | collective-permute-done | bytes 524320 | tf_op jit(solution)/shard_map/ppermute | solution.py:37
  60.2 5.0 %collective-permute-done.13 = bf16[16,48,512]{2,1,0:T(8,128)(2,1)S(1)} collective-permute-done((bf16[16,48,512]{2,1,0:T(8,128)(2,1)S(1)}, bf16[16,48,512]{2,1,0:T(8,128)(2,1)S(1)}, u32[]{:S(2)}, u32[]{:S(2)}) %collective-permute-start.13) | collective-permute-done | bytes 786464 | tf_op jit(solution)/shard_map/ppermute | solution.py:37
  69.4 5.8 %collective-permute-done.23 = bf16[16,32,512]{2,1,0:T(8,128)(2,1)S(1)} collective-permute-done((bf16[16,32,512]{2,1,0:T(8,128)(2,1)S(1)}, bf16[16,32,512]{2,1,0:T(8,128)(2,1)S(1)}, u32[]{:S(2)}, u32[]{:S(2)}) %collective-permute-start.23) | collective-permute-done | bytes 524320 | tf_op jit(solution)/shard_map/ppermute | solution.py:37
  75.2 2.8 %collective-permute-start.19 = (bf16[8,48,512]{2,1,0:T(8,128)(2,1)S(1)}, bf16[8,48,512]{2,1,0:T(8,128)(2,1)S(1)}, u32[]{:S(2)}, u32[]{:S(2)}) collective-permute-start(bf16[8,48,512]{2,1,0:T(8,128)(2,1)S(1)} %slice.159), channel_id=1, source_target_pairs={{0,96},{8,104},{16,112},{24,120},{1,97},{9,105},{17,113},{25,121},... | collective-permute-start | bytes 1179656 | tf_op jit(solution)/shard_map/ppermute | solution.py:37
  78.0 6.2 %collective-permute-done.19 = bf16[8,48,512]{2,1,0:T(8,128)(2,1)S(1)} collective-permute-done((bf16[8,48,512]{2,1,0:T(8,128)(2,1)S(1)}, bf16[8,48,512]{2,1,0:T(8,128)(2,1)S(1)}, u32[]{:S(2)}, u32[]{:S(2)}) %collective-permute-start.19) | collective-permute-done | bytes 393248 | tf_op jit(solution)/shard_map/ppermute | solution.py:37
  84.3 30.4 %experts.1 = (bf16[8,256,192]{2,1,0:T(8,128)(2,1)}, bf16[8,128,256]{2,1,0:T(8,128)(2,1)S(1)}, bf16[2,4,48,512]{3,2,1,0:T(8,128)(2,1)S(1)}, bf16[2,4,48,512]{3,2,...) custom-call(f32[8]{0:T(128)S(1)} %add_convert_fusion.5.ids_ref, ...), custom_call_target="tpu_custom_call" | custom-call | flops 20000000000 | bytes 50000000 | tf_op jit(solution)/shard_map/experts/pallas_call | solution.py:393
  115.5 2.8 %collective-permute-start.37 = (bf16[4,2,48,512]{3,2,1,0:T(8,128)(2,1)S(1)}, bf16[4,2,48,512]{3,2,1,0:T(8,128)(2,1)S(1)}, u32[]{:S(2)}, u32[]{:S(2)}) collective-permute-start(bf16[4,2,48,512]{3,2,1,0:T(8,128)(2,1)S(1)} %get-tuple-element.79), channel_id=1, source_target_pairs={{0,96},{8,104},{16,112},{24,120},{1,97},{9,105},{17,113},{25,121},... | collective-permute-start | bytes 1179656 | tf_op jit(solution)/shard_map/ppermute | solution.py:37
  119.3 10.6 %down.1 = (bf16[2,4,48,512]{3,2,1,0:T(8,128)(2,1)S(1)}, bf16[2,4,48,512]{3,2,1,0:T(8,128)(2,1)S(1)}, bf16[2,4,48,512]{3,2,1,0:T(8,128)(2,1)S(1)}, bf16[2,4,48,51...) custom-call(s32[8]{0:T(128)S(1)} %stack.35.cols_ref, ...), custom_call_target="tpu_custom_call" | custom-call | flops 6000000000 | bytes 12000000 | tf_op jit(solution)/shard_map/down/pallas_call | solution.py:418
  130.9 2.2 %collective-permute-start.26 = (bf16[2,4,48,512]{3,2,1,0:T(8,128)(2,1)S(1)}, bf16[2,4,48,512]{3,2,1,0:T(8,128)(2,1)S(1)}, u32[]{:S(2)}, u32[]{:S(2)}) collective-permute-start(bf16[2,4,48,512]{3,2,1,0:T(8,128)(2,1)S(1)} %get-tuple-element.71), channel_id=1, source_target_pairs={{0,16},{8,24},{16,0},{24,8},{1,17},{9,25},{17,1},{25,9},{2,18},{10... | collective-permute-start | bytes 1179656 | tf_op jit(solution)/shard_map/ppermute | solution.py:37
  134.4 5.6 %collective-permute-done.39 = bf16[4,2,48,512]{3,2,1,0:T(8,128)(2,1)S(1)} collective-permute-done((bf16[4,2,48,512]{3,2,1,0:T(8,128)(2,1)S(1)}, bf16[4,2,48,512]{3,2,1,0:T(8,128)(2,1)S(1)}, u32[]{:S(2)}, u32[]{:S(2)}) %collective-permute-start.39) | collective-permute-done | bytes 393248 | tf_op jit(solution)/shard_map/ppermute | solution.py:37
  142.3 2.2 %collective-permute-start.25 = (bf16[4,4,48,512]{3,2,1,0:T(8,128)(2,1)S(1)}, bf16[4,4,48,512]{3,2,1,0:T(8,128)(2,1)S(1)}, u32[]{:S(2)}, u32[]{:S(2)}) collective-permute-start(bf16[4,4,48,512]{3,2,1,0:T(8,128)(2,1)S(1)} %pad_maximum_fusion.2), channel_id=1, source_target_pairs={{0,16},{8,24},{16,0},{24,8},{1,17},{9,25},{17,1},{25,9},{2,18},{10... | collective-permute-start | bytes 2359304 | tf_op jit(solution)/shard_map/ppermute | solution.py:37
  144.7 5.9 %collective-permute-done.31 = bf16[4,4,32,512]{3,2,1,0:T(8,128)(2,1)S(1)} collective-permute-done((bf16[4,4,32,512]{3,2,1,0:T(8,128)(2,1)S(1)}, bf16[4,4,32,512]{3,2,1,0:T(8,128)(2,1)S(1)}, u32[]{:S(2)}, u32[]{:S(2)}) %collective-permute-start.31) | collective-permute-done | bytes 524320 | tf_op jit(solution)/shard_map/ppermute | solution.py:37
  151.0 3.7 %collective-permute-done.38 = bf16[8,2,48,512]{3,2,1,0:T(8,128)(2,1)S(1)} collective-permute-done((bf16[8,2,48,512]{3,2,1,0:T(8,128)(2,1)S(1)}, bf16[8,2,48,512]{3,2,1,0:T(8,128)(2,1)S(1)}, u32[]{:S(2)}, u32[]{:S(2)}) %collective-permute-start.38) | collective-permute-done | bytes 786464 | tf_op jit(solution)/shard_map/ppermute | solution.py:37
  157.3 7.8 %collective-permute-done.33 = bf16[2,4,32,512]{3,2,1,0:T(8,128)(2,1)S(1)} collective-permute-done((bf16[2,4,32,512]{3,2,1,0:T(8,128)(2,1)S(1)}, bf16[2,4,32,512]{3,2,1,0:T(8,128)(2,1)S(1)}, u32[]{:S(2)}, u32[]{:S(2)}) %collective-permute-start.33) | collective-permute-done | bytes 262176 | tf_op jit(solution)/shard_map/ppermute | solution.py:37
  167.6 2.7 %collective-permute-done.34 = bf16[4,32,512]{2,1,0:T(8,128)(2,1)S(1)} collective-permute-done((bf16[4,32,512]{2,1,0:T(8,128)(2,1)S(1)}, bf16[4,32,512]{2,1,0:T(8,128)(2,1)S(1)}, u32[]{:S(2)}, u32[]{:S(2)}) %collective-permute-start.34) | collective-permute-done | bytes 131104 | tf_op jit(solution)/shard_map/ppermute | solution.py:37
  170.7 6.6 %collective-permute-done.28 = bf16[2,4,48,512]{3,2,1,0:T(8,128)(2,1)S(1)} collective-permute-done((bf16[2,4,48,512]{3,2,1,0:T(8,128)(2,1)S(1)}, bf16[2,4,48,512]{3,2,1,0:T(8,128)(2,1)S(1)}, u32[]{:S(2)}, u32[]{:S(2)}) %collective-permute-start.28) | collective-permute-done | bytes 393248 | tf_op jit(solution)/shard_map/ppermute | solution.py:37
  178.1 5.2 %collective-permute-done.29 = bf16[4,48,512]{2,1,0:T(8,128)(2,1)S(1)} collective-permute-done((bf16[4,48,512]{2,1,0:T(8,128)(2,1)S(1)}, bf16[4,48,512]{2,1,0:T(8,128)(2,1)S(1)}, u32[]{:S(2)}, u32[]{:S(2)}) %collective-permute-start.29) | collective-permute-done | bytes 196640 | tf_op jit(solution)/shard_map/ppermute | solution.py:37
  184.6 5.5 %collective-permute-done.35 = bf16[2,80,512]{2,1,0:T(8,128)(2,1)S(1)} collective-permute-done((bf16[2,80,512]{2,1,0:T(8,128)(2,1)S(1)}, bf16[2,80,512]{2,1,0:T(8,128)(2,1)S(1)}, u32[]{:S(2)}, u32[]{:S(2)}) %collective-permute-start.35) | collective-permute-done | bytes 163872 | tf_op jit(solution)/shard_map/ppermute | solution.py:37
  190.3 4.3 %collective-permute-done.36 = bf16[1,80,512]{2,1,0:T(8,128)(2,1)S(1)} collective-permute-done((bf16[1,80,512]{2,1,0:T(8,128)(2,1)S(1)}, bf16[1,80,512]{2,1,0:T(8,128)(2,1)S(1)}, u32[]{:S(2)}, u32[]{:S(2)}) %collective-permute-start.36) | collective-permute-done | bytes 81952 | tf_op jit(solution)/shard_map/ppermute | solution.py:37
  (138 shorter events, 34.6 us)
Async XLA Ops:
  0.0 17.2 %collective-permute-start.4 = (bf16[4,192,4096]{2,1,0:T(8,128)(2,1)}, bf16[4,192,4096]{2,1,0:T(8,128)(2,1)}, u32[]{:S(2)}, u32[]{:S(2)}) collective-permute-start(bf16[4,192,4096]{2,1,0:T(8,128)(2,1)} %wg.1), channel_id=1, source_target_pairs={{0,8},{8,0},{16,24},{24,16},{1,9},{9,1},{17,25},{25,17},{2,10},{10... | collective-permute-start | bytes 18874376 | tf_op jit(solution)/shard_map/ppermute | solution.py:42
  17.2 10.6 %collective-permute-start.8 = (bf16[4,192,4096]{2,1,0:T(8,128)(2,1)}, bf16[4,192,4096]{2,1,0:T(8,128)(2,1)}, u32[]{:S(2)}, u32[]{:S(2)}) collective-permute-start(bf16[4,192,4096]{2,1,0:T(8,128)(2,1)} %wu), channel_id=1, source_target_pairs={{0,8},{8,0},{16,24},{24,16},{1,9},{9,1},{17,25},{25,17},{2,10},{10... | collective-permute-start | bytes 18874376 | tf_op jit(solution)/shard_map/ppermute | solution.py:42
  18.1 8.5 %collective-permute-start.6 = (bf16[4,48,512]{2,1,0:T(8,128)(2,1)S(1)}, bf16[4,48,512]{2,1,0:T(8,128)(2,1)S(1)}, u32[]{:S(2)}, u32[]{:S(2)}) collective-permute-start(bf16[4,48,512]{2,1,0:T(8,128)(2,1)S(1)} %pad_maximum_fusion.12), channel_id=1, source_target_pairs={{0,17},{8,25},{16,1},{24,9},{1,16},{9,24},{17,0},{25,8},{2,19},{10... | collective-permute-start | bytes 589832 | tf_op jit(solution)/shard_map/ppermute | solution.py:37
  27.8 15.6 %collective-permute-start.12 = (bf16[4,192,4096]{2,1,0:T(8,128)(2,1)}, bf16[4,192,4096]{2,1,0:T(8,128)(2,1)S(1)}, u32[]{:S(2)}, u32[]{:S(2)}) collective-permute-start(bf16[4,192,4096]{2,1,0:T(8,128)(2,1)} %wd.1), channel_id=1, source_target_pairs={{0,8},{8,0},{16,24},{24,16},{1,9},{9,1},{17,25},{25,17},{2,10},{10... | collective-permute-start | bytes 18874376 | tf_op jit(solution)/shard_map/ppermute | solution.py:42
  27.9 12.6 %collective-permute-start.9 = (bf16[8,48,512]{2,1,0:T(8,128)(2,1)S(1)}, bf16[8,48,512]{2,1,0:T(8,128)(2,1)S(1)}, u32[]{:S(2)}, u32[]{:S(2)}) collective-permute-start(bf16[8,48,512]{2,1,0:T(8,128)(2,1)S(1)} %pad_maximum_fusion.9), channel_id=1, source_target_pairs={{0,6},{8,14},{16,22},{24,30},{1,7},{9,15},{17,23},{25,31},{2,4},{1... | collective-permute-start | bytes 1179656 | tf_op jit(solution)/shard_map/ppermute | solution.py:37
  30.1 8.5 %collective-permute-start.11 = (bf16[8,32,512]{2,1,0:T(8,128)(2,1)S(1)}, bf16[8,32,512]{2,1,0:T(8,128)(2,1)S(1)}, u32[]{:S(2)}, u32[]{:S(2)}) collective-permute-start(bf16[8,32,512]{2,1,0:T(8,128)(2,1)S(1)} %fusion.3), channel_id=1, source_target_pairs={{0,17},{8,25},{16,1},{24,9},{1,16},{9,24},{17,0},{25,8},{2,19},{10... | collective-permute-start | bytes 786440 | tf_op jit(solution)/shard_map/ppermute | solution.py:37
  32.1 11.3 %collective-permute-start.10 = (bf16[8,48,512]{2,1,0:T(8,128)(2,1)S(1)}, bf16[8,48,512]{2,1,0:T(8,128)(2,1)S(1)}, u32[]{:S(2)}, u32[]{:S(2)}) collective-permute-start(bf16[8,48,512]{2,1,0:T(8,128)(2,1)S(1)} %pad_maximum_fusion.10), channel_id=1, source_target_pairs={{0,16},{8,24},{16,0},{24,8},{1,17},{9,25},{17,1},{25,9},{2,18},{10... | collective-permute-start | bytes 1179656 | tf_op jit(solution)/shard_map/ppermute | solution.py:37
  46.1 13.1 %collective-permute-start.21 = (bf16[16,32,512]{2,1,0:T(8,128)(2,1)S(1)}, bf16[16,32,512]{2,1,0:T(8,128)(2,1)S(1)}, u32[]{:S(2)}, u32[]{:S(2)}) collective-permute-start(bf16[16,32,512]{2,1,0:T(8,128)(2,1)S(1)} %pad_maximum_fusion.6), channel_id=1, source_target_pairs={{0,2},{8,10},{16,18},{24,26},{1,3},{9,11},{17,19},{25,27},{2,0},{1... | collective-permute-start | bytes 1572872 | tf_op jit(solution)/shard_map/ppermute | solution.py:37
  46.8 18.4 %collective-permute-start.13 = (bf16[16,48,512]{2,1,0:T(8,128)(2,1)S(1)}, bf16[16,48,512]{2,1,0:T(8,128)(2,1)S(1)}, u32[]{:S(2)}, u32[]{:S(2)}) collective-permute-start(bf16[16,48,512]{2,1,0:T(8,128)(2,1)S(1)} %pad_maximum_fusion), channel_id=1, source_target_pairs={{0,16},{8,24},{16,0},{24,8},{1,17},{9,25},{17,1},{25,9},{2,18},{10... | collective-permute-start | bytes 2359304 | tf_op jit(solution)/shard_map/ppermute | solution.py:37
  48.5 17.9 %collective-permute-start.14 = (bf16[16,48,512]{2,1,0:T(8,128)(2,1)S(1)}, bf16[16,48,512]{2,1,0:T(8,128)(2,1)S(1)}, u32[]{:S(2)}, u32[]{:S(2)}) collective-permute-start(bf16[16,48,512]{2,1,0:T(8,128)(2,1)S(1)} %pad_maximum_fusion), channel_id=1, source_target_pairs={{0,17},{8,25},{16,1},{24,9},{1,16},{9,24},{17,0},{25,8},{2,19},{10... | collective-permute-start | bytes 2359304 | tf_op jit(solution)/shard_map/ppermute | solution.py:37
  48.5 19.8 %collective-permute-start.18 = (bf16[16,48,512]{2,1,0:T(8,128)(2,1)S(1)}, bf16[16,48,512]{2,1,0:T(8,128)(2,1)S(1)}, u32[]{:S(2)}, u32[]{:S(2)}) collective-permute-start(bf16[16,48,512]{2,1,0:T(8,128)(2,1)S(1)} %pad_maximum_fusion.1), channel_id=1, source_target_pairs={{0,96},{8,104},{16,112},{24,120},{1,97},{9,105},{17,113},{25,121},... | collective-permute-start | bytes 2359304 | tf_op jit(solution)/shard_map/ppermute | solution.py:37
  51.3 18.0 %collective-permute-start.17 = (bf16[16,48,512]{2,1,0:T(8,128)(2,1)S(1)}, bf16[16,48,512]{2,1,0:T(8,128)(2,1)S(1)}, u32[]{:S(2)}, u32[]{:S(2)}) collective-permute-start(bf16[16,48,512]{2,1,0:T(8,128)(2,1)S(1)} %pad_maximum_fusion.1), channel_id=1, source_target_pairs={{0,32},{8,40},{16,48},{24,56},{1,33},{9,41},{17,49},{25,57},{2,34}... | collective-permute-start | bytes 2359304 | tf_op jit(solution)/shard_map/ppermute | solution.py:37
  59.1 16.1 %collective-permute-start.23 = (bf16[16,32,512]{2,1,0:T(8,128)(2,1)S(1)}, bf16[16,32,512]{2,1,0:T(8,128)(2,1)S(1)}, u32[]{:S(2)}, u32[]{:S(2)}) collective-permute-start(bf16[16,32,512]{2,1,0:T(8,128)(2,1)S(1)} %collective-permute-done.21), channel_id=1, source_target_pairs={{0,6},{8,14},{16,22},{24,30},{1,7},{9,15},{17,23},{25,31},{2,4},{1... | collective-permute-start | bytes 1572872 | tf_op jit(solution)/shard_map/ppermute | solution.py:37
  65.2 19.0 %collective-permute-start.22 = (bf16[16,32,512]{2,1,0:T(8,128)(2,1)S(1)}, bf16[16,32,512]{2,1,0:T(8,128)(2,1)S(1)}, u32[]{:S(2)}, u32[]{:S(2)}) collective-permute-start(bf16[16,32,512]{2,1,0:T(8,128)(2,1)S(1)} %pad_maximum_fusion.6), channel_id=1, source_target_pairs={{0,6},{8,14},{16,22},{24,30},{1,7},{9,15},{17,23},{25,31},{2,4},{1... | collective-permute-start | bytes 1572872 | tf_op jit(solution)/shard_map/ppermute | solution.py:37
  66.4 11.6 %collective-permute-start.16 = (bf16[8,48,512]{2,1,0:T(8,128)(2,1)S(1)}, bf16[8,48,512]{2,1,0:T(8,128)(2,1)S(1)}, u32[]{:S(2)}, u32[]{:S(2)}) collective-permute-start(bf16[8,48,512]{2,1,0:T(8,128)(2,1)S(1)} %slice.158), channel_id=1, source_target_pairs={{0,16},{8,24},{16,0},{24,8},{1,17},{9,25},{17,1},{25,9},{2,18},{10... | collective-permute-start | bytes 1179656 | tf_op jit(solution)/shard_map/ppermute | solution.py:37
  68.3 9.7 %collective-permute-start.15 = (bf16[8,48,512]{2,1,0:T(8,128)(2,1)S(1)}, bf16[8,48,512]{2,1,0:T(8,128)(2,1)S(1)}, u32[]{:S(2)}, u32[]{:S(2)}) collective-permute-start(bf16[8,48,512]{2,1,0:T(8,128)(2,1)S(1)} %slice.124), channel_id=1, source_target_pairs={{0,17},{8,25},{16,1},{24,9},{1,16},{9,24},{17,0},{25,8},{2,19},{10... | collective-permute-start | bytes 1179656 | tf_op jit(solution)/shard_map/ppermute | solution.py:37
  69.3 8.7 %collective-permute-start.20 = (bf16[8,48,512]{2,1,0:T(8,128)(2,1)S(1)}, bf16[8,48,512]{2,1,0:T(8,128)(2,1)S(1)}, u32[]{:S(2)}, u32[]{:S(2)}) collective-permute-start(bf16[8,48,512]{2,1,0:T(8,128)(2,1)S(1)} %slice.160), channel_id=1, source_target_pairs={{0,32},{8,40},{16,48},{24,56},{1,33},{9,41},{17,49},{25,57},{2,34}... | collective-permute-start | bytes 1179656 | tf_op jit(solution)/shard_map/ppermute | solution.py:37
  75.2 9.0 %collective-permute-start.19 = (bf16[8,48,512]{2,1,0:T(8,128)(2,1)S(1)}, bf16[8,48,512]{2,1,0:T(8,128)(2,1)S(1)}, u32[]{:S(2)}, u32[]{:S(2)}) collective-permute-start(bf16[8,48,512]{2,1,0:T(8,128)(2,1)S(1)} %slice.159), channel_id=1, source_target_pairs={{0,96},{8,104},{16,112},{24,120},{1,97},{9,105},{17,113},{25,121},... | collective-permute-start | bytes 1179656 | tf_op jit(solution)/shard_map/ppermute | solution.py:37
  115.5 17.6 %collective-permute-start.37 = (bf16[4,2,48,512]{3,2,1,0:T(8,128)(2,1)S(1)}, bf16[4,2,48,512]{3,2,1,0:T(8,128)(2,1)S(1)}, u32[]{:S(2)}, u32[]{:S(2)}) collective-permute-start(bf16[4,2,48,512]{3,2,1,0:T(8,128)(2,1)S(1)} %get-tuple-element.79), channel_id=1, source_target_pairs={{0,96},{8,104},{16,112},{24,120},{1,97},{9,105},{17,113},{25,121},... | collective-permute-start | bytes 1179656 | tf_op jit(solution)/shard_map/ppermute | solution.py:37
  118.3 21.8 %collective-permute-start.30 = (bf16[4,4,32,512]{3,2,1,0:T(8,128)(2,1)S(1)}, bf16[4,4,32,512]{3,2,1,0:T(8,128)(2,1)S(1)}, u32[]{:S(2)}, u32[]{:S(2)}) collective-permute-start(bf16[4,4,32,512]{3,2,1,0:T(8,128)(2,1)S(1)} %get-tuple-element.75), channel_id=1, source_target_pairs={{0,6},{8,14},{16,22},{24,30},{1,7},{9,15},{17,23},{25,31},{2,4},{1... | collective-permute-start | bytes 1572872 | tf_op jit(solution)/shard_map/ppermute | solution.py:37
  130.0 10.0 %collective-permute-start.39 = (bf16[4,2,48,512]{3,2,1,0:T(8,128)(2,1)S(1)}, bf16[4,2,48,512]{3,2,1,0:T(8,128)(2,1)S(1)}, u32[]{:S(2)}, u32[]{:S(2)}) collective-permute-start(bf16[4,2,48,512]{3,2,1,0:T(8,128)(2,1)S(1)} %get-tuple-element.83), channel_id=1, source_target_pairs={{0,32},{8,40},{16,48},{24,56},{1,33},{9,41},{17,49},{25,57},{2,34}... | collective-permute-start | bytes 1179656 | tf_op jit(solution)/shard_map/ppermute | solution.py:37
  130.1 11.4 %collective-permute-start.24 = (bf16[2,4,48,512]{3,2,1,0:T(8,128)(2,1)S(1)}, bf16[2,4,48,512]{3,2,1,0:T(8,128)(2,1)S(1)}, u32[]{:S(2)}, u32[]{:S(2)}) collective-permute-start(bf16[2,4,48,512]{3,2,1,0:T(8,128)(2,1)S(1)} %get-tuple-element.67), channel_id=1, source_target_pairs={{0,17},{8,25},{16,1},{24,9},{1,16},{9,24},{17,0},{25,8},{2,19},{10... | collective-permute-start | bytes 1179656 | tf_op jit(solution)/shard_map/ppermute | solution.py:37
  130.9 11.4 %collective-permute-start.26 = (bf16[2,4,48,512]{3,2,1,0:T(8,128)(2,1)S(1)}, bf16[2,4,48,512]{3,2,1,0:T(8,128)(2,1)S(1)}, u32[]{:S(2)}, u32[]{:S(2)}) collective-permute-start(bf16[2,4,48,512]{3,2,1,0:T(8,128)(2,1)S(1)} %get-tuple-element.71), channel_id=1, source_target_pairs={{0,16},{8,24},{16,0},{24,8},{1,17},{9,25},{17,1},{25,9},{2,18},{10... | collective-permute-start | bytes 1179656 | tf_op jit(solution)/shard_map/ppermute | solution.py:37
  133.1 11.5 %collective-permute-start.32 = (bf16[4,4,32,512]{3,2,1,0:T(8,128)(2,1)S(1)}, bf16[4,4,32,512]{3,2,1,0:T(8,128)(2,1)S(1)}, u32[]{:S(2)}, u32[]{:S(2)}) collective-permute-start(bf16[4,4,32,512]{3,2,1,0:T(8,128)(2,1)S(1)} %get-tuple-element.76), channel_id=1, source_target_pairs={{0,6},{8,14},{16,22},{24,30},{1,7},{9,15},{17,23},{25,31},{2,4},{1... | collective-permute-start | bytes 1572872 | tf_op jit(solution)/shard_map/ppermute | solution.py:37
  140.0 14.7 %collective-permute-start.38 = (bf16[8,2,48,512]{3,2,1,0:T(8,128)(2,1)S(1)}, bf16[8,2,48,512]{3,2,1,0:T(8,128)(2,1)S(1)}, u32[]{:S(2)}, u32[]{:S(2)}) collective-permute-start(bf16[8,2,48,512]{3,2,1,0:T(8,128)(2,1)S(1)} %pad_maximum_fusion.4), channel_id=1, source_target_pairs={{0,32},{8,40},{16,48},{24,56},{1,33},{9,41},{17,49},{25,57},{2,34}... | collective-permute-start | bytes 2359304 | tf_op jit(solution)/shard_map/ppermute | solution.py:37
  141.3 9.3 %collective-permute-start.31 = (bf16[4,4,32,512]{3,2,1,0:T(8,128)(2,1)S(1)}, bf16[4,4,32,512]{3,2,1,0:T(8,128)(2,1)S(1)}, u32[]{:S(2)}, u32[]{:S(2)}) collective-permute-start(bf16[4,4,32,512]{3,2,1,0:T(8,128)(2,1)S(1)} %add.139), channel_id=1, source_target_pairs={{0,2},{8,10},{16,18},{24,26},{1,3},{9,11},{17,19},{25,27},{2,0},{1... | collective-permute-start | bytes 1572872 | tf_op jit(solution)/shard_map/ppermute | solution.py:37
  141.5 13.9 %collective-permute-start.40 = (bf16[8,2,48,512]{3,2,1,0:T(8,128)(2,1)S(1)}, bf16[8,2,48,512]{3,2,1,0:T(8,128)(2,1)S(1)}, u32[]{:S(2)}, u32[]{:S(2)}) collective-permute-start(bf16[8,2,48,512]{3,2,1,0:T(8,128)(2,1)S(1)} %pad_maximum_fusion.5), channel_id=1, source_target_pairs={{0,96},{8,104},{16,112},{24,120},{1,97},{9,105},{17,113},{25,121},... | collective-permute-start | bytes 2359304 | tf_op jit(solution)/shard_map/ppermute | solution.py:37
  142.3 24.8 %collective-permute-start.25 = (bf16[4,4,48,512]{3,2,1,0:T(8,128)(2,1)S(1)}, bf16[4,4,48,512]{3,2,1,0:T(8,128)(2,1)S(1)}, u32[]{:S(2)}, u32[]{:S(2)}) collective-permute-start(bf16[4,4,48,512]{3,2,1,0:T(8,128)(2,1)S(1)} %pad_maximum_fusion.2), channel_id=1, source_target_pairs={{0,16},{8,24},{16,0},{24,8},{1,17},{9,25},{17,1},{25,9},{2,18},{10... | collective-permute-start | bytes 2359304 | tf_op jit(solution)/shard_map/ppermute | solution.py:37
  144.6 22.5 %collective-permute-start.27 = (bf16[4,4,48,512]{3,2,1,0:T(8,128)(2,1)S(1)}, bf16[4,4,48,512]{3,2,1,0:T(8,128)(2,1)S(1)}, u32[]{:S(2)}, u32[]{:S(2)}) collective-permute-start(bf16[4,4,48,512]{3,2,1,0:T(8,128)(2,1)S(1)} %pad_maximum_fusion.3), channel_id=1, source_target_pairs={{0,17},{8,25},{16,1},{24,9},{1,16},{9,24},{17,0},{25,8},{2,19},{10... | collective-permute-start | bytes 2359304 | tf_op jit(solution)/shard_map/ppermute | solution.py:37
  150.8 14.3 %collective-permute-start.33 = (bf16[2,4,32,512]{3,2,1,0:T(8,128)(2,1)S(1)}, bf16[2,4,32,512]{3,2,1,0:T(8,128)(2,1)S(1)}, u32[]{:S(2)}, u32[]{:S(2)}) collective-permute-start(bf16[2,4,32,512]{3,2,1,0:T(8,128)(2,1)S(1)} %slice.168), channel_id=1, source_target_pairs={{0,17},{8,25},{16,1},{24,9},{1,16},{9,24},{17,0},{25,8},{2,19},{10... | collective-permute-start | bytes 786440 | tf_op jit(solution)/shard_map/ppermute | solution.py:37
  155.8 14.5 %collective-permute-start.41 = (bf16[2,4,48,512]{3,2,1,0:T(8,128)(2,1)S(1)}, bf16[2,4,48,512]{3,2,1,0:T(8,128)(2,1)S(1)}, u32[]{:S(2)}, u32[]{:S(2)}) collective-permute-start(bf16[2,4,48,512]{3,2,1,0:T(8,128)(2,1)S(1)} %pad_maximum_fusion.7), channel_id=1, source_target_pairs={{0,16},{8,24},{16,0},{24,8},{1,17},{9,25},{17,1},{25,9},{2,18},{10... | collective-permute-start | bytes 1179656 | tf_op jit(solution)/shard_map/ppermute | solution.py:37
  167.2 10.1 %collective-permute-start.28 = (bf16[2,4,48,512]{3,2,1,0:T(8,128)(2,1)S(1)}, bf16[2,4,48,512]{3,2,1,0:T(8,128)(2,1)S(1)}, u32[]{:S(2)}, u32[]{:S(2)}) collective-permute-start(bf16[2,4,48,512]{3,2,1,0:T(8,128)(2,1)S(1)} %add_convert_fusion.3), channel_id=1, source_target_pairs={{0,6},{8,14},{16,22},{24,30},{1,7},{9,15},{17,23},{25,31},{2,4},{1... | collective-permute-start | bytes 1179656 | tf_op jit(solution)/shard_map/ppermute | solution.py:37
  (22 other events, 245.2 us)

commit v4 on v3

--- a/solution.py
+++ b/solution.py
@@ -14,7 +14,7 @@
 MIDDLE = (1, 2, 2)
 MASKS = ((1, 3), (3, 1), (1, 3))
 ROWS = (48, 48, 32)
-VMEM_EXPERTS = 46 * 2**20
+VMEM_EXPERTS = 36 * 2**20
 FIRST = (0, 48, 96)
 BF16 = jnp.bfloat16
 F32 = jnp.float32
@@ -180,15 +180,8 @@
 
 def expert_kernel(kys, ids_ref, cols_ref, mine_ref, wg, wu, wg2, wu2, wd, wd2, *rest):
     token_refs, rest = rest[:14], rest[14:]
-    (h_ref, put), outs = rest[:2], rest[2:-7]
-    tokens, sorted_rows, wbuf, gate_col, pick, t_sem, w_sem = rest[-7:]
-    d_sem = t_sem.at[0]
-
-    def fetch(e, j, gate, up):
-        return [
-            pltpu.make_async_copy(gate.at[e], wbuf.at[j, pl.ds(0, 192)], w_sem.at[j, 0]),
-            pltpu.make_async_copy(up.at[e], wbuf.at[j, pl.ds(192, 192)], w_sem.at[j, 1]),
-        ]
+    (h_ref, put), outs = rest[:2], rest[2:-8]
+    tokens, sorted_rows, wbuf, act, gate_col, pick, t_sem, w_sem = rest[-8:]
 
     def load(ky):
         def column(ky, high):
@@ -201,32 +194,44 @@
         ]
         return [pltpu.make_async_copy(a, b, t_sem.at[ky, m]) for m, (a, b) in enumerate(pairs)]
 
-    def down_tile(slot, e):
-        return wbuf.at[slot, pl.ds(e // 4 * 192, 192), pl.ds(e % 4 * 1024, 1024)]
+    def fetch(ky):
+        col, slot = columns_of(cols_ref, ky), ky % 2
+        places = [(w, first, row) for first, pair in ((0, (wg, wu)), (4, (wg2, wu2)))
+                  for row, w in zip((0, 192), pair)]
+        return [
+            pltpu.make_async_copy(
+                w.at[:, :, col], wbuf.at[slot, pl.ds(first, 4), pl.ds(row, 192)], w_sem.at[slot, m]
+            )
+            for m, (w, first, row) in enumerate(places)
+        ]
 
     def fetch_down(n):
         col = columns_of(cols_ref, kys[n])
         return [
             pltpu.make_async_copy(
-                (wd if e < 4 else wd2).at[e % 4, :, col], down_tile(n, e), d_sem.at[n * 8 + e]
+                w.at[:, :, col],
+                wbuf.at[0, pl.ds(first, 4), pl.ds(n * 192, 192)],
+                w_sem.at[0, n * 2 + m],
             )
-            for e in range(8)
+            for m, (w, first) in enumerate(((wd, 0), (wd2, 4)))
         ]
 
-    loads = [load(ky) for ky in range(4)]
-    for ky in range(4):
-        for copy in loads[ky]:
+    def start(copies):
+        for copy in copies:
             copy.start()
-    for j in range(2):
-        for copy in fetch(j, j, wg, wu):
-            copy.start()
+
+    def finish(copies):
+        for copy in copies:
+            copy.wait()
+
+    for ky in range(2):
+        start(load(ky))
+        start(fetch(ky))
     route(ids_ref, mine_ref, gate_col, pick, put)
     for ky in range(4):
-        for copy in loads[ky]:
-            copy.wait()
+        finish(load(ky))
         if ky < 2:
-            for copy in fetch(ky + 2, ky + 2, wg, wu):
-                copy.start()
+            start(load(ky + 2))
         col = columns_of(cols_ref, ky)
 
         def dispatch(b, carry):
@@ -234,71 +239,60 @@
                 pick[b], tokens[b // 2, lax.rem(b, 2), :, col], preferred_element_type=F32
             )
             rows = rows.astype(BF16).reshape(4, 2, 32, 1024)
-            sorted_rows[:, :, pl.ds(pl.multiple_of(b * 32, 32), 32), col] = rows
-            return carry
-
-        lax.fori_loop(0, 8, dispatch, 0, unroll=2)
-
-    def experts(turn, carry):
-        for j in range(4):
-            e = turn * 4 + j
-            for copy in fetch(j, j, wg, wu):
-                copy.wait()
-            act = lax.dot_general(
-                sorted_rows[turn * 2 + j // 2, j % 2],
-                wbuf[j],
+            sorted_rows[:, :, pl.ds(pl.multiple_of(b * 32, 32), 32)] = rows
+            return carry
+
+        lax.fori_loop(0, 8, dispatch, 0, unroll=4)
+        finish(fetch(ky))
+
+        def project(e, carry):
+            part = lax.dot_general(
+                sorted_rows[e // 2, lax.rem(e, 2)],
+                wbuf[ky % 2, e],
                 (((1,), (1,)), ((), ())),
                 preferred_element_type=F32,
             )
-            gate, up = act[:, :192], act[:, 192:]
-            hidden = gate / (1.0 + jnp.exp(-gate)) * up * gate_col[e]
-            h_ref[e] = hidden.astype(BF16)
-
-            @pl.when(turn == 0)
-            def _():
-                for copy in fetch(j, j, wg2, wu2):
-                    copy.start()
-
-            if j < 2:
-
-                @pl.when(turn == 1)
-                def _():
-                    for copy in fetch_down(j):
-                        copy.start()
-
-        return carry
-
-    lax.fori_loop(0, 2, experts, 0)
+            if ky > 0:
+                part = act[e] + part
+            if ky < 3:
+                act[e] = part
+            else:
+                gate, up = part[:, :192], part[:, 192:]
+                h_ref[e] = (gate / (1.0 + jnp.exp(-gate)) * up * gate_col[e]).astype(BF16)
+            return carry
+
+        lax.fori_loop(0, 8, project, 0, unroll=4)
+        if ky < 2:
+            start(fetch(ky + 2))
+        if ky == 2:
+            start(fetch_down(0) + fetch_down(1))
+    stores = []
     for n in range(2):
-        for copy in fetch_down(n):
-            copy.wait()
-        for e in range(8):
-            out = jnp.dot(h_ref[e], down_tile(n, e)[...], preferred_element_type=F32)
-            sorted_rows[:, :, pl.ds(e * 32, 32), pl.ds(0, 1024)] = out.astype(BF16).reshape(
-                4, 2, 32, 1024
-            )
-        col = pl.ds(1024 * (n + 1), 1024)
+        finish(fetch_down(n))
+
+        def project_out(e, carry):
+            down = wbuf[0, e, pl.ds(n * 192, 192)]
+            out = jnp.dot(h_ref[e], down, preferred_element_type=F32)
+            rows = pl.ds(pl.multiple_of(e * 32, 32), 32)
+            sorted_rows[:, :, rows] = out.astype(BF16).reshape(4, 2, 32, 1024)
+            return carry
+
+        lax.fori_loop(0, 8, project_out, 0, unroll=4)
+        col = pl.ds(1024 * n, 1024)
 
         def combine(b, carry):
             at = b // 2, lax.rem(b, 2)
-            out = jnp.dot(
-                put[b], sorted_rows[at[0], at[1], :, pl.ds(0, 1024)], preferred_element_type=F32
-            )
-            sorted_rows[at[0], at[1], pl.ds(0, 128), col] = out.astype(BF16)
-            return carry
-
-        lax.fori_loop(0, 8, combine, 0, unroll=2)
-        tile = sorted_rows.at[:, :, pl.ds(0, 128), col]
-        stores = [
-            pltpu.make_async_copy(b, a, t_sem.at[2 + n, m])
-            for m, (a, b) in enumerate(y_pairs(outs, kys, n, cols_ref, tile))
-        ]
-        for copy in stores:
-            copy.start()
-        if n == 0:
-            first_stores = stores
-    for copy in first_stores + stores:
-        copy.wait()
+            out = jnp.dot(put[b], sorted_rows[at[0], at[1]], preferred_element_type=F32)
+            tokens[at[0], at[1], :, col] = out.astype(BF16)
+            return carry
+
+        lax.fori_loop(0, 8, combine, 0, unroll=4)
+        pairs = y_pairs(outs, kys, n, cols_ref, tokens.at[:, :, :, col])
+        stores.append(
+            [pltpu.make_async_copy(b, a, t_sem.at[n, m]) for m, (a, b) in enumerate(pairs)]
+        )
+        start(stores[n])
+    finish(stores[0] + stores[1])
 
 
 def down_kernel(kys, cols_ref, h_ref, put_ref, wd, wd2, *rest):
@@ -334,14 +328,14 @@
             expert_rows[:, rows] = out.astype(BF16).reshape(8, 32, 1024)
             return carry
 
-        lax.fori_loop(0, 8, project, 0, unroll=2)
+        lax.fori_loop(0, 8, project, 0, unroll=4)
 
         def combine(b, carry):
             out = jnp.dot(put[b], expert_rows[b], preferred_element_type=F32)
             ybuf[n, b // 2, lax.rem(b, 2)] = out.astype(BF16)
             return carry
 
-        lax.fori_loop(0, 8, combine, 0, unroll=2)
+        lax.fori_loop(0, 8, combine, 0, unroll=4)
         for copy in stores(n):
             copy.start()
     for n in range(2):
@@ -401,12 +395,13 @@
         out_specs=[vmem, vmem] + [hbm] * 10,
         scratch_shapes=[
             pltpu.VMEM((4, 2, 128, 4096), BF16),
-            pltpu.VMEM((4, 2, 256, 4096), BF16),
-            pltpu.VMEM((4, 384, 4096), BF16),
+            pltpu.VMEM((4, 2, 256, 1024), BF16),
+            pltpu.VMEM((2, 8, 384, 1024), BF16),
+            pltpu.VMEM((8, 256, 384), F32),
             pltpu.VMEM((8, 256, 1), F32),
             pltpu.VMEM((8, 256, 128), BF16),
             pltpu.SemaphoreType.DMA((4, 24)),
-            pltpu.SemaphoreType.DMA((4, 2)),
+            pltpu.SemaphoreType.DMA((2, 4)),
         ],
         compiler_params=pltpu.CompilerParams(vmem_limit_bytes=VMEM_EXPERTS),
         cost_estimate=pl.CostEstimate(

time: 196 us -> 189 us (0.964)
  Pallas kernels: 41.1 us -> 36.1 us
    pallas_call x1, Pallas kernels: 30.4 us -> 26.8 us  [local(): pl.pallas_call(functools.partial(expert_kernel, (2, 3)), out_shape=[jax.S...]
where the time goes in v4:
time: 189 us
  waiting for transfers between devices  94 us (50%)
  starting transfers between devices  48.7 us (26%)
  Pallas kernels  36.1 us (19%)
  other arithmetic  5.73 us (3%)
  local copies, waits for them, and re-layouts  3.71 us (2%)
    ppermute x42, waiting for transfers between devices, swap(): return lax.ppermute(value, AXES, pairs)  92.8 us
    ppermute x42, starting transfers between devices, swap(): return lax.ppermute(value, AXES, pairs)  48.5 us
    pallas_call x1, Pallas kernels, local(): pl.pallas_call(functools.partial(expert_kernel, (2, 3)), out_shape=[jax.S...  26.8 us
    pallas_call x1, Pallas kernels, local(): pl.pallas_call(functools.partial(down_kernel, (0, 1)), out_shape=shapes,...  9.31 us
  transfers between devices with their start and end apart: 45, of which 23 were waited for; matrix products, arithmetic and copies ran while one was open for 4% of the time, Pallas kernels for 5%

profile of v4, /device:TPU:32, one launch (start us, length us, event | category | flops | bytes accessed | tf_op | source)
XLA Modules:
  0.0 188.7 jit_solution(950390498843559237)
XLA Ops:
  6.2 2.3 %collective-permute-start.3 = (bf16[2,48,512]{2,1,0:T(8,128)(2,1)S(1)}, bf16[2,48,512]{2,1,0:T(8,128)(2,1)S(1)}, u32[]{:S(2)}, u32[]{:S(2)}) collective-permute-start(bf16[2,48,512]{2,1,0:T(8,128)(2,1)S(1)} %pad_maximum_fusion.16), channel_id=1, source_target_pairs={{0,6},{8,14},{16,22},{24,30},{1,7},{9,15},{17,23},{25,31},{2,4},{1... | collective-permute-start | bytes 294920 | tf_op jit(solution)/shard_map/ppermute | solution.py:37
  9.7 2.8 %collective-permute-start.1 = (bf16[2,96,512]{2,1,0:T(8,128)(2,1)S(1)}, bf16[2,96,512]{2,1,0:T(8,128)(2,1)S(1)}, u32[]{:S(2)}, u32[]{:S(2)}) collective-permute-start(bf16[2,96,512]{2,1,0:T(8,128)(2,1)S(1)} %pad_maximum_fusion.11), channel_id=1, source_target_pairs={{0,96},{8,104},{16,112},{24,120},{1,97},{9,105},{17,113},{25,121},... | collective-permute-start | bytes 589832 | tf_op jit(solution)/shard_map/ppermute | solution.py:37
  12.5 4.6 %collective-permute-done.1 = bf16[2,96,512]{2,1,0:T(8,128)(2,1)S(1)} collective-permute-done((bf16[2,96,512]{2,1,0:T(8,128)(2,1)S(1)}, bf16[2,96,512]{2,1,0:T(8,128)(2,1)S(1)}, u32[]{:S(2)}, u32[]{:S(2)}) %collective-permute-start.1) | collective-permute-done | bytes 196640 | tf_op jit(solution)/shard_map/ppermute | solution.py:37
  18.1 3.5 %collective-permute-start.6 = (bf16[4,48,512]{2,1,0:T(8,128)(2,1)S(1)}, bf16[4,48,512]{2,1,0:T(8,128)(2,1)S(1)}, u32[]{:S(2)}, u32[]{:S(2)}) collective-permute-start(bf16[4,48,512]{2,1,0:T(8,128)(2,1)S(1)} %pad_maximum_fusion.12), channel_id=1, source_target_pairs={{0,17},{8,25},{16,1},{24,9},{1,16},{9,24},{17,0},{25,8},{2,19},{10... | collective-permute-start | bytes 589832 | tf_op jit(solution)/shard_map/ppermute | solution.py:37
  21.6 3.2 %collective-permute-done.7 = bf16[4,48,512]{2,1,0:T(8,128)(2,1)S(1)} collective-permute-done((bf16[4,48,512]{2,1,0:T(8,128)(2,1)S(1)}, bf16[4,48,512]{2,1,0:T(8,128)(2,1)S(1)}, u32[]{:S(2)}, u32[]{:S(2)}) %collective-permute-start.7) | collective-permute-done | bytes 196640 | tf_op jit(solution)/shard_map/ppermute | solution.py:37
  27.9 2.2 %collective-permute-start.9 = (bf16[8,48,512]{2,1,0:T(8,128)(2,1)S(1)}, bf16[8,48,512]{2,1,0:T(8,128)(2,1)S(1)}, u32[]{:S(2)}, u32[]{:S(2)}) collective-permute-start(bf16[8,48,512]{2,1,0:T(8,128)(2,1)S(1)} %pad_maximum_fusion.9), channel_id=1, source_target_pairs={{0,6},{8,14},{16,22},{24,30},{1,7},{9,15},{17,23},{25,31},{2,4},{1... | collective-permute-start | bytes 1179656 | tf_op jit(solution)/shard_map/ppermute | solution.py:37
  30.1 1.9 %collective-permute-start.11 = (bf16[8,32,512]{2,1,0:T(8,128)(2,1)S(1)}, bf16[8,32,512]{2,1,0:T(8,128)(2,1)S(1)}, u32[]{:S(2)}, u32[]{:S(2)}) collective-permute-start(bf16[8,32,512]{2,1,0:T(8,128)(2,1)S(1)} %fusion.3), channel_id=1, source_target_pairs={{0,17},{8,25},{16,1},{24,9},{1,16},{9,24},{17,0},{25,8},{2,19},{10... | collective-permute-start | bytes 786440 | tf_op jit(solution)/shard_map/ppermute | solution.py:37
  32.1 2.2 %collective-permute-start.10 = (bf16[8,48,512]{2,1,0:T(8,128)(2,1)S(1)}, bf16[8,48,512]{2,1,0:T(8,128)(2,1)S(1)}, u32[]{:S(2)}, u32[]{:S(2)}) collective-permute-start(bf16[8,48,512]{2,1,0:T(8,128)(2,1)S(1)} %pad_maximum_fusion.10), channel_id=1, source_target_pairs={{0,16},{8,24},{16,0},{24,8},{1,17},{9,25},{17,1},{25,9},{2,18},{10... | collective-permute-start | bytes 1179656 | tf_op jit(solution)/shard_map/ppermute | solution.py:37
  34.3 4.3 %collective-permute-done.11 = bf16[8,32,512]{2,1,0:T(8,128)(2,1)S(1)} collective-permute-done((bf16[8,32,512]{2,1,0:T(8,128)(2,1)S(1)}, bf16[8,32,512]{2,1,0:T(8,128)(2,1)S(1)}, u32[]{:S(2)}, u32[]{:S(2)}) %collective-permute-start.11) | collective-permute-done | bytes 262176 | tf_op jit(solution)/shard_map/ppermute | solution.py:37
  38.7 1.9 %collective-permute-done.9 = bf16[8,48,512]{2,1,0:T(8,128)(2,1)S(1)} collective-permute-done((bf16[8,48,512]{2,1,0:T(8,128)(2,1)S(1)}, bf16[8,48,512]{2,1,0:T(8,128)(2,1)S(1)}, u32[]{:S(2)}, u32[]{:S(2)}) %collective-permute-start.9) | collective-permute-done | bytes 393248 | tf_op jit(solution)/shard_map/ppermute | solution.py:37
  40.6 2.7 %collective-permute-done.10 = bf16[8,48,512]{2,1,0:T(8,128)(2,1)S(1)} collective-permute-done((bf16[8,48,512]{2,1,0:T(8,128)(2,1)S(1)}, bf16[8,48,512]{2,1,0:T(8,128)(2,1)S(1)}, u32[]{:S(2)}, u32[]{:S(2)}) %collective-permute-start.10) | collective-permute-done | bytes 393248 | tf_op jit(solution)/shard_map/ppermute | solution.py:37
  46.0 2.8 %collective-permute-start.18 = (bf16[16,48,512]{2,1,0:T(8,128)(2,1)S(1)}, bf16[16,48,512]{2,1,0:T(8,128)(2,1)S(1)}, u32[]{:S(2)}, u32[]{:S(2)}) collective-permute-start(bf16[16,48,512]{2,1,0:T(8,128)(2,1)S(1)} %pad_maximum_fusion.1), channel_id=1, source_target_pairs={{0,96},{8,104},{16,112},{24,120},{1,97},{9,105},{17,113},{25,121},... | collective-permute-start | bytes 2359304 | tf_op jit(solution)/shard_map/ppermute | solution.py:37
  48.7 7.9 %collective-permute-done.21 = bf16[16,32,512]{2,1,0:T(8,128)(2,1)S(1)} collective-permute-done((bf16[16,32,512]{2,1,0:T(8,128)(2,1)S(1)}, bf16[16,32,512]{2,1,0:T(8,128)(2,1)S(1)}, u32[]{:S(2)}, u32[]{:S(2)}) %collective-permute-start.21) | collective-permute-done | bytes 524320 | tf_op jit(solution)/shard_map/ppermute | solution.py:37
  57.7 5.0 %collective-permute-done.13 = bf16[16,48,512]{2,1,0:T(8,128)(2,1)S(1)} collective-permute-done((bf16[16,48,512]{2,1,0:T(8,128)(2,1)S(1)}, bf16[16,48,512]{2,1,0:T(8,128)(2,1)S(1)}, u32[]{:S(2)}, u32[]{:S(2)}) %collective-permute-start.13) | collective-permute-done | bytes 786464 | tf_op jit(solution)/shard_map/ppermute | solution.py:37
  66.9 5.8 %collective-permute-done.23 = bf16[16,32,512]{2,1,0:T(8,128)(2,1)S(1)} collective-permute-done((bf16[16,32,512]{2,1,0:T(8,128)(2,1)S(1)}, bf16[16,32,512]{2,1,0:T(8,128)(2,1)S(1)}, u32[]{:S(2)}, u32[]{:S(2)}) %collective-permute-start.23) | collective-permute-done | bytes 524320 | tf_op jit(solution)/shard_map/ppermute | solution.py:37
  72.7 2.8 %collective-permute-start.19 = (bf16[8,48,512]{2,1,0:T(8,128)(2,1)S(1)}, bf16[8,48,512]{2,1,0:T(8,128)(2,1)S(1)}, u32[]{:S(2)}, u32[]{:S(2)}) collective-permute-start(bf16[8,48,512]{2,1,0:T(8,128)(2,1)S(1)} %slice.159), channel_id=1, source_target_pairs={{0,96},{8,104},{16,112},{24,120},{1,97},{9,105},{17,113},{25,121},... | collective-permute-start | bytes 1179656 | tf_op jit(solution)/shard_map/ppermute | solution.py:37
  75.4 6.2 %collective-permute-done.19 = bf16[8,48,512]{2,1,0:T(8,128)(2,1)S(1)} collective-permute-done((bf16[8,48,512]{2,1,0:T(8,128)(2,1)S(1)}, bf16[8,48,512]{2,1,0:T(8,128)(2,1)S(1)}, u32[]{:S(2)}, u32[]{:S(2)}) %collective-permute-start.19) | collective-permute-done | bytes 393248 | tf_op jit(solution)/shard_map/ppermute | solution.py:37
  81.7 26.8 %experts.1 = (bf16[8,256,192]{2,1,0:T(8,128)(2,1)S(1)}, bf16[8,128,256]{2,1,0:T(8,128)(2,1)S(1)}, bf16[2,4,48,512]{3,2,1,0:T(8,128)(2,1)S(1)}, bf16[2,4,48,512]{...) custom-call(f32[8]{0:T(128)S(1)} %add_convert_fusion.5.ids_ref, ...), custom_call_target="tpu_custom_call" | custom-call | flops 20000000000 | bytes 50000000 | tf_op jit(solution)/shard_map/experts/pallas_call | solution.py:387
  110.3 2.8 %collective-permute-start.37 = (bf16[4,2,48,512]{3,2,1,0:T(8,128)(2,1)S(1)}, bf16[4,2,48,512]{3,2,1,0:T(8,128)(2,1)S(1)}, u32[]{:S(2)}, u32[]{:S(2)}) collective-permute-start(bf16[4,2,48,512]{3,2,1,0:T(8,128)(2,1)S(1)} %get-tuple-element.79), channel_id=1, source_target_pairs={{0,96},{8,104},{16,112},{24,120},{1,97},{9,105},{17,113},{25,121},... | collective-permute-start | bytes 1179656 | tf_op jit(solution)/shard_map/ppermute | solution.py:37
  114.1 9.3 %down.1 = (bf16[2,4,48,512]{3,2,1,0:T(8,128)(2,1)S(1)}, bf16[2,4,48,512]{3,2,1,0:T(8,128)(2,1)S(1)}, bf16[2,4,48,512]{3,2,1,0:T(8,128)(2,1)S(1)}, bf16[2,4,48,51...) custom-call(s32[8]{0:T(128)S(1)} %stack.35.cols_ref, ...), custom_call_target="tpu_custom_call" | custom-call | flops 6000000000 | bytes 12000000 | tf_op jit(solution)/shard_map/down/pallas_call | solution.py:413
  124.2 2.2 %collective-permute-start.26 = (bf16[2,4,48,512]{3,2,1,0:T(8,128)(2,1)S(1)}, bf16[2,4,48,512]{3,2,1,0:T(8,128)(2,1)S(1)}, u32[]{:S(2)}, u32[]{:S(2)}) collective-permute-start(bf16[2,4,48,512]{3,2,1,0:T(8,128)(2,1)S(1)} %get-tuple-element.71), channel_id=1, source_target_pairs={{0,16},{8,24},{16,0},{24,8},{1,17},{9,25},{17,1},{25,9},{2,18},{10... | collective-permute-start | bytes 1179656 | tf_op jit(solution)/shard_map/ppermute | solution.py:37
  127.8 5.6 %collective-permute-done.39 = bf16[4,2,48,512]{3,2,1,0:T(8,128)(2,1)S(1)} collective-permute-done((bf16[4,2,48,512]{3,2,1,0:T(8,128)(2,1)S(1)}, bf16[4,2,48,512]{3,2,1,0:T(8,128)(2,1)S(1)}, u32[]{:S(2)}, u32[]{:S(2)}) %collective-permute-start.39) | collective-permute-done | bytes 393248 | tf_op jit(solution)/shard_map/ppermute | solution.py:37
  135.6 2.2 %collective-permute-start.25 = (bf16[4,4,48,512]{3,2,1,0:T(8,128)(2,1)S(1)}, bf16[4,4,48,512]{3,2,1,0:T(8,128)(2,1)S(1)}, u32[]{:S(2)}, u32[]{:S(2)}) collective-permute-start(bf16[4,4,48,512]{3,2,1,0:T(8,128)(2,1)S(1)} %pad_maximum_fusion.2), channel_id=1, source_target_pairs={{0,16},{8,24},{16,0},{24,8},{1,17},{9,25},{17,1},{25,9},{2,18},{10... | collective-permute-start | bytes 2359304 | tf_op jit(solution)/shard_map/ppermute | solution.py:37
  138.1 5.9 %collective-permute-done.31 = bf16[4,4,32,512]{3,2,1,0:T(8,128)(2,1)S(1)} collective-permute-done((bf16[4,4,32,512]{3,2,1,0:T(8,128)(2,1)S(1)}, bf16[4,4,32,512]{3,2,1,0:T(8,128)(2,1)S(1)}, u32[]{:S(2)}, u32[]{:S(2)}) %collective-permute-start.31) | collective-permute-done | bytes 524320 | tf_op jit(solution)/shard_map/ppermute | solution.py:37
  144.4 3.7 %collective-permute-done.38 = bf16[8,2,48,512]{3,2,1,0:T(8,128)(2,1)S(1)} collective-permute-done((bf16[8,2,48,512]{3,2,1,0:T(8,128)(2,1)S(1)}, bf16[8,2,48,512]{3,2,1,0:T(8,128)(2,1)S(1)}, u32[]{:S(2)}, u32[]{:S(2)}) %collective-permute-start.38) | collective-permute-done | bytes 786464 | tf_op jit(solution)/shard_map/ppermute | solution.py:37
  150.8 7.8 %collective-permute-done.33 = bf16[2,4,32,512]{3,2,1,0:T(8,128)(2,1)S(1)} collective-permute-done((bf16[2,4,32,512]{3,2,1,0:T(8,128)(2,1)S(1)}, bf16[2,4,32,512]{3,2,1,0:T(8,128)(2,1)S(1)}, u32[]{:S(2)}, u32[]{:S(2)}) %collective-permute-start.33) | collective-permute-done | bytes 262176 | tf_op jit(solution)/shard_map/ppermute | solution.py:37
  158.6 1.9 collective-permute-start.34
  160.9 2.8 %collective-permute-done.34 = bf16[4,32,512]{2,1,0:T(8,128)(2,1)S(1)} collective-permute-done((bf16[4,32,512]{2,1,0:T(8,128)(2,1)S(1)}, bf16[4,32,512]{2,1,0:T(8,128)(2,1)S(1)}, u32[]{:S(2)}, u32[]{:S(2)}) %collective-permute-start.34) | collective-permute-done | bytes 131104 | tf_op jit(solution)/shard_map/ppermute | solution.py:37
  164.1 6.6 %collective-permute-done.28 = bf16[2,4,48,512]{3,2,1,0:T(8,128)(2,1)S(1)} collective-permute-done((bf16[2,4,48,512]{3,2,1,0:T(8,128)(2,1)S(1)}, bf16[2,4,48,512]{3,2,1,0:T(8,128)(2,1)S(1)}, u32[]{:S(2)}, u32[]{:S(2)}) %collective-permute-start.28) | collective-permute-done | bytes 393248 | tf_op jit(solution)/shard_map/ppermute | solution.py:37
  171.4 5.4 %collective-permute-done.29 = bf16[4,48,512]{2,1,0:T(8,128)(2,1)S(1)} collective-permute-done((bf16[4,48,512]{2,1,0:T(8,128)(2,1)S(1)}, bf16[4,48,512]{2,1,0:T(8,128)(2,1)S(1)}, u32[]{:S(2)}, u32[]{:S(2)}) %collective-permute-start.29) | collective-permute-done | bytes 196640 | tf_op jit(solution)/shard_map/ppermute | solution.py:37
  178.0 5.5 %collective-permute-done.35 = bf16[2,80,512]{2,1,0:T(8,128)(2,1)S(1)} collective-permute-done((bf16[2,80,512]{2,1,0:T(8,128)(2,1)S(1)}, bf16[2,80,512]{2,1,0:T(8,128)(2,1)S(1)}, u32[]{:S(2)}, u32[]{:S(2)}) %collective-permute-start.35) | collective-permute-done | bytes 163872 | tf_op jit(solution)/shard_map/ppermute | solution.py:37
  183.7 4.3 %collective-permute-done.36 = bf16[1,80,512]{2,1,0:T(8,128)(2,1)S(1)} collective-permute-done((bf16[1,80,512]{2,1,0:T(8,128)(2,1)S(1)}, bf16[1,80,512]{2,1,0:T(8,128)(2,1)S(1)}, u32[]{:S(2)}, u32[]{:S(2)}) %collective-permute-start.36) | collective-permute-done | bytes 81952 | tf_op jit(solution)/shard_map/ppermute | solution.py:37
  (126 shorter events, 33.5 us)
Async XLA Ops:
  0.0 17.2 %collective-permute-start.4 = (bf16[4,192,4096]{2,1,0:T(8,128)(2,1)}, bf16[4,192,4096]{2,1,0:T(8,128)(2,1)}, u32[]{:S(2)}, u32[]{:S(2)}) collective-permute-start(bf16[4,192,4096]{2,1,0:T(8,128)(2,1)} %wg.1), channel_id=1, source_target_pairs={{0,8},{8,0},{16,24},{24,16},{1,9},{9,1},{17,25},{25,17},{2,10},{10... | collective-permute-start | bytes 18874376 | tf_op jit(solution)/shard_map/ppermute | solution.py:42
  17.2 10.6 %collective-permute-start.8 = (bf16[4,192,4096]{2,1,0:T(8,128)(2,1)}, bf16[4,192,4096]{2,1,0:T(8,128)(2,1)}, u32[]{:S(2)}, u32[]{:S(2)}) collective-permute-start(bf16[4,192,4096]{2,1,0:T(8,128)(2,1)} %wu), channel_id=1, source_target_pairs={{0,8},{8,0},{16,24},{24,16},{1,9},{9,1},{17,25},{25,17},{2,10},{10... | collective-permute-start | bytes 18874376 | tf_op jit(solution)/shard_map/ppermute | solution.py:42
  18.1 8.5 %collective-permute-start.6 = (bf16[4,48,512]{2,1,0:T(8,128)(2,1)S(1)}, bf16[4,48,512]{2,1,0:T(8,128)(2,1)S(1)}, u32[]{:S(2)}, u32[]{:S(2)}) collective-permute-start(bf16[4,48,512]{2,1,0:T(8,128)(2,1)S(1)} %pad_maximum_fusion.12), channel_id=1, source_target_pairs={{0,17},{8,25},{16,1},{24,9},{1,16},{9,24},{17,0},{25,8},{2,19},{10... | collective-permute-start | bytes 589832 | tf_op jit(solution)/shard_map/ppermute | solution.py:37
  27.8 15.6 %collective-permute-start.12 = (bf16[4,192,4096]{2,1,0:T(8,128)(2,1)}, bf16[4,192,4096]{2,1,0:T(8,128)(2,1)S(1)}, u32[]{:S(2)}, u32[]{:S(2)}) collective-permute-start(bf16[4,192,4096]{2,1,0:T(8,128)(2,1)} %wd.1), channel_id=1, source_target_pairs={{0,8},{8,0},{16,24},{24,16},{1,9},{9,1},{17,25},{25,17},{2,10},{10... | collective-permute-start | bytes 18874376 | tf_op jit(solution)/shard_map/ppermute | solution.py:42
  27.9 12.6 %collective-permute-start.9 = (bf16[8,48,512]{2,1,0:T(8,128)(2,1)S(1)}, bf16[8,48,512]{2,1,0:T(8,128)(2,1)S(1)}, u32[]{:S(2)}, u32[]{:S(2)}) collective-permute-start(bf16[8,48,512]{2,1,0:T(8,128)(2,1)S(1)} %pad_maximum_fusion.9), channel_id=1, source_target_pairs={{0,6},{8,14},{16,22},{24,30},{1,7},{9,15},{17,23},{25,31},{2,4},{1... | collective-permute-start | bytes 1179656 | tf_op jit(solution)/shard_map/ppermute | solution.py:37
  30.1 8.5 %collective-permute-start.11 = (bf16[8,32,512]{2,1,0:T(8,128)(2,1)S(1)}, bf16[8,32,512]{2,1,0:T(8,128)(2,1)S(1)}, u32[]{:S(2)}, u32[]{:S(2)}) collective-permute-start(bf16[8,32,512]{2,1,0:T(8,128)(2,1)S(1)} %fusion.3), channel_id=1, source_target_pairs={{0,17},{8,25},{16,1},{24,9},{1,16},{9,24},{17,0},{25,8},{2,19},{10... | collective-permute-start | bytes 786440 | tf_op jit(solution)/shard_map/ppermute | solution.py:37
  32.1 11.3 %collective-permute-start.10 = (bf16[8,48,512]{2,1,0:T(8,128)(2,1)S(1)}, bf16[8,48,512]{2,1,0:T(8,128)(2,1)S(1)}, u32[]{:S(2)}, u32[]{:S(2)}) collective-permute-start(bf16[8,48,512]{2,1,0:T(8,128)(2,1)S(1)} %pad_maximum_fusion.10), channel_id=1, source_target_pairs={{0,16},{8,24},{16,0},{24,8},{1,17},{9,25},{17,1},{25,9},{2,18},{10... | collective-permute-start | bytes 1179656 | tf_op jit(solution)/shard_map/ppermute | solution.py:37
  43.5 13.1 %collective-permute-start.21 = (bf16[16,32,512]{2,1,0:T(8,128)(2,1)S(1)}, bf16[16,32,512]{2,1,0:T(8,128)(2,1)S(1)}, u32[]{:S(2)}, u32[]{:S(2)}) collective-permute-start(bf16[16,32,512]{2,1,0:T(8,128)(2,1)S(1)} %pad_maximum_fusion.6), channel_id=1, source_target_pairs={{0,2},{8,10},{16,18},{24,26},{1,3},{9,11},{17,19},{25,27},{2,0},{1... | collective-permute-start | bytes 1572872 | tf_op jit(solution)/shard_map/ppermute | solution.py:37
  44.2 18.4 %collective-permute-start.13 = (bf16[16,48,512]{2,1,0:T(8,128)(2,1)S(1)}, bf16[16,48,512]{2,1,0:T(8,128)(2,1)S(1)}, u32[]{:S(2)}, u32[]{:S(2)}) collective-permute-start(bf16[16,48,512]{2,1,0:T(8,128)(2,1)S(1)} %pad_maximum_fusion), channel_id=1, source_target_pairs={{0,16},{8,24},{16,0},{24,8},{1,17},{9,25},{17,1},{25,9},{2,18},{10... | collective-permute-start | bytes 2359304 | tf_op jit(solution)/shard_map/ppermute | solution.py:37
  46.0 17.9 %collective-permute-start.14 = (bf16[16,48,512]{2,1,0:T(8,128)(2,1)S(1)}, bf16[16,48,512]{2,1,0:T(8,128)(2,1)S(1)}, u32[]{:S(2)}, u32[]{:S(2)}) collective-permute-start(bf16[16,48,512]{2,1,0:T(8,128)(2,1)S(1)} %pad_maximum_fusion), channel_id=1, source_target_pairs={{0,17},{8,25},{16,1},{24,9},{1,16},{9,24},{17,0},{25,8},{2,19},{10... | collective-permute-start | bytes 2359304 | tf_op jit(solution)/shard_map/ppermute | solution.py:37
  46.0 19.8 %collective-permute-start.18 = (bf16[16,48,512]{2,1,0:T(8,128)(2,1)S(1)}, bf16[16,48,512]{2,1,0:T(8,128)(2,1)S(1)}, u32[]{:S(2)}, u32[]{:S(2)}) collective-permute-start(bf16[16,48,512]{2,1,0:T(8,128)(2,1)S(1)} %pad_maximum_fusion.1), channel_id=1, source_target_pairs={{0,96},{8,104},{16,112},{24,120},{1,97},{9,105},{17,113},{25,121},... | collective-permute-start | bytes 2359304 | tf_op jit(solution)/shard_map/ppermute | solution.py:37
  48.7 18.0 %collective-permute-start.17 = (bf16[16,48,512]{2,1,0:T(8,128)(2,1)S(1)}, bf16[16,48,512]{2,1,0:T(8,128)(2,1)S(1)}, u32[]{:S(2)}, u32[]{:S(2)}) collective-permute-start(bf16[16,48,512]{2,1,0:T(8,128)(2,1)S(1)} %pad_maximum_fusion.1), channel_id=1, source_target_pairs={{0,32},{8,40},{16,48},{24,56},{1,33},{9,41},{17,49},{25,57},{2,34}... | collective-permute-start | bytes 2359304 | tf_op jit(solution)/shard_map/ppermute | solution.py:37
  56.6 16.1 %collective-permute-start.23 = (bf16[16,32,512]{2,1,0:T(8,128)(2,1)S(1)}, bf16[16,32,512]{2,1,0:T(8,128)(2,1)S(1)}, u32[]{:S(2)}, u32[]{:S(2)}) collective-permute-start(bf16[16,32,512]{2,1,0:T(8,128)(2,1)S(1)} %collective-permute-done.21), channel_id=1, source_target_pairs={{0,6},{8,14},{16,22},{24,30},{1,7},{9,15},{17,23},{25,31},{2,4},{1... | collective-permute-start | bytes 1572872 | tf_op jit(solution)/shard_map/ppermute | solution.py:37
  62.6 19.0 %collective-permute-start.22 = (bf16[16,32,512]{2,1,0:T(8,128)(2,1)S(1)}, bf16[16,32,512]{2,1,0:T(8,128)(2,1)S(1)}, u32[]{:S(2)}, u32[]{:S(2)}) collective-permute-start(bf16[16,32,512]{2,1,0:T(8,128)(2,1)S(1)} %pad_maximum_fusion.6), channel_id=1, source_target_pairs={{0,6},{8,14},{16,22},{24,30},{1,7},{9,15},{17,23},{25,31},{2,4},{1... | collective-permute-start | bytes 1572872 | tf_op jit(solution)/shard_map/ppermute | solution.py:37
  63.9 11.6 %collective-permute-start.16 = (bf16[8,48,512]{2,1,0:T(8,128)(2,1)S(1)}, bf16[8,48,512]{2,1,0:T(8,128)(2,1)S(1)}, u32[]{:S(2)}, u32[]{:S(2)}) collective-permute-start(bf16[8,48,512]{2,1,0:T(8,128)(2,1)S(1)} %slice.158), channel_id=1, source_target_pairs={{0,16},{8,24},{16,0},{24,8},{1,17},{9,25},{17,1},{25,9},{2,18},{10... | collective-permute-start | bytes 1179656 | tf_op jit(solution)/shard_map/ppermute | solution.py:37
  65.7 9.7 %collective-permute-start.15 = (bf16[8,48,512]{2,1,0:T(8,128)(2,1)S(1)}, bf16[8,48,512]{2,1,0:T(8,128)(2,1)S(1)}, u32[]{:S(2)}, u32[]{:S(2)}) collective-permute-start(bf16[8,48,512]{2,1,0:T(8,128)(2,1)S(1)} %slice.124), channel_id=1, source_target_pairs={{0,17},{8,25},{16,1},{24,9},{1,16},{9,24},{17,0},{25,8},{2,19},{10... | collective-permute-start | bytes 1179656 | tf_op jit(solution)/shard_map/ppermute | solution.py:37
  66.8 8.7 %collective-permute-start.20 = (bf16[8,48,512]{2,1,0:T(8,128)(2,1)S(1)}, bf16[8,48,512]{2,1,0:T(8,128)(2,1)S(1)}, u32[]{:S(2)}, u32[]{:S(2)}) collective-permute-start(bf16[8,48,512]{2,1,0:T(8,128)(2,1)S(1)} %slice.160), channel_id=1, source_target_pairs={{0,32},{8,40},{16,48},{24,56},{1,33},{9,41},{17,49},{25,57},{2,34}... | collective-permute-start | bytes 1179656 | tf_op jit(solution)/shard_map/ppermute | solution.py:37
  72.7 9.0 %collective-permute-start.19 = (bf16[8,48,512]{2,1,0:T(8,128)(2,1)S(1)}, bf16[8,48,512]{2,1,0:T(8,128)(2,1)S(1)}, u32[]{:S(2)}, u32[]{:S(2)}) collective-permute-start(bf16[8,48,512]{2,1,0:T(8,128)(2,1)S(1)} %slice.159), channel_id=1, source_target_pairs={{0,96},{8,104},{16,112},{24,120},{1,97},{9,105},{17,113},{25,121},... | collective-permute-start | bytes 1179656 | tf_op jit(solution)/shard_map/ppermute | solution.py:37
  110.3 16.2 %collective-permute-start.37 = (bf16[4,2,48,512]{3,2,1,0:T(8,128)(2,1)S(1)}, bf16[4,2,48,512]{3,2,1,0:T(8,128)(2,1)S(1)}, u32[]{:S(2)}, u32[]{:S(2)}) collective-permute-start(bf16[4,2,48,512]{3,2,1,0:T(8,128)(2,1)S(1)} %get-tuple-element.79), channel_id=1, source_target_pairs={{0,96},{8,104},{16,112},{24,120},{1,97},{9,105},{17,113},{25,121},... | collective-permute-start | bytes 1179656 | tf_op jit(solution)/shard_map/ppermute | solution.py:37
  113.0 20.5 %collective-permute-start.30 = (bf16[4,4,32,512]{3,2,1,0:T(8,128)(2,1)S(1)}, bf16[4,4,32,512]{3,2,1,0:T(8,128)(2,1)S(1)}, u32[]{:S(2)}, u32[]{:S(2)}) collective-permute-start(bf16[4,4,32,512]{3,2,1,0:T(8,128)(2,1)S(1)} %get-tuple-element.75), channel_id=1, source_target_pairs={{0,6},{8,14},{16,22},{24,30},{1,7},{9,15},{17,23},{25,31},{2,4},{1... | collective-permute-start | bytes 1572872 | tf_op jit(solution)/shard_map/ppermute | solution.py:37
  123.4 10.0 %collective-permute-start.39 = (bf16[4,2,48,512]{3,2,1,0:T(8,128)(2,1)S(1)}, bf16[4,2,48,512]{3,2,1,0:T(8,128)(2,1)S(1)}, u32[]{:S(2)}, u32[]{:S(2)}) collective-permute-start(bf16[4,2,48,512]{3,2,1,0:T(8,128)(2,1)S(1)} %get-tuple-element.83), channel_id=1, source_target_pairs={{0,32},{8,40},{16,48},{24,56},{1,33},{9,41},{17,49},{25,57},{2,34}... | collective-permute-start | bytes 1179656 | tf_op jit(solution)/shard_map/ppermute | solution.py:37
  123.5 11.4 %collective-permute-start.24 = (bf16[2,4,48,512]{3,2,1,0:T(8,128)(2,1)S(1)}, bf16[2,4,48,512]{3,2,1,0:T(8,128)(2,1)S(1)}, u32[]{:S(2)}, u32[]{:S(2)}) collective-permute-start(bf16[2,4,48,512]{3,2,1,0:T(8,128)(2,1)S(1)} %get-tuple-element.67), channel_id=1, source_target_pairs={{0,17},{8,25},{16,1},{24,9},{1,16},{9,24},{17,0},{25,8},{2,19},{10... | collective-permute-start | bytes 1179656 | tf_op jit(solution)/shard_map/ppermute | solution.py:37
  124.2 11.4 %collective-permute-start.26 = (bf16[2,4,48,512]{3,2,1,0:T(8,128)(2,1)S(1)}, bf16[2,4,48,512]{3,2,1,0:T(8,128)(2,1)S(1)}, u32[]{:S(2)}, u32[]{:S(2)}) collective-permute-start(bf16[2,4,48,512]{3,2,1,0:T(8,128)(2,1)S(1)} %get-tuple-element.71), channel_id=1, source_target_pairs={{0,16},{8,24},{16,0},{24,8},{1,17},{9,25},{17,1},{25,9},{2,18},{10... | collective-permute-start | bytes 1179656 | tf_op jit(solution)/shard_map/ppermute | solution.py:37
  126.5 11.5 %collective-permute-start.32 = (bf16[4,4,32,512]{3,2,1,0:T(8,128)(2,1)S(1)}, bf16[4,4,32,512]{3,2,1,0:T(8,128)(2,1)S(1)}, u32[]{:S(2)}, u32[]{:S(2)}) collective-permute-start(bf16[4,4,32,512]{3,2,1,0:T(8,128)(2,1)S(1)} %get-tuple-element.76), channel_id=1, source_target_pairs={{0,6},{8,14},{16,22},{24,30},{1,7},{9,15},{17,23},{25,31},{2,4},{1... | collective-permute-start | bytes 1572872 | tf_op jit(solution)/shard_map/ppermute | solution.py:37
  133.4 14.7 %collective-permute-start.38 = (bf16[8,2,48,512]{3,2,1,0:T(8,128)(2,1)S(1)}, bf16[8,2,48,512]{3,2,1,0:T(8,128)(2,1)S(1)}, u32[]{:S(2)}, u32[]{:S(2)}) collective-permute-start(bf16[8,2,48,512]{3,2,1,0:T(8,128)(2,1)S(1)} %pad_maximum_fusion.4), channel_id=1, source_target_pairs={{0,32},{8,40},{16,48},{24,56},{1,33},{9,41},{17,49},{25,57},{2,34}... | collective-permute-start | bytes 2359304 | tf_op jit(solution)/shard_map/ppermute | solution.py:37
  134.7 9.3 %collective-permute-start.31 = (bf16[4,4,32,512]{3,2,1,0:T(8,128)(2,1)S(1)}, bf16[4,4,32,512]{3,2,1,0:T(8,128)(2,1)S(1)}, u32[]{:S(2)}, u32[]{:S(2)}) collective-permute-start(bf16[4,4,32,512]{3,2,1,0:T(8,128)(2,1)S(1)} %add.139), channel_id=1, source_target_pairs={{0,2},{8,10},{16,18},{24,26},{1,3},{9,11},{17,19},{25,27},{2,0},{1... | collective-permute-start | bytes 1572872 | tf_op jit(solution)/shard_map/ppermute | solution.py:37
  134.9 14.0 %collective-permute-start.40 = (bf16[8,2,48,512]{3,2,1,0:T(8,128)(2,1)S(1)}, bf16[8,2,48,512]{3,2,1,0:T(8,128)(2,1)S(1)}, u32[]{:S(2)}, u32[]{:S(2)}) collective-permute-start(bf16[8,2,48,512]{3,2,1,0:T(8,128)(2,1)S(1)} %pad_maximum_fusion.5), channel_id=1, source_target_pairs={{0,96},{8,104},{16,112},{24,120},{1,97},{9,105},{17,113},{25,121},... | collective-permute-start | bytes 2359304 | tf_op jit(solution)/shard_map/ppermute | solution.py:37
  135.6 24.8 %collective-permute-start.25 = (bf16[4,4,48,512]{3,2,1,0:T(8,128)(2,1)S(1)}, bf16[4,4,48,512]{3,2,1,0:T(8,128)(2,1)S(1)}, u32[]{:S(2)}, u32[]{:S(2)}) collective-permute-start(bf16[4,4,48,512]{3,2,1,0:T(8,128)(2,1)S(1)} %pad_maximum_fusion.2), channel_id=1, source_target_pairs={{0,16},{8,24},{16,0},{24,8},{1,17},{9,25},{17,1},{25,9},{2,18},{10... | collective-permute-start | bytes 2359304 | tf_op jit(solution)/shard_map/ppermute | solution.py:37
  138.0 22.5 %collective-permute-start.27 = (bf16[4,4,48,512]{3,2,1,0:T(8,128)(2,1)S(1)}, bf16[4,4,48,512]{3,2,1,0:T(8,128)(2,1)S(1)}, u32[]{:S(2)}, u32[]{:S(2)}) collective-permute-start(bf16[4,4,48,512]{3,2,1,0:T(8,128)(2,1)S(1)} %pad_maximum_fusion.3), channel_id=1, source_target_pairs={{0,17},{8,25},{16,1},{24,9},{1,16},{9,24},{17,0},{25,8},{2,19},{10... | collective-permute-start | bytes 2359304 | tf_op jit(solution)/shard_map/ppermute | solution.py:37
  144.3 14.3 %collective-permute-start.33 = (bf16[2,4,32,512]{3,2,1,0:T(8,128)(2,1)S(1)}, bf16[2,4,32,512]{3,2,1,0:T(8,128)(2,1)S(1)}, u32[]{:S(2)}, u32[]{:S(2)}) collective-permute-start(bf16[2,4,32,512]{3,2,1,0:T(8,128)(2,1)S(1)} %slice.168), channel_id=1, source_target_pairs={{0,17},{8,25},{16,1},{24,9},{1,16},{9,24},{17,0},{25,8},{2,19},{10... | collective-permute-start | bytes 786440 | tf_op jit(solution)/shard_map/ppermute | solution.py:37
  149.3 14.4 %collective-permute-start.41 = (bf16[2,4,48,512]{3,2,1,0:T(8,128)(2,1)S(1)}, bf16[2,4,48,512]{3,2,1,0:T(8,128)(2,1)S(1)}, u32[]{:S(2)}, u32[]{:S(2)}) collective-permute-start(bf16[2,4,48,512]{3,2,1,0:T(8,128)(2,1)S(1)} %pad_maximum_fusion.7), channel_id=1, source_target_pairs={{0,16},{8,24},{16,0},{24,8},{1,17},{9,25},{17,1},{25,9},{2,18},{10... | collective-permute-start | bytes 1179656 | tf_op jit(solution)/shard_map/ppermute | solution.py:37
  160.6 10.1 %collective-permute-start.28 = (bf16[2,4,48,512]{3,2,1,0:T(8,128)(2,1)S(1)}, bf16[2,4,48,512]{3,2,1,0:T(8,128)(2,1)S(1)}, u32[]{:S(2)}, u32[]{:S(2)}) collective-permute-start(bf16[2,4,48,512]{3,2,1,0:T(8,128)(2,1)S(1)} %add_convert_fusion.3), channel_id=1, source_target_pairs={{0,6},{8,14},{16,22},{24,30},{1,7},{9,15},{17,23},{25,31},{2,4},{1... | collective-permute-start | bytes 1179656 | tf_op jit(solution)/shard_map/ppermute | solution.py:37
  (16 other events, 120.5 us)

commit v5 on v4

--- a/solution.py
+++ b/solution.py
@@ -242,7 +242,7 @@
             sorted_rows[:, :, pl.ds(pl.multiple_of(b * 32, 32), 32)] = rows
             return carry
 
-        lax.fori_loop(0, 8, dispatch, 0, unroll=4)
+        lax.fori_loop(0, 8, dispatch, 0, unroll=8)
         finish(fetch(ky))
 
         def project(e, carry):
@@ -261,7 +261,7 @@
                 h_ref[e] = (gate / (1.0 + jnp.exp(-gate)) * up * gate_col[e]).astype(BF16)
             return carry
 
-        lax.fori_loop(0, 8, project, 0, unroll=4)
+        lax.fori_loop(0, 8, project, 0, unroll=8)
         if ky < 2:
             start(fetch(ky + 2))
         if ky == 2:
@@ -277,7 +277,7 @@
             sorted_rows[:, :, rows] = out.astype(BF16).reshape(4, 2, 32, 1024)
             return carry
 
-        lax.fori_loop(0, 8, project_out, 0, unroll=4)
+        lax.fori_loop(0, 8, project_out, 0, unroll=8)
         col = pl.ds(1024 * n, 1024)
 
         def combine(b, carry):
@@ -286,7 +286,7 @@
             tokens[at[0], at[1], :, col] = out.astype(BF16)
             return carry
 
-        lax.fori_loop(0, 8, combine, 0, unroll=4)
+        lax.fori_loop(0, 8, combine, 0, unroll=8)
         pairs = y_pairs(outs, kys, n, cols_ref, tokens.at[:, :, :, col])
         stores.append(
             [pltpu.make_async_copy(b, a, t_sem.at[n, m]) for m, (a, b) in enumerate(pairs)]
@@ -335,7 +335,7 @@
             ybuf[n, b // 2, lax.rem(b, 2)] = out.astype(BF16)
             return carry
 
-        lax.fori_loop(0, 8, combine, 0, unroll=4)
+        lax.fori_loop(0, 8, combine, 0, unroll=8)
         for copy in stores(n):
             copy.start()
     for n in range(2):

time: 189 us -> 187 us (0.989)
  Pallas kernels: 36.1 us -> 33.8 us
    pallas_call x1, Pallas kernels: 26.8 us -> 24.8 us  [local(): pl.pallas_call(functools.partial(expert_kernel, (2, 3)), out_shape=[jax.S...]
where the time goes in v5:
time: 187 us; the launch traced here: 186 us
  waiting for transfers between devices  94 us (50%)
  starting transfers between devices  48.6 us (26%)
  Pallas kernels  33.8 us (18%)
  other arithmetic  5.73 us (3%)
  local copies, waits for them, and re-layouts  3.71 us (2%)
    ppermute x42, waiting for transfers between devices, swap(): return lax.ppermute(value, AXES, pairs)  92.8 us
    ppermute x42, starting transfers between devices, swap(): return lax.ppermute(value, AXES, pairs)  48.4 us
    pallas_call x1, Pallas kernels, local(): pl.pallas_call(functools.partial(expert_kernel, (2, 3)), out_shape=[jax.S...  24.8 us
    pallas_call x1, Pallas kernels, local(): pl.pallas_call(functools.partial(down_kernel, (0, 1)), out_shape=shapes,...  8.96 us
  transfers between devices with their start and end apart: 45, of which 23 were waited for; matrix products, arithmetic and copies ran while one was open for 4% of the time, Pallas kernels for 5%

profile of v5, /device:TPU:32, one launch (start us, length us, event | category | flops | bytes accessed | tf_op | source)
XLA Modules:
  0.0 186.4 jit_solution(734065150890471221)
XLA Ops:
  6.2 2.3 %collective-permute-start.3 = (bf16[2,48,512]{2,1,0:T(8,128)(2,1)S(1)}, bf16[2,48,512]{2,1,0:T(8,128)(2,1)S(1)}, u32[]{:S(2)}, u32[]{:S(2)}) collective-permute-start(bf16[2,48,512]{2,1,0:T(8,128)(2,1)S(1)} %pad_maximum_fusion.16), channel_id=1, source_target_pairs={{0,6},{8,14},{16,22},{24,30},{1,7},{9,15},{17,23},{25,31},{2,4},{1... | collective-permute-start | bytes 294920 | tf_op jit(solution)/shard_map/ppermute | solution.py:37
  9.7 2.8 %collective-permute-start.1 = (bf16[2,96,512]{2,1,0:T(8,128)(2,1)S(1)}, bf16[2,96,512]{2,1,0:T(8,128)(2,1)S(1)}, u32[]{:S(2)}, u32[]{:S(2)}) collective-permute-start(bf16[2,96,512]{2,1,0:T(8,128)(2,1)S(1)} %pad_maximum_fusion.11), channel_id=1, source_target_pairs={{0,96},{8,104},{16,112},{24,120},{1,97},{9,105},{17,113},{25,121},... | collective-permute-start | bytes 589832 | tf_op jit(solution)/shard_map/ppermute | solution.py:37
  12.5 4.6 %collective-permute-done.1 = bf16[2,96,512]{2,1,0:T(8,128)(2,1)S(1)} collective-permute-done((bf16[2,96,512]{2,1,0:T(8,128)(2,1)S(1)}, bf16[2,96,512]{2,1,0:T(8,128)(2,1)S(1)}, u32[]{:S(2)}, u32[]{:S(2)}) %collective-permute-start.1) | collective-permute-done | bytes 196640 | tf_op jit(solution)/shard_map/ppermute | solution.py:37
  18.1 3.5 %collective-permute-start.6 = (bf16[4,48,512]{2,1,0:T(8,128)(2,1)S(1)}, bf16[4,48,512]{2,1,0:T(8,128)(2,1)S(1)}, u32[]{:S(2)}, u32[]{:S(2)}) collective-permute-start(bf16[4,48,512]{2,1,0:T(8,128)(2,1)S(1)} %pad_maximum_fusion.12), channel_id=1, source_target_pairs={{0,17},{8,25},{16,1},{24,9},{1,16},{9,24},{17,0},{25,8},{2,19},{10... | collective-permute-start | bytes 589832 | tf_op jit(solution)/shard_map/ppermute | solution.py:37
  21.6 3.2 %collective-permute-done.7 = bf16[4,48,512]{2,1,0:T(8,128)(2,1)S(1)} collective-permute-done((bf16[4,48,512]{2,1,0:T(8,128)(2,1)S(1)}, bf16[4,48,512]{2,1,0:T(8,128)(2,1)S(1)}, u32[]{:S(2)}, u32[]{:S(2)}) %collective-permute-start.7) | collective-permute-done | bytes 196640 | tf_op jit(solution)/shard_map/ppermute | solution.py:37
  27.9 2.2 %collective-permute-start.9 = (bf16[8,48,512]{2,1,0:T(8,128)(2,1)S(1)}, bf16[8,48,512]{2,1,0:T(8,128)(2,1)S(1)}, u32[]{:S(2)}, u32[]{:S(2)}) collective-permute-start(bf16[8,48,512]{2,1,0:T(8,128)(2,1)S(1)} %pad_maximum_fusion.9), channel_id=1, source_target_pairs={{0,6},{8,14},{16,22},{24,30},{1,7},{9,15},{17,23},{25,31},{2,4},{1... | collective-permute-start | bytes 1179656 | tf_op jit(solution)/shard_map/ppermute | solution.py:37
  30.1 1.9 %collective-permute-start.11 = (bf16[8,32,512]{2,1,0:T(8,128)(2,1)S(1)}, bf16[8,32,512]{2,1,0:T(8,128)(2,1)S(1)}, u32[]{:S(2)}, u32[]{:S(2)}) collective-permute-start(bf16[8,32,512]{2,1,0:T(8,128)(2,1)S(1)} %fusion.3), channel_id=1, source_target_pairs={{0,17},{8,25},{16,1},{24,9},{1,16},{9,24},{17,0},{25,8},{2,19},{10... | collective-permute-start | bytes 786440 | tf_op jit(solution)/shard_map/ppermute | solution.py:37
  32.1 2.2 %collective-permute-start.10 = (bf16[8,48,512]{2,1,0:T(8,128)(2,1)S(1)}, bf16[8,48,512]{2,1,0:T(8,128)(2,1)S(1)}, u32[]{:S(2)}, u32[]{:S(2)}) collective-permute-start(bf16[8,48,512]{2,1,0:T(8,128)(2,1)S(1)} %pad_maximum_fusion.10), channel_id=1, source_target_pairs={{0,16},{8,24},{16,0},{24,8},{1,17},{9,25},{17,1},{25,9},{2,18},{10... | collective-permute-start | bytes 1179656 | tf_op jit(solution)/shard_map/ppermute | solution.py:37
  34.3 4.3 %collective-permute-done.11 = bf16[8,32,512]{2,1,0:T(8,128)(2,1)S(1)} collective-permute-done((bf16[8,32,512]{2,1,0:T(8,128)(2,1)S(1)}, bf16[8,32,512]{2,1,0:T(8,128)(2,1)S(1)}, u32[]{:S(2)}, u32[]{:S(2)}) %collective-permute-start.11) | collective-permute-done | bytes 262176 | tf_op jit(solution)/shard_map/ppermute | solution.py:37
  38.7 1.9 %collective-permute-done.9 = bf16[8,48,512]{2,1,0:T(8,128)(2,1)S(1)} collective-permute-done((bf16[8,48,512]{2,1,0:T(8,128)(2,1)S(1)}, bf16[8,48,512]{2,1,0:T(8,128)(2,1)S(1)}, u32[]{:S(2)}, u32[]{:S(2)}) %collective-permute-start.9) | collective-permute-done | bytes 393248 | tf_op jit(solution)/shard_map/ppermute | solution.py:37
  40.6 2.7 %collective-permute-done.10 = bf16[8,48,512]{2,1,0:T(8,128)(2,1)S(1)} collective-permute-done((bf16[8,48,512]{2,1,0:T(8,128)(2,1)S(1)}, bf16[8,48,512]{2,1,0:T(8,128)(2,1)S(1)}, u32[]{:S(2)}, u32[]{:S(2)}) %collective-permute-start.10) | collective-permute-done | bytes 393248 | tf_op jit(solution)/shard_map/ppermute | solution.py:37
  46.0 2.8 %collective-permute-start.18 = (bf16[16,48,512]{2,1,0:T(8,128)(2,1)S(1)}, bf16[16,48,512]{2,1,0:T(8,128)(2,1)S(1)}, u32[]{:S(2)}, u32[]{:S(2)}) collective-permute-start(bf16[16,48,512]{2,1,0:T(8,128)(2,1)S(1)} %pad_maximum_fusion.1), channel_id=1, source_target_pairs={{0,96},{8,104},{16,112},{24,120},{1,97},{9,105},{17,113},{25,121},... | collective-permute-start | bytes 2359304 | tf_op jit(solution)/shard_map/ppermute | solution.py:37
  48.7 7.9 %collective-permute-done.21 = bf16[16,32,512]{2,1,0:T(8,128)(2,1)S(1)} collective-permute-done((bf16[16,32,512]{2,1,0:T(8,128)(2,1)S(1)}, bf16[16,32,512]{2,1,0:T(8,128)(2,1)S(1)}, u32[]{:S(2)}, u32[]{:S(2)}) %collective-permute-start.21) | collective-permute-done | bytes 524320 | tf_op jit(solution)/shard_map/ppermute | solution.py:37
  57.7 5.0 %collective-permute-done.13 = bf16[16,48,512]{2,1,0:T(8,128)(2,1)S(1)} collective-permute-done((bf16[16,48,512]{2,1,0:T(8,128)(2,1)S(1)}, bf16[16,48,512]{2,1,0:T(8,128)(2,1)S(1)}, u32[]{:S(2)}, u32[]{:S(2)}) %collective-permute-start.13) | collective-permute-done | bytes 786464 | tf_op jit(solution)/shard_map/ppermute | solution.py:37
  66.9 5.8 %collective-permute-done.23 = bf16[16,32,512]{2,1,0:T(8,128)(2,1)S(1)} collective-permute-done((bf16[16,32,512]{2,1,0:T(8,128)(2,1)S(1)}, bf16[16,32,512]{2,1,0:T(8,128)(2,1)S(1)}, u32[]{:S(2)}, u32[]{:S(2)}) %collective-permute-start.23) | collective-permute-done | bytes 524320 | tf_op jit(solution)/shard_map/ppermute | solution.py:37
  72.7 2.8 %collective-permute-start.19 = (bf16[8,48,512]{2,1,0:T(8,128)(2,1)S(1)}, bf16[8,48,512]{2,1,0:T(8,128)(2,1)S(1)}, u32[]{:S(2)}, u32[]{:S(2)}) collective-permute-start(bf16[8,48,512]{2,1,0:T(8,128)(2,1)S(1)} %slice.159), channel_id=1, source_target_pairs={{0,96},{8,104},{16,112},{24,120},{1,97},{9,105},{17,113},{25,121},... | collective-permute-start | bytes 1179656 | tf_op jit(solution)/shard_map/ppermute | solution.py:37
  75.4 6.2 %collective-permute-done.19 = bf16[8,48,512]{2,1,0:T(8,128)(2,1)S(1)} collective-permute-done((bf16[8,48,512]{2,1,0:T(8,128)(2,1)S(1)}, bf16[8,48,512]{2,1,0:T(8,128)(2,1)S(1)}, u32[]{:S(2)}, u32[]{:S(2)}) %collective-permute-start.19) | collective-permute-done | bytes 393248 | tf_op jit(solution)/shard_map/ppermute | solution.py:37
  81.7 24.8 %experts.1 = (bf16[8,256,192]{2,1,0:T(8,128)(2,1)S(1)}, bf16[8,128,256]{2,1,0:T(8,128)(2,1)S(1)}, bf16[2,4,48,512]{3,2,1,0:T(8,128)(2,1)S(1)}, bf16[2,4,48,512]{...) custom-call(f32[8]{0:T(128)S(1)} %add_convert_fusion.5.ids_ref, ...), custom_call_target="tpu_custom_call" | custom-call | flops 20000000000 | bytes 50000000 | tf_op jit(solution)/shard_map/experts/pallas_call | solution.py:387
  108.3 2.8 %collective-permute-start.37 = (bf16[4,2,48,512]{3,2,1,0:T(8,128)(2,1)S(1)}, bf16[4,2,48,512]{3,2,1,0:T(8,128)(2,1)S(1)}, u32[]{:S(2)}, u32[]{:S(2)}) collective-permute-start(bf16[4,2,48,512]{3,2,1,0:T(8,128)(2,1)S(1)} %get-tuple-element.79), channel_id=1, source_target_pairs={{0,96},{8,104},{16,112},{24,120},{1,97},{9,105},{17,113},{25,121},... | collective-permute-start | bytes 1179656 | tf_op jit(solution)/shard_map/ppermute | solution.py:37
  112.1 9.0 %down.1 = (bf16[2,4,48,512]{3,2,1,0:T(8,128)(2,1)S(1)}, bf16[2,4,48,512]{3,2,1,0:T(8,128)(2,1)S(1)}, bf16[2,4,48,512]{3,2,1,0:T(8,128)(2,1)S(1)}, bf16[2,4,48,51...) custom-call(s32[8]{0:T(128)S(1)} %stack.35.cols_ref, ...), custom_call_target="tpu_custom_call" | custom-call | flops 6000000000 | bytes 12000000 | tf_op jit(solution)/shard_map/down/pallas_call | solution.py:413
  121.9 2.2 %collective-permute-start.26 = (bf16[2,4,48,512]{3,2,1,0:T(8,128)(2,1)S(1)}, bf16[2,4,48,512]{3,2,1,0:T(8,128)(2,1)S(1)}, u32[]{:S(2)}, u32[]{:S(2)}) collective-permute-start(bf16[2,4,48,512]{3,2,1,0:T(8,128)(2,1)S(1)} %get-tuple-element.71), channel_id=1, source_target_pairs={{0,16},{8,24},{16,0},{24,8},{1,17},{9,25},{17,1},{25,9},{2,18},{10... | collective-permute-start | bytes 1179656 | tf_op jit(solution)/shard_map/ppermute | solution.py:37
  125.5 5.6 %collective-permute-done.39 = bf16[4,2,48,512]{3,2,1,0:T(8,128)(2,1)S(1)} collective-permute-done((bf16[4,2,48,512]{3,2,1,0:T(8,128)(2,1)S(1)}, bf16[4,2,48,512]{3,2,1,0:T(8,128)(2,1)S(1)}, u32[]{:S(2)}, u32[]{:S(2)}) %collective-permute-start.39) | collective-permute-done | bytes 393248 | tf_op jit(solution)/shard_map/ppermute | solution.py:37
  133.4 2.2 %collective-permute-start.25 = (bf16[4,4,48,512]{3,2,1,0:T(8,128)(2,1)S(1)}, bf16[4,4,48,512]{3,2,1,0:T(8,128)(2,1)S(1)}, u32[]{:S(2)}, u32[]{:S(2)}) collective-permute-start(bf16[4,4,48,512]{3,2,1,0:T(8,128)(2,1)S(1)} %pad_maximum_fusion.2), channel_id=1, source_target_pairs={{0,16},{8,24},{16,0},{24,8},{1,17},{9,25},{17,1},{25,9},{2,18},{10... | collective-permute-start | bytes 2359304 | tf_op jit(solution)/shard_map/ppermute | solution.py:37
  135.8 5.8 %collective-permute-done.31 = bf16[4,4,32,512]{3,2,1,0:T(8,128)(2,1)S(1)} collective-permute-done((bf16[4,4,32,512]{3,2,1,0:T(8,128)(2,1)S(1)}, bf16[4,4,32,512]{3,2,1,0:T(8,128)(2,1)S(1)}, u32[]{:S(2)}, u32[]{:S(2)}) %collective-permute-start.31) | collective-permute-done | bytes 524320 | tf_op jit(solution)/shard_map/ppermute | solution.py:37
  142.1 3.8 %collective-permute-done.38 = bf16[8,2,48,512]{3,2,1,0:T(8,128)(2,1)S(1)} collective-permute-done((bf16[8,2,48,512]{3,2,1,0:T(8,128)(2,1)S(1)}, bf16[8,2,48,512]{3,2,1,0:T(8,128)(2,1)S(1)}, u32[]{:S(2)}, u32[]{:S(2)}) %collective-permute-start.38) | collective-permute-done | bytes 786464 | tf_op jit(solution)/shard_map/ppermute | solution.py:37
  148.5 7.8 %collective-permute-done.33 = bf16[2,4,32,512]{3,2,1,0:T(8,128)(2,1)S(1)} collective-permute-done((bf16[2,4,32,512]{3,2,1,0:T(8,128)(2,1)S(1)}, bf16[2,4,32,512]{3,2,1,0:T(8,128)(2,1)S(1)}, u32[]{:S(2)}, u32[]{:S(2)}) %collective-permute-start.33) | collective-permute-done | bytes 262176 | tf_op jit(solution)/shard_map/ppermute | solution.py:37
  156.3 1.9 collective-permute-start.34
  158.5 2.8 %collective-permute-done.34 = bf16[4,32,512]{2,1,0:T(8,128)(2,1)S(1)} collective-permute-done((bf16[4,32,512]{2,1,0:T(8,128)(2,1)S(1)}, bf16[4,32,512]{2,1,0:T(8,128)(2,1)S(1)}, u32[]{:S(2)}, u32[]{:S(2)}) %collective-permute-start.34) | collective-permute-done | bytes 131104 | tf_op jit(solution)/shard_map/ppermute | solution.py:37
  161.8 6.6 %collective-permute-done.28 = bf16[2,4,48,512]{3,2,1,0:T(8,128)(2,1)S(1)} collective-permute-done((bf16[2,4,48,512]{3,2,1,0:T(8,128)(2,1)S(1)}, bf16[2,4,48,512]{3,2,1,0:T(8,128)(2,1)S(1)}, u32[]{:S(2)}, u32[]{:S(2)}) %collective-permute-start.28) | collective-permute-done | bytes 393248 | tf_op jit(solution)/shard_map/ppermute | solution.py:37
  169.1 5.4 %collective-permute-done.29 = bf16[4,48,512]{2,1,0:T(8,128)(2,1)S(1)} collective-permute-done((bf16[4,48,512]{2,1,0:T(8,128)(2,1)S(1)}, bf16[4,48,512]{2,1,0:T(8,128)(2,1)S(1)}, u32[]{:S(2)}, u32[]{:S(2)}) %collective-permute-start.29) | collective-permute-done | bytes 196640 | tf_op jit(solution)/shard_map/ppermute | solution.py:37
  175.7 5.5 %collective-permute-done.35 = bf16[2,80,512]{2,1,0:T(8,128)(2,1)S(1)} collective-permute-done((bf16[2,80,512]{2,1,0:T(8,128)(2,1)S(1)}, bf16[2,80,512]{2,1,0:T(8,128)(2,1)S(1)}, u32[]{:S(2)}, u32[]{:S(2)}) %collective-permute-start.35) | collective-permute-done | bytes 163872 | tf_op jit(solution)/shard_map/ppermute | solution.py:37
  181.4 4.3 %collective-permute-done.36 = bf16[1,80,512]{2,1,0:T(8,128)(2,1)S(1)} collective-permute-done((bf16[1,80,512]{2,1,0:T(8,128)(2,1)S(1)}, bf16[1,80,512]{2,1,0:T(8,128)(2,1)S(1)}, u32[]{:S(2)}, u32[]{:S(2)}) %collective-permute-start.36) | collective-permute-done | bytes 81952 | tf_op jit(solution)/shard_map/ppermute | solution.py:37
  (126 shorter events, 33.4 us)
Async XLA Ops:
  0.0 17.2 %collective-permute-start.4 = (bf16[4,192,4096]{2,1,0:T(8,128)(2,1)}, bf16[4,192,4096]{2,1,0:T(8,128)(2,1)}, u32[]{:S(2)}, u32[]{:S(2)}) collective-permute-start(bf16[4,192,4096]{2,1,0:T(8,128)(2,1)} %wg.1), channel_id=1, source_target_pairs={{0,8},{8,0},{16,24},{24,16},{1,9},{9,1},{17,25},{25,17},{2,10},{10... | collective-permute-start | bytes 18874376 | tf_op jit(solution)/shard_map/ppermute | solution.py:42
  17.2 10.6 %collective-permute-start.8 = (bf16[4,192,4096]{2,1,0:T(8,128)(2,1)}, bf16[4,192,4096]{2,1,0:T(8,128)(2,1)}, u32[]{:S(2)}, u32[]{:S(2)}) collective-permute-start(bf16[4,192,4096]{2,1,0:T(8,128)(2,1)} %wu), channel_id=1, source_target_pairs={{0,8},{8,0},{16,24},{24,16},{1,9},{9,1},{17,25},{25,17},{2,10},{10... | collective-permute-start | bytes 18874376 | tf_op jit(solution)/shard_map/ppermute | solution.py:42
  18.1 8.5 %collective-permute-start.6 = (bf16[4,48,512]{2,1,0:T(8,128)(2,1)S(1)}, bf16[4,48,512]{2,1,0:T(8,128)(2,1)S(1)}, u32[]{:S(2)}, u32[]{:S(2)}) collective-permute-start(bf16[4,48,512]{2,1,0:T(8,128)(2,1)S(1)} %pad_maximum_fusion.12), channel_id=1, source_target_pairs={{0,17},{8,25},{16,1},{24,9},{1,16},{9,24},{17,0},{25,8},{2,19},{10... | collective-permute-start | bytes 589832 | tf_op jit(solution)/shard_map/ppermute | solution.py:37
  27.8 15.6 %collective-permute-start.12 = (bf16[4,192,4096]{2,1,0:T(8,128)(2,1)}, bf16[4,192,4096]{2,1,0:T(8,128)(2,1)S(1)}, u32[]{:S(2)}, u32[]{:S(2)}) collective-permute-start(bf16[4,192,4096]{2,1,0:T(8,128)(2,1)} %wd.1), channel_id=1, source_target_pairs={{0,8},{8,0},{16,24},{24,16},{1,9},{9,1},{17,25},{25,17},{2,10},{10... | collective-permute-start | bytes 18874376 | tf_op jit(solution)/shard_map/ppermute | solution.py:42
  27.9 12.6 %collective-permute-start.9 = (bf16[8,48,512]{2,1,0:T(8,128)(2,1)S(1)}, bf16[8,48,512]{2,1,0:T(8,128)(2,1)S(1)}, u32[]{:S(2)}, u32[]{:S(2)}) collective-permute-start(bf16[8,48,512]{2,1,0:T(8,128)(2,1)S(1)} %pad_maximum_fusion.9), channel_id=1, source_target_pairs={{0,6},{8,14},{16,22},{24,30},{1,7},{9,15},{17,23},{25,31},{2,4},{1... | collective-permute-start | bytes 1179656 | tf_op jit(solution)/shard_map/ppermute | solution.py:37
  30.1 8.5 %collective-permute-start.11 = (bf16[8,32,512]{2,1,0:T(8,128)(2,1)S(1)}, bf16[8,32,512]{2,1,0:T(8,128)(2,1)S(1)}, u32[]{:S(2)}, u32[]{:S(2)}) collective-permute-start(bf16[8,32,512]{2,1,0:T(8,128)(2,1)S(1)} %fusion.3), channel_id=1, source_target_pairs={{0,17},{8,25},{16,1},{24,9},{1,16},{9,24},{17,0},{25,8},{2,19},{10... | collective-permute-start | bytes 786440 | tf_op jit(solution)/shard_map/ppermute | solution.py:37
  32.1 11.3 %collective-permute-start.10 = (bf16[8,48,512]{2,1,0:T(8,128)(2,1)S(1)}, bf16[8,48,512]{2,1,0:T(8,128)(2,1)S(1)}, u32[]{:S(2)}, u32[]{:S(2)}) collective-permute-start(bf16[8,48,512]{2,1,0:T(8,128)(2,1)S(1)} %pad_maximum_fusion.10), channel_id=1, source_target_pairs={{0,16},{8,24},{16,0},{24,8},{1,17},{9,25},{17,1},{25,9},{2,18},{10... | collective-permute-start | bytes 1179656 | tf_op jit(solution)/shard_map/ppermute | solution.py:37
  43.5 13.1 %collective-permute-start.21 = (bf16[16,32,512]{2,1,0:T(8,128)(2,1)S(1)}, bf16[16,32,512]{2,1,0:T(8,128)(2,1)S(1)}, u32[]{:S(2)}, u32[]{:S(2)}) collective-permute-start(bf16[16,32,512]{2,1,0:T(8,128)(2,1)S(1)} %pad_maximum_fusion.6), channel_id=1, source_target_pairs={{0,2},{8,10},{16,18},{24,26},{1,3},{9,11},{17,19},{25,27},{2,0},{1... | collective-permute-start | bytes 1572872 | tf_op jit(solution)/shard_map/ppermute | solution.py:37
  44.2 18.4 %collective-permute-start.13 = (bf16[16,48,512]{2,1,0:T(8,128)(2,1)S(1)}, bf16[16,48,512]{2,1,0:T(8,128)(2,1)S(1)}, u32[]{:S(2)}, u32[]{:S(2)}) collective-permute-start(bf16[16,48,512]{2,1,0:T(8,128)(2,1)S(1)} %pad_maximum_fusion), channel_id=1, source_target_pairs={{0,16},{8,24},{16,0},{24,8},{1,17},{9,25},{17,1},{25,9},{2,18},{10... | collective-permute-start | bytes 2359304 | tf_op jit(solution)/shard_map/ppermute | solution.py:37
  46.0 17.9 %collective-permute-start.14 = (bf16[16,48,512]{2,1,0:T(8,128)(2,1)S(1)}, bf16[16,48,512]{2,1,0:T(8,128)(2,1)S(1)}, u32[]{:S(2)}, u32[]{:S(2)}) collective-permute-start(bf16[16,48,512]{2,1,0:T(8,128)(2,1)S(1)} %pad_maximum_fusion), channel_id=1, source_target_pairs={{0,17},{8,25},{16,1},{24,9},{1,16},{9,24},{17,0},{25,8},{2,19},{10... | collective-permute-start | bytes 2359304 | tf_op jit(solution)/shard_map/ppermute | solution.py:37
  46.0 19.8 %collective-permute-start.18 = (bf16[16,48,512]{2,1,0:T(8,128)(2,1)S(1)}, bf16[16,48,512]{2,1,0:T(8,128)(2,1)S(1)}, u32[]{:S(2)}, u32[]{:S(2)}) collective-permute-start(bf16[16,48,512]{2,1,0:T(8,128)(2,1)S(1)} %pad_maximum_fusion.1), channel_id=1, source_target_pairs={{0,96},{8,104},{16,112},{24,120},{1,97},{9,105},{17,113},{25,121},... | collective-permute-start | bytes 2359304 | tf_op jit(solution)/shard_map/ppermute | solution.py:37
  48.7 18.0 %collective-permute-start.17 = (bf16[16,48,512]{2,1,0:T(8,128)(2,1)S(1)}, bf16[16,48,512]{2,1,0:T(8,128)(2,1)S(1)}, u32[]{:S(2)}, u32[]{:S(2)}) collective-permute-start(bf16[16,48,512]{2,1,0:T(8,128)(2,1)S(1)} %pad_maximum_fusion.1), channel_id=1, source_target_pairs={{0,32},{8,40},{16,48},{24,56},{1,33},{9,41},{17,49},{25,57},{2,34}... | collective-permute-start | bytes 2359304 | tf_op jit(solution)/shard_map/ppermute | solution.py:37
  56.6 16.1 %collective-permute-start.23 = (bf16[16,32,512]{2,1,0:T(8,128)(2,1)S(1)}, bf16[16,32,512]{2,1,0:T(8,128)(2,1)S(1)}, u32[]{:S(2)}, u32[]{:S(2)}) collective-permute-start(bf16[16,32,512]{2,1,0:T(8,128)(2,1)S(1)} %collective-permute-done.21), channel_id=1, source_target_pairs={{0,6},{8,14},{16,22},{24,30},{1,7},{9,15},{17,23},{25,31},{2,4},{1... | collective-permute-start | bytes 1572872 | tf_op jit(solution)/shard_map/ppermute | solution.py:37
  62.6 19.0 %collective-permute-start.22 = (bf16[16,32,512]{2,1,0:T(8,128)(2,1)S(1)}, bf16[16,32,512]{2,1,0:T(8,128)(2,1)S(1)}, u32[]{:S(2)}, u32[]{:S(2)}) collective-permute-start(bf16[16,32,512]{2,1,0:T(8,128)(2,1)S(1)} %pad_maximum_fusion.6), channel_id=1, source_target_pairs={{0,6},{8,14},{16,22},{24,30},{1,7},{9,15},{17,23},{25,31},{2,4},{1... | collective-permute-start | bytes 1572872 | tf_op jit(solution)/shard_map/ppermute | solution.py:37
  63.9 11.6 %collective-permute-start.16 = (bf16[8,48,512]{2,1,0:T(8,128)(2,1)S(1)}, bf16[8,48,512]{2,1,0:T(8,128)(2,1)S(1)}, u32[]{:S(2)}, u32[]{:S(2)}) collective-permute-start(bf16[8,48,512]{2,1,0:T(8,128)(2,1)S(1)} %slice.158), channel_id=1, source_target_pairs={{0,16},{8,24},{16,0},{24,8},{1,17},{9,25},{17,1},{25,9},{2,18},{10... | collective-permute-start | bytes 1179656 | tf_op jit(solution)/shard_map/ppermute | solution.py:37
  65.7 9.7 %collective-permute-start.15 = (bf16[8,48,512]{2,1,0:T(8,128)(2,1)S(1)}, bf16[8,48,512]{2,1,0:T(8,128)(2,1)S(1)}, u32[]{:S(2)}, u32[]{:S(2)}) collective-permute-start(bf16[8,48,512]{2,1,0:T(8,128)(2,1)S(1)} %slice.124), channel_id=1, source_target_pairs={{0,17},{8,25},{16,1},{24,9},{1,16},{9,24},{17,0},{25,8},{2,19},{10... | collective-permute-start | bytes 1179656 | tf_op jit(solution)/shard_map/ppermute | solution.py:37
  66.8 8.7 %collective-permute-start.20 = (bf16[8,48,512]{2,1,0:T(8,128)(2,1)S(1)}, bf16[8,48,512]{2,1,0:T(8,128)(2,1)S(1)}, u32[]{:S(2)}, u32[]{:S(2)}) collective-permute-start(bf16[8,48,512]{2,1,0:T(8,128)(2,1)S(1)} %slice.160), channel_id=1, source_target_pairs={{0,32},{8,40},{16,48},{24,56},{1,33},{9,41},{17,49},{25,57},{2,34}... | collective-permute-start | bytes 1179656 | tf_op jit(solution)/shard_map/ppermute | solution.py:37
  72.7 9.0 %collective-permute-start.19 = (bf16[8,48,512]{2,1,0:T(8,128)(2,1)S(1)}, bf16[8,48,512]{2,1,0:T(8,128)(2,1)S(1)}, u32[]{:S(2)}, u32[]{:S(2)}) collective-permute-start(bf16[8,48,512]{2,1,0:T(8,128)(2,1)S(1)} %slice.159), channel_id=1, source_target_pairs={{0,96},{8,104},{16,112},{24,120},{1,97},{9,105},{17,113},{25,121},... | collective-permute-start | bytes 1179656 | tf_op jit(solution)/shard_map/ppermute | solution.py:37
  108.3 15.8 %collective-permute-start.37 = (bf16[4,2,48,512]{3,2,1,0:T(8,128)(2,1)S(1)}, bf16[4,2,48,512]{3,2,1,0:T(8,128)(2,1)S(1)}, u32[]{:S(2)}, u32[]{:S(2)}) collective-permute-start(bf16[4,2,48,512]{3,2,1,0:T(8,128)(2,1)S(1)} %get-tuple-element.79), channel_id=1, source_target_pairs={{0,96},{8,104},{16,112},{24,120},{1,97},{9,105},{17,113},{25,121},... | collective-permute-start | bytes 1179656 | tf_op jit(solution)/shard_map/ppermute | solution.py:37
  111.1 20.1 %collective-permute-start.30 = (bf16[4,4,32,512]{3,2,1,0:T(8,128)(2,1)S(1)}, bf16[4,4,32,512]{3,2,1,0:T(8,128)(2,1)S(1)}, u32[]{:S(2)}, u32[]{:S(2)}) collective-permute-start(bf16[4,4,32,512]{3,2,1,0:T(8,128)(2,1)S(1)} %get-tuple-element.75), channel_id=1, source_target_pairs={{0,6},{8,14},{16,22},{24,30},{1,7},{9,15},{17,23},{25,31},{2,4},{1... | collective-permute-start | bytes 1572872 | tf_op jit(solution)/shard_map/ppermute | solution.py:37
  121.1 10.0 %collective-permute-start.39 = (bf16[4,2,48,512]{3,2,1,0:T(8,128)(2,1)S(1)}, bf16[4,2,48,512]{3,2,1,0:T(8,128)(2,1)S(1)}, u32[]{:S(2)}, u32[]{:S(2)}) collective-permute-start(bf16[4,2,48,512]{3,2,1,0:T(8,128)(2,1)S(1)} %get-tuple-element.83), channel_id=1, source_target_pairs={{0,32},{8,40},{16,48},{24,56},{1,33},{9,41},{17,49},{25,57},{2,34}... | collective-permute-start | bytes 1179656 | tf_op jit(solution)/shard_map/ppermute | solution.py:37
  121.2 11.4 %collective-permute-start.24 = (bf16[2,4,48,512]{3,2,1,0:T(8,128)(2,1)S(1)}, bf16[2,4,48,512]{3,2,1,0:T(8,128)(2,1)S(1)}, u32[]{:S(2)}, u32[]{:S(2)}) collective-permute-start(bf16[2,4,48,512]{3,2,1,0:T(8,128)(2,1)S(1)} %get-tuple-element.67), channel_id=1, source_target_pairs={{0,17},{8,25},{16,1},{24,9},{1,16},{9,24},{17,0},{25,8},{2,19},{10... | collective-permute-start | bytes 1179656 | tf_op jit(solution)/shard_map/ppermute | solution.py:37
  121.9 11.4 %collective-permute-start.26 = (bf16[2,4,48,512]{3,2,1,0:T(8,128)(2,1)S(1)}, bf16[2,4,48,512]{3,2,1,0:T(8,128)(2,1)S(1)}, u32[]{:S(2)}, u32[]{:S(2)}) collective-permute-start(bf16[2,4,48,512]{3,2,1,0:T(8,128)(2,1)S(1)} %get-tuple-element.71), channel_id=1, source_target_pairs={{0,16},{8,24},{16,0},{24,8},{1,17},{9,25},{17,1},{25,9},{2,18},{10... | collective-permute-start | bytes 1179656 | tf_op jit(solution)/shard_map/ppermute | solution.py:37
  124.2 11.6 %collective-permute-start.32 = (bf16[4,4,32,512]{3,2,1,0:T(8,128)(2,1)S(1)}, bf16[4,4,32,512]{3,2,1,0:T(8,128)(2,1)S(1)}, u32[]{:S(2)}, u32[]{:S(2)}) collective-permute-start(bf16[4,4,32,512]{3,2,1,0:T(8,128)(2,1)S(1)} %get-tuple-element.76), channel_id=1, source_target_pairs={{0,6},{8,14},{16,22},{24,30},{1,7},{9,15},{17,23},{25,31},{2,4},{1... | collective-permute-start | bytes 1572872 | tf_op jit(solution)/shard_map/ppermute | solution.py:37
  131.1 14.7 %collective-permute-start.38 = (bf16[8,2,48,512]{3,2,1,0:T(8,128)(2,1)S(1)}, bf16[8,2,48,512]{3,2,1,0:T(8,128)(2,1)S(1)}, u32[]{:S(2)}, u32[]{:S(2)}) collective-permute-start(bf16[8,2,48,512]{3,2,1,0:T(8,128)(2,1)S(1)} %pad_maximum_fusion.4), channel_id=1, source_target_pairs={{0,32},{8,40},{16,48},{24,56},{1,33},{9,41},{17,49},{25,57},{2,34}... | collective-permute-start | bytes 2359304 | tf_op jit(solution)/shard_map/ppermute | solution.py:37
  132.4 9.3 %collective-permute-start.31 = (bf16[4,4,32,512]{3,2,1,0:T(8,128)(2,1)S(1)}, bf16[4,4,32,512]{3,2,1,0:T(8,128)(2,1)S(1)}, u32[]{:S(2)}, u32[]{:S(2)}) collective-permute-start(bf16[4,4,32,512]{3,2,1,0:T(8,128)(2,1)S(1)} %add.139), channel_id=1, source_target_pairs={{0,2},{8,10},{16,18},{24,26},{1,3},{9,11},{17,19},{25,27},{2,0},{1... | collective-permute-start | bytes 1572872 | tf_op jit(solution)/shard_map/ppermute | solution.py:37
  132.6 14.0 %collective-permute-start.40 = (bf16[8,2,48,512]{3,2,1,0:T(8,128)(2,1)S(1)}, bf16[8,2,48,512]{3,2,1,0:T(8,128)(2,1)S(1)}, u32[]{:S(2)}, u32[]{:S(2)}) collective-permute-start(bf16[8,2,48,512]{3,2,1,0:T(8,128)(2,1)S(1)} %pad_maximum_fusion.5), channel_id=1, source_target_pairs={{0,96},{8,104},{16,112},{24,120},{1,97},{9,105},{17,113},{25,121},... | collective-permute-start | bytes 2359304 | tf_op jit(solution)/shard_map/ppermute | solution.py:37
  133.4 24.8 %collective-permute-start.25 = (bf16[4,4,48,512]{3,2,1,0:T(8,128)(2,1)S(1)}, bf16[4,4,48,512]{3,2,1,0:T(8,128)(2,1)S(1)}, u32[]{:S(2)}, u32[]{:S(2)}) collective-permute-start(bf16[4,4,48,512]{3,2,1,0:T(8,128)(2,1)S(1)} %pad_maximum_fusion.2), channel_id=1, source_target_pairs={{0,16},{8,24},{16,0},{24,8},{1,17},{9,25},{17,1},{25,9},{2,18},{10... | collective-permute-start | bytes 2359304 | tf_op jit(solution)/shard_map/ppermute | solution.py:37
  135.7 22.4 %collective-permute-start.27 = (bf16[4,4,48,512]{3,2,1,0:T(8,128)(2,1)S(1)}, bf16[4,4,48,512]{3,2,1,0:T(8,128)(2,1)S(1)}, u32[]{:S(2)}, u32[]{:S(2)}) collective-permute-start(bf16[4,4,48,512]{3,2,1,0:T(8,128)(2,1)S(1)} %pad_maximum_fusion.3), channel_id=1, source_target_pairs={{0,17},{8,25},{16,1},{24,9},{1,16},{9,24},{17,0},{25,8},{2,19},{10... | collective-permute-start | bytes 2359304 | tf_op jit(solution)/shard_map/ppermute | solution.py:37
  142.0 14.3 %collective-permute-start.33 = (bf16[2,4,32,512]{3,2,1,0:T(8,128)(2,1)S(1)}, bf16[2,4,32,512]{3,2,1,0:T(8,128)(2,1)S(1)}, u32[]{:S(2)}, u32[]{:S(2)}) collective-permute-start(bf16[2,4,32,512]{3,2,1,0:T(8,128)(2,1)S(1)} %slice.168), channel_id=1, source_target_pairs={{0,17},{8,25},{16,1},{24,9},{1,16},{9,24},{17,0},{25,8},{2,19},{10... | collective-permute-start | bytes 786440 | tf_op jit(solution)/shard_map/ppermute | solution.py:37
  147.0 14.4 %collective-permute-start.41 = (bf16[2,4,48,512]{3,2,1,0:T(8,128)(2,1)S(1)}, bf16[2,4,48,512]{3,2,1,0:T(8,128)(2,1)S(1)}, u32[]{:S(2)}, u32[]{:S(2)}) collective-permute-start(bf16[2,4,48,512]{3,2,1,0:T(8,128)(2,1)S(1)} %pad_maximum_fusion.7), channel_id=1, source_target_pairs={{0,16},{8,24},{16,0},{24,8},{1,17},{9,25},{17,1},{25,9},{2,18},{10... | collective-permute-start | bytes 1179656 | tf_op jit(solution)/shard_map/ppermute | solution.py:37
  158.3 10.1 %collective-permute-start.28 = (bf16[2,4,48,512]{3,2,1,0:T(8,128)(2,1)S(1)}, bf16[2,4,48,512]{3,2,1,0:T(8,128)(2,1)S(1)}, u32[]{:S(2)}, u32[]{:S(2)}) collective-permute-start(bf16[2,4,48,512]{3,2,1,0:T(8,128)(2,1)S(1)} %add_convert_fusion.3), channel_id=1, source_target_pairs={{0,6},{8,14},{16,22},{24,30},{1,7},{9,15},{17,23},{25,31},{2,4},{1... | collective-permute-start | bytes 1179656 | tf_op jit(solution)/shard_map/ppermute | solution.py:37
  (16 other events, 120.5 us)

commit v6 on v5

--- a/solution.py
+++ b/solution.py
@@ -51,9 +51,9 @@
     one_c = swap(c, LAST[2], 1)
     one_a, one_b = swap(a, LAST[0], 1), swap(b, LAST[1], 1)
     three_a, three_b = swap(a, LAST[0], 3), swap(b, LAST[1], 3)
+    c, one_c = lax.optimization_barrier((c, one_c))
+    three_c = swap(c, LAST[2], 3)
     two_c = swap(one_c, LAST[2], 3)
-    c, one_a = lax.optimization_barrier((c, one_a))
-    three_c = swap(c, LAST[2], 3)
     two_a = swap(one_a[:8], LAST[0], 3), swap(three_a[8:], LAST[0], 1)
     two_b = swap(one_b[:8], LAST[1], 3), swap(three_b[8:], LAST[1], 1)
     return [a, one_a, three_a, *two_a, b, one_b, three_b, *two_b, c, one_c, three_c, two_c]

time: 187 us -> 187 us (level)
  transfers between devices with their start and end apart: 45 -> 45, of which waited for: 23 -> 25; matrix products, arithmetic and copies ran while one was open for 4% -> 4% of each run, Pallas kernels for 5% -> 5%
where the time goes in v6:
time: 187 us
  waiting for transfers between devices  93.6 us (50%)
  starting transfers between devices  49.3 us (26%)
  Pallas kernels  33.8 us (18%)
  other arithmetic  5.73 us (3%)
  local copies, waits for them, and re-layouts  3.71 us (2%)
    ppermute x42, waiting for transfers between devices, swap(): return lax.ppermute(value, AXES, pairs)  92.4 us
    ppermute x42, starting transfers between devices, swap(): return lax.ppermute(value, AXES, pairs)  49.1 us
    pallas_call x1, Pallas kernels, local(): pl.pallas_call(functools.partial(expert_kernel, (2, 3)), out_shape=[jax.S...  24.8 us
    pallas_call x1, Pallas kernels, local(): pl.pallas_call(functools.partial(down_kernel, (0, 1)), out_shape=shapes,...  8.96 us
  transfers between devices with their start and end apart: 45, of which 25 were waited for; matrix products, arithmetic and copies ran while one was open for 4% of the time, Pallas kernels for 5%

profile of v6, /device:TPU:32, one launch (start us, length us, event | category | flops | bytes accessed | tf_op | source)
XLA Modules:
  0.0 186.6 jit_solution(9850151941179460683)
XLA Ops:
  6.2 2.3 %collective-permute-start.3 = (bf16[2,48,512]{2,1,0:T(8,128)(2,1)S(1)}, bf16[2,48,512]{2,1,0:T(8,128)(2,1)S(1)}, u32[]{:S(2)}, u32[]{:S(2)}) collective-permute-start(bf16[2,48,512]{2,1,0:T(8,128)(2,1)S(1)} %pad_maximum_fusion.16), channel_id=1, source_target_pairs={{0,6},{8,14},{16,22},{24,30},{1,7},{9,15},{17,23},{25,31},{2,4},{1... | collective-permute-start | bytes 294920 | tf_op jit(solution)/shard_map/ppermute | solution.py:37
  9.7 2.8 %collective-permute-start.1 = (bf16[2,96,512]{2,1,0:T(8,128)(2,1)S(1)}, bf16[2,96,512]{2,1,0:T(8,128)(2,1)S(1)}, u32[]{:S(2)}, u32[]{:S(2)}) collective-permute-start(bf16[2,96,512]{2,1,0:T(8,128)(2,1)S(1)} %pad_maximum_fusion.11), channel_id=1, source_target_pairs={{0,96},{8,104},{16,112},{24,120},{1,97},{9,105},{17,113},{25,121},... | collective-permute-start | bytes 589832 | tf_op jit(solution)/shard_map/ppermute | solution.py:37
  12.5 4.6 %collective-permute-done.1 = bf16[2,96,512]{2,1,0:T(8,128)(2,1)S(1)} collective-permute-done((bf16[2,96,512]{2,1,0:T(8,128)(2,1)S(1)}, bf16[2,96,512]{2,1,0:T(8,128)(2,1)S(1)}, u32[]{:S(2)}, u32[]{:S(2)}) %collective-permute-start.1) | collective-permute-done | bytes 196640 | tf_op jit(solution)/shard_map/ppermute | solution.py:37
  18.1 3.5 %collective-permute-start.6 = (bf16[4,48,512]{2,1,0:T(8,128)(2,1)S(1)}, bf16[4,48,512]{2,1,0:T(8,128)(2,1)S(1)}, u32[]{:S(2)}, u32[]{:S(2)}) collective-permute-start(bf16[4,48,512]{2,1,0:T(8,128)(2,1)S(1)} %pad_maximum_fusion.12), channel_id=1, source_target_pairs={{0,17},{8,25},{16,1},{24,9},{1,16},{9,24},{17,0},{25,8},{2,19},{10... | collective-permute-start | bytes 589832 | tf_op jit(solution)/shard_map/ppermute | solution.py:37
  21.6 3.2 %collective-permute-done.7 = bf16[4,48,512]{2,1,0:T(8,128)(2,1)S(1)} collective-permute-done((bf16[4,48,512]{2,1,0:T(8,128)(2,1)S(1)}, bf16[4,48,512]{2,1,0:T(8,128)(2,1)S(1)}, u32[]{:S(2)}, u32[]{:S(2)}) %collective-permute-start.7) | collective-permute-done | bytes 196640 | tf_op jit(solution)/shard_map/ppermute | solution.py:37
  27.9 2.2 %collective-permute-start.9 = (bf16[8,48,512]{2,1,0:T(8,128)(2,1)S(1)}, bf16[8,48,512]{2,1,0:T(8,128)(2,1)S(1)}, u32[]{:S(2)}, u32[]{:S(2)}) collective-permute-start(bf16[8,48,512]{2,1,0:T(8,128)(2,1)S(1)} %pad_maximum_fusion.9), channel_id=1, source_target_pairs={{0,6},{8,14},{16,22},{24,30},{1,7},{9,15},{17,23},{25,31},{2,4},{1... | collective-permute-start | bytes 1179656 | tf_op jit(solution)/shard_map/ppermute | solution.py:37
  30.1 1.9 %collective-permute-start.11 = (bf16[8,32,512]{2,1,0:T(8,128)(2,1)S(1)}, bf16[8,32,512]{2,1,0:T(8,128)(2,1)S(1)}, u32[]{:S(2)}, u32[]{:S(2)}) collective-permute-start(bf16[8,32,512]{2,1,0:T(8,128)(2,1)S(1)} %fusion.3), channel_id=1, source_target_pairs={{0,17},{8,25},{16,1},{24,9},{1,16},{9,24},{17,0},{25,8},{2,19},{10... | collective-permute-start | bytes 786440 | tf_op jit(solution)/shard_map/ppermute | solution.py:37
  32.1 2.2 %collective-permute-start.10 = (bf16[8,48,512]{2,1,0:T(8,128)(2,1)S(1)}, bf16[8,48,512]{2,1,0:T(8,128)(2,1)S(1)}, u32[]{:S(2)}, u32[]{:S(2)}) collective-permute-start(bf16[8,48,512]{2,1,0:T(8,128)(2,1)S(1)} %pad_maximum_fusion.10), channel_id=1, source_target_pairs={{0,16},{8,24},{16,0},{24,8},{1,17},{9,25},{17,1},{25,9},{2,18},{10... | collective-permute-start | bytes 1179656 | tf_op jit(solution)/shard_map/ppermute | solution.py:37
  34.3 4.3 %collective-permute-done.11 = bf16[8,32,512]{2,1,0:T(8,128)(2,1)S(1)} collective-permute-done((bf16[8,32,512]{2,1,0:T(8,128)(2,1)S(1)}, bf16[8,32,512]{2,1,0:T(8,128)(2,1)S(1)}, u32[]{:S(2)}, u32[]{:S(2)}) %collective-permute-start.11) | collective-permute-done | bytes 262176 | tf_op jit(solution)/shard_map/ppermute | solution.py:37
  40.6 2.7 %collective-permute-done.10 = bf16[8,48,512]{2,1,0:T(8,128)(2,1)S(1)} collective-permute-done((bf16[8,48,512]{2,1,0:T(8,128)(2,1)S(1)}, bf16[8,48,512]{2,1,0:T(8,128)(2,1)S(1)}, u32[]{:S(2)}, u32[]{:S(2)}) %collective-permute-start.10) | collective-permute-done | bytes 393248 | tf_op jit(solution)/shard_map/ppermute | solution.py:37
  44.2 2.0 %collective-permute-start.13 = (bf16[16,48,512]{2,1,0:T(8,128)(2,1)S(1)}, bf16[16,48,512]{2,1,0:T(8,128)(2,1)S(1)}, u32[]{:S(2)}, u32[]{:S(2)}) collective-permute-start(bf16[16,48,512]{2,1,0:T(8,128)(2,1)S(1)} %pad_maximum_fusion), channel_id=1, source_target_pairs={{0,16},{8,24},{16,0},{24,8},{1,17},{9,25},{17,1},{25,9},{2,18},{10... | collective-permute-start | bytes 2359304 | tf_op jit(solution)/shard_map/ppermute | solution.py:37
  46.2 2.8 %collective-permute-start.18 = (bf16[16,48,512]{2,1,0:T(8,128)(2,1)S(1)}, bf16[16,48,512]{2,1,0:T(8,128)(2,1)S(1)}, u32[]{:S(2)}, u32[]{:S(2)}) collective-permute-start(bf16[16,48,512]{2,1,0:T(8,128)(2,1)S(1)} %pad_maximum_fusion.1), channel_id=1, source_target_pairs={{0,96},{8,104},{16,112},{24,120},{1,97},{9,105},{17,113},{25,121},... | collective-permute-start | bytes 2359304 | tf_op jit(solution)/shard_map/ppermute | solution.py:37
  49.0 7.6 %collective-permute-done.21 = bf16[16,32,512]{2,1,0:T(8,128)(2,1)S(1)} collective-permute-done((bf16[16,32,512]{2,1,0:T(8,128)(2,1)S(1)}, bf16[16,32,512]{2,1,0:T(8,128)(2,1)S(1)}, u32[]{:S(2)}, u32[]{:S(2)}) %collective-permute-start.21) | collective-permute-done | bytes 524320 | tf_op jit(solution)/shard_map/ppermute | solution.py:37
  57.7 5.0 %collective-permute-done.14 = bf16[16,48,512]{2,1,0:T(8,128)(2,1)S(1)} collective-permute-done((bf16[16,48,512]{2,1,0:T(8,128)(2,1)S(1)}, bf16[16,48,512]{2,1,0:T(8,128)(2,1)S(1)}, u32[]{:S(2)}, u32[]{:S(2)}) %collective-permute-start.14) | collective-permute-done | bytes 786464 | tf_op jit(solution)/shard_map/ppermute | solution.py:37
  63.9 2.7 %collective-permute-start.16 = (bf16[8,48,512]{2,1,0:T(8,128)(2,1)S(1)}, bf16[8,48,512]{2,1,0:T(8,128)(2,1)S(1)}, u32[]{:S(2)}, u32[]{:S(2)}) collective-permute-start(bf16[8,48,512]{2,1,0:T(8,128)(2,1)S(1)} %slice.159), channel_id=1, source_target_pairs={{0,16},{8,24},{16,0},{24,8},{1,17},{9,25},{17,1},{25,9},{2,18},{10... | collective-permute-start | bytes 1179656 | tf_op jit(solution)/shard_map/ppermute | solution.py:37
  67.5 5.2 %collective-permute-done.22 = bf16[16,32,512]{2,1,0:T(8,128)(2,1)S(1)} collective-permute-done((bf16[16,32,512]{2,1,0:T(8,128)(2,1)S(1)}, bf16[16,32,512]{2,1,0:T(8,128)(2,1)S(1)}, u32[]{:S(2)}, u32[]{:S(2)}) %collective-permute-start.22) | collective-permute-done | bytes 524320 | tf_op jit(solution)/shard_map/ppermute | solution.py:37
  72.7 2.8 %collective-permute-start.19 = (bf16[8,48,512]{2,1,0:T(8,128)(2,1)S(1)}, bf16[8,48,512]{2,1,0:T(8,128)(2,1)S(1)}, u32[]{:S(2)}, u32[]{:S(2)}) collective-permute-start(bf16[8,48,512]{2,1,0:T(8,128)(2,1)S(1)} %slice.160), channel_id=1, source_target_pairs={{0,96},{8,104},{16,112},{24,120},{1,97},{9,105},{17,113},{25,121},... | collective-permute-start | bytes 1179656 | tf_op jit(solution)/shard_map/ppermute | solution.py:37
  75.4 5.8 %collective-permute-done.23 = bf16[16,32,512]{2,1,0:T(8,128)(2,1)S(1)} collective-permute-done((bf16[16,32,512]{2,1,0:T(8,128)(2,1)S(1)}, bf16[16,32,512]{2,1,0:T(8,128)(2,1)S(1)}, u32[]{:S(2)}, u32[]{:S(2)}) %collective-permute-start.23) | collective-permute-done | bytes 524320 | tf_op jit(solution)/shard_map/ppermute | solution.py:37
  81.7 24.8 %experts.1 = (bf16[8,256,192]{2,1,0:T(8,128)(2,1)S(1)}, bf16[8,128,256]{2,1,0:T(8,128)(2,1)S(1)}, bf16[2,4,48,512]{3,2,1,0:T(8,128)(2,1)S(1)}, bf16[2,4,48,512]{...) custom-call(f32[8]{0:T(128)S(1)} %add_convert_fusion.5.ids_ref, ...), custom_call_target="tpu_custom_call" | custom-call | flops 20000000000 | bytes 50000000 | tf_op jit(solution)/shard_map/experts/pallas_call | solution.py:387
  108.3 2.8 %collective-permute-start.37 = (bf16[4,2,48,512]{3,2,1,0:T(8,128)(2,1)S(1)}, bf16[4,2,48,512]{3,2,1,0:T(8,128)(2,1)S(1)}, u32[]{:S(2)}, u32[]{:S(2)}) collective-permute-start(bf16[4,2,48,512]{3,2,1,0:T(8,128)(2,1)S(1)} %get-tuple-element.79), channel_id=1, source_target_pairs={{0,96},{8,104},{16,112},{24,120},{1,97},{9,105},{17,113},{25,121},... | collective-permute-start | bytes 1179656 | tf_op jit(solution)/shard_map/ppermute | solution.py:37
  112.1 9.0 %down.1 = (bf16[2,4,48,512]{3,2,1,0:T(8,128)(2,1)S(1)}, bf16[2,4,48,512]{3,2,1,0:T(8,128)(2,1)S(1)}, bf16[2,4,48,512]{3,2,1,0:T(8,128)(2,1)S(1)}, bf16[2,4,48,51...) custom-call(s32[8]{0:T(128)S(1)} %stack.35.cols_ref, ...), custom_call_target="tpu_custom_call" | custom-call | flops 6000000000 | bytes 12000000 | tf_op jit(solution)/shard_map/down/pallas_call | solution.py:413
  121.9 2.2 %collective-permute-start.26 = (bf16[2,4,48,512]{3,2,1,0:T(8,128)(2,1)S(1)}, bf16[2,4,48,512]{3,2,1,0:T(8,128)(2,1)S(1)}, u32[]{:S(2)}, u32[]{:S(2)}) collective-permute-start(bf16[2,4,48,512]{3,2,1,0:T(8,128)(2,1)S(1)} %get-tuple-element.71), channel_id=1, source_target_pairs={{0,16},{8,24},{16,0},{24,8},{1,17},{9,25},{17,1},{25,9},{2,18},{10... | collective-permute-start | bytes 1179656 | tf_op jit(solution)/shard_map/ppermute | solution.py:37
  125.5 5.5 %collective-permute-done.39 = bf16[4,2,48,512]{3,2,1,0:T(8,128)(2,1)S(1)} collective-permute-done((bf16[4,2,48,512]{3,2,1,0:T(8,128)(2,1)S(1)}, bf16[4,2,48,512]{3,2,1,0:T(8,128)(2,1)S(1)}, u32[]{:S(2)}, u32[]{:S(2)}) %collective-permute-start.39) | collective-permute-done | bytes 393248 | tf_op jit(solution)/shard_map/ppermute | solution.py:37
  133.3 2.2 %collective-permute-start.25 = (bf16[4,4,48,512]{3,2,1,0:T(8,128)(2,1)S(1)}, bf16[4,4,48,512]{3,2,1,0:T(8,128)(2,1)S(1)}, u32[]{:S(2)}, u32[]{:S(2)}) collective-permute-start(bf16[4,4,48,512]{3,2,1,0:T(8,128)(2,1)S(1)} %pad_maximum_fusion.2), channel_id=1, source_target_pairs={{0,16},{8,24},{16,0},{24,8},{1,17},{9,25},{17,1},{25,9},{2,18},{10... | collective-permute-start | bytes 2359304 | tf_op jit(solution)/shard_map/ppermute | solution.py:37
  135.8 5.8 %collective-permute-done.31 = bf16[4,4,32,512]{3,2,1,0:T(8,128)(2,1)S(1)} collective-permute-done((bf16[4,4,32,512]{3,2,1,0:T(8,128)(2,1)S(1)}, bf16[4,4,32,512]{3,2,1,0:T(8,128)(2,1)S(1)}, u32[]{:S(2)}, u32[]{:S(2)}) %collective-permute-start.31) | collective-permute-done | bytes 524320 | tf_op jit(solution)/shard_map/ppermute | solution.py:37
  142.1 3.7 %collective-permute-done.38 = bf16[8,2,48,512]{3,2,1,0:T(8,128)(2,1)S(1)} collective-permute-done((bf16[8,2,48,512]{3,2,1,0:T(8,128)(2,1)S(1)}, bf16[8,2,48,512]{3,2,1,0:T(8,128)(2,1)S(1)}, u32[]{:S(2)}, u32[]{:S(2)}) %collective-permute-start.38) | collective-permute-done | bytes 786464 | tf_op jit(solution)/shard_map/ppermute | solution.py:37
  148.3 8.1 %collective-permute-done.33 = bf16[2,4,32,512]{3,2,1,0:T(8,128)(2,1)S(1)} collective-permute-done((bf16[2,4,32,512]{3,2,1,0:T(8,128)(2,1)S(1)}, bf16[2,4,32,512]{3,2,1,0:T(8,128)(2,1)S(1)}, u32[]{:S(2)}, u32[]{:S(2)}) %collective-permute-start.33) | collective-permute-done | bytes 262176 | tf_op jit(solution)/shard_map/ppermute | solution.py:37
  158.7 2.8 %collective-permute-done.34 = bf16[4,32,512]{2,1,0:T(8,128)(2,1)S(1)} collective-permute-done((bf16[4,32,512]{2,1,0:T(8,128)(2,1)S(1)}, bf16[4,32,512]{2,1,0:T(8,128)(2,1)S(1)}, u32[]{:S(2)}, u32[]{:S(2)}) %collective-permute-start.34) | collective-permute-done | bytes 131104 | tf_op jit(solution)/shard_map/ppermute | solution.py:37
  162.0 6.6 %collective-permute-done.28 = bf16[2,4,48,512]{3,2,1,0:T(8,128)(2,1)S(1)} collective-permute-done((bf16[2,4,48,512]{3,2,1,0:T(8,128)(2,1)S(1)}, bf16[2,4,48,512]{3,2,1,0:T(8,128)(2,1)S(1)}, u32[]{:S(2)}, u32[]{:S(2)}) %collective-permute-start.28) | collective-permute-done | bytes 393248 | tf_op jit(solution)/shard_map/ppermute | solution.py:37
  169.2 5.4 %collective-permute-done.29 = bf16[4,48,512]{2,1,0:T(8,128)(2,1)S(1)} collective-permute-done((bf16[4,48,512]{2,1,0:T(8,128)(2,1)S(1)}, bf16[4,48,512]{2,1,0:T(8,128)(2,1)S(1)}, u32[]{:S(2)}, u32[]{:S(2)}) %collective-permute-start.29) | collective-permute-done | bytes 196640 | tf_op jit(solution)/shard_map/ppermute | solution.py:37
  175.9 5.5 %collective-permute-done.35 = bf16[2,80,512]{2,1,0:T(8,128)(2,1)S(1)} collective-permute-done((bf16[2,80,512]{2,1,0:T(8,128)(2,1)S(1)}, bf16[2,80,512]{2,1,0:T(8,128)(2,1)S(1)}, u32[]{:S(2)}, u32[]{:S(2)}) %collective-permute-start.35) | collective-permute-done | bytes 163872 | tf_op jit(solution)/shard_map/ppermute | solution.py:37
  181.6 4.3 %collective-permute-done.36 = bf16[1,80,512]{2,1,0:T(8,128)(2,1)S(1)} collective-permute-done((bf16[1,80,512]{2,1,0:T(8,128)(2,1)S(1)}, bf16[1,80,512]{2,1,0:T(8,128)(2,1)S(1)}, u32[]{:S(2)}, u32[]{:S(2)}) %collective-permute-start.36) | collective-permute-done | bytes 81952 | tf_op jit(solution)/shard_map/ppermute | solution.py:37
  (126 shorter events, 33.9 us)
Async XLA Ops:
  0.0 17.2 %collective-permute-start.4 = (bf16[4,192,4096]{2,1,0:T(8,128)(2,1)}, bf16[4,192,4096]{2,1,0:T(8,128)(2,1)}, u32[]{:S(2)}, u32[]{:S(2)}) collective-permute-start(bf16[4,192,4096]{2,1,0:T(8,128)(2,1)} %wg.1), channel_id=1, source_target_pairs={{0,8},{8,0},{16,24},{24,16},{1,9},{9,1},{17,25},{25,17},{2,10},{10... | collective-permute-start | bytes 18874376 | tf_op jit(solution)/shard_map/ppermute | solution.py:42
  17.2 10.6 %collective-permute-start.8 = (bf16[4,192,4096]{2,1,0:T(8,128)(2,1)}, bf16[4,192,4096]{2,1,0:T(8,128)(2,1)}, u32[]{:S(2)}, u32[]{:S(2)}) collective-permute-start(bf16[4,192,4096]{2,1,0:T(8,128)(2,1)} %wu), channel_id=1, source_target_pairs={{0,8},{8,0},{16,24},{24,16},{1,9},{9,1},{17,25},{25,17},{2,10},{10... | collective-permute-start | bytes 18874376 | tf_op jit(solution)/shard_map/ppermute | solution.py:42
  18.1 8.5 %collective-permute-start.6 = (bf16[4,48,512]{2,1,0:T(8,128)(2,1)S(1)}, bf16[4,48,512]{2,1,0:T(8,128)(2,1)S(1)}, u32[]{:S(2)}, u32[]{:S(2)}) collective-permute-start(bf16[4,48,512]{2,1,0:T(8,128)(2,1)S(1)} %pad_maximum_fusion.12), channel_id=1, source_target_pairs={{0,17},{8,25},{16,1},{24,9},{1,16},{9,24},{17,0},{25,8},{2,19},{10... | collective-permute-start | bytes 589832 | tf_op jit(solution)/shard_map/ppermute | solution.py:37
  27.8 15.6 %collective-permute-start.12 = (bf16[4,192,4096]{2,1,0:T(8,128)(2,1)}, bf16[4,192,4096]{2,1,0:T(8,128)(2,1)S(1)}, u32[]{:S(2)}, u32[]{:S(2)}) collective-permute-start(bf16[4,192,4096]{2,1,0:T(8,128)(2,1)} %wd.1), channel_id=1, source_target_pairs={{0,8},{8,0},{16,24},{24,16},{1,9},{9,1},{17,25},{25,17},{2,10},{10... | collective-permute-start | bytes 18874376 | tf_op jit(solution)/shard_map/ppermute | solution.py:42
  27.9 12.6 %collective-permute-start.9 = (bf16[8,48,512]{2,1,0:T(8,128)(2,1)S(1)}, bf16[8,48,512]{2,1,0:T(8,128)(2,1)S(1)}, u32[]{:S(2)}, u32[]{:S(2)}) collective-permute-start(bf16[8,48,512]{2,1,0:T(8,128)(2,1)S(1)} %pad_maximum_fusion.9), channel_id=1, source_target_pairs={{0,6},{8,14},{16,22},{24,30},{1,7},{9,15},{17,23},{25,31},{2,4},{1... | collective-permute-start | bytes 1179656 | tf_op jit(solution)/shard_map/ppermute | solution.py:37
  30.1 8.5 %collective-permute-start.11 = (bf16[8,32,512]{2,1,0:T(8,128)(2,1)S(1)}, bf16[8,32,512]{2,1,0:T(8,128)(2,1)S(1)}, u32[]{:S(2)}, u32[]{:S(2)}) collective-permute-start(bf16[8,32,512]{2,1,0:T(8,128)(2,1)S(1)} %fusion.3), channel_id=1, source_target_pairs={{0,17},{8,25},{16,1},{24,9},{1,16},{9,24},{17,0},{25,8},{2,19},{10... | collective-permute-start | bytes 786440 | tf_op jit(solution)/shard_map/ppermute | solution.py:37
  32.1 11.3 %collective-permute-start.10 = (bf16[8,48,512]{2,1,0:T(8,128)(2,1)S(1)}, bf16[8,48,512]{2,1,0:T(8,128)(2,1)S(1)}, u32[]{:S(2)}, u32[]{:S(2)}) collective-permute-start(bf16[8,48,512]{2,1,0:T(8,128)(2,1)S(1)} %pad_maximum_fusion.10), channel_id=1, source_target_pairs={{0,16},{8,24},{16,0},{24,8},{1,17},{9,25},{17,1},{25,9},{2,18},{10... | collective-permute-start | bytes 1179656 | tf_op jit(solution)/shard_map/ppermute | solution.py:37
  43.5 13.1 %collective-permute-start.21 = (bf16[16,32,512]{2,1,0:T(8,128)(2,1)S(1)}, bf16[16,32,512]{2,1,0:T(8,128)(2,1)S(1)}, u32[]{:S(2)}, u32[]{:S(2)}) collective-permute-start(bf16[16,32,512]{2,1,0:T(8,128)(2,1)S(1)} %pad_maximum_fusion.6), channel_id=1, source_target_pairs={{0,2},{8,10},{16,18},{24,26},{1,3},{9,11},{17,19},{25,27},{2,0},{1... | collective-permute-start | bytes 1572872 | tf_op jit(solution)/shard_map/ppermute | solution.py:37
  44.2 18.4 %collective-permute-start.14 = (bf16[16,48,512]{2,1,0:T(8,128)(2,1)S(1)}, bf16[16,48,512]{2,1,0:T(8,128)(2,1)S(1)}, u32[]{:S(2)}, u32[]{:S(2)}) collective-permute-start(bf16[16,48,512]{2,1,0:T(8,128)(2,1)S(1)} %pad_maximum_fusion), channel_id=1, source_target_pairs={{0,17},{8,25},{16,1},{24,9},{1,16},{9,24},{17,0},{25,8},{2,19},{10... | collective-permute-start | bytes 2359304 | tf_op jit(solution)/shard_map/ppermute | solution.py:37
  44.2 19.6 %collective-permute-start.13 = (bf16[16,48,512]{2,1,0:T(8,128)(2,1)S(1)}, bf16[16,48,512]{2,1,0:T(8,128)(2,1)S(1)}, u32[]{:S(2)}, u32[]{:S(2)}) collective-permute-start(bf16[16,48,512]{2,1,0:T(8,128)(2,1)S(1)} %pad_maximum_fusion), channel_id=1, source_target_pairs={{0,16},{8,24},{16,0},{24,8},{1,17},{9,25},{17,1},{25,9},{2,18},{10... | collective-permute-start | bytes 2359304 | tf_op jit(solution)/shard_map/ppermute | solution.py:37
  46.2 20.4 %collective-permute-start.18 = (bf16[16,48,512]{2,1,0:T(8,128)(2,1)S(1)}, bf16[16,48,512]{2,1,0:T(8,128)(2,1)S(1)}, u32[]{:S(2)}, u32[]{:S(2)}) collective-permute-start(bf16[16,48,512]{2,1,0:T(8,128)(2,1)S(1)} %pad_maximum_fusion.1), channel_id=1, source_target_pairs={{0,96},{8,104},{16,112},{24,120},{1,97},{9,105},{17,113},{25,121},... | collective-permute-start | bytes 2359304 | tf_op jit(solution)/shard_map/ppermute | solution.py:37
  49.0 18.4 %collective-permute-start.17 = (bf16[16,48,512]{2,1,0:T(8,128)(2,1)S(1)}, bf16[16,48,512]{2,1,0:T(8,128)(2,1)S(1)}, u32[]{:S(2)}, u32[]{:S(2)}) collective-permute-start(bf16[16,48,512]{2,1,0:T(8,128)(2,1)S(1)} %pad_maximum_fusion.1), channel_id=1, source_target_pairs={{0,32},{8,40},{16,48},{24,56},{1,33},{9,41},{17,49},{25,57},{2,34}... | collective-permute-start | bytes 2359304 | tf_op jit(solution)/shard_map/ppermute | solution.py:37
  56.6 16.1 %collective-permute-start.22 = (bf16[16,32,512]{2,1,0:T(8,128)(2,1)S(1)}, bf16[16,32,512]{2,1,0:T(8,128)(2,1)S(1)}, u32[]{:S(2)}, u32[]{:S(2)}) collective-permute-start(bf16[16,32,512]{2,1,0:T(8,128)(2,1)S(1)} %pad_maximum_fusion.6), channel_id=1, source_target_pairs={{0,6},{8,14},{16,22},{24,30},{1,7},{9,15},{17,23},{25,31},{2,4},{1... | collective-permute-start | bytes 1572872 | tf_op jit(solution)/shard_map/ppermute | solution.py:37
  62.6 18.6 %collective-permute-start.23 = (bf16[16,32,512]{2,1,0:T(8,128)(2,1)S(1)}, bf16[16,32,512]{2,1,0:T(8,128)(2,1)S(1)}, u32[]{:S(2)}, u32[]{:S(2)}) collective-permute-start(bf16[16,32,512]{2,1,0:T(8,128)(2,1)S(1)} %collective-permute-done.21), channel_id=1, source_target_pairs={{0,6},{8,14},{16,22},{24,30},{1,7},{9,15},{17,23},{25,31},{2,4},{1... | collective-permute-start | bytes 1572872 | tf_op jit(solution)/shard_map/ppermute | solution.py:37
  63.9 17.3 %collective-permute-start.16 = (bf16[8,48,512]{2,1,0:T(8,128)(2,1)S(1)}, bf16[8,48,512]{2,1,0:T(8,128)(2,1)S(1)}, u32[]{:S(2)}, u32[]{:S(2)}) collective-permute-start(bf16[8,48,512]{2,1,0:T(8,128)(2,1)S(1)} %slice.159), channel_id=1, source_target_pairs={{0,16},{8,24},{16,0},{24,8},{1,17},{9,25},{17,1},{25,9},{2,18},{10... | collective-permute-start | bytes 1179656 | tf_op jit(solution)/shard_map/ppermute | solution.py:37
  66.6 14.6 %collective-permute-start.15 = (bf16[8,48,512]{2,1,0:T(8,128)(2,1)S(1)}, bf16[8,48,512]{2,1,0:T(8,128)(2,1)S(1)}, u32[]{:S(2)}, u32[]{:S(2)}) collective-permute-start(bf16[8,48,512]{2,1,0:T(8,128)(2,1)S(1)} %slice.158), channel_id=1, source_target_pairs={{0,17},{8,25},{16,1},{24,9},{1,16},{9,24},{17,0},{25,8},{2,19},{10... | collective-permute-start | bytes 1179656 | tf_op jit(solution)/shard_map/ppermute | solution.py:37
  67.4 13.8 %collective-permute-start.20 = (bf16[8,48,512]{2,1,0:T(8,128)(2,1)S(1)}, bf16[8,48,512]{2,1,0:T(8,128)(2,1)S(1)}, u32[]{:S(2)}, u32[]{:S(2)}) collective-permute-start(bf16[8,48,512]{2,1,0:T(8,128)(2,1)S(1)} %slice.161), channel_id=1, source_target_pairs={{0,32},{8,40},{16,48},{24,56},{1,33},{9,41},{17,49},{25,57},{2,34}... | collective-permute-start | bytes 1179656 | tf_op jit(solution)/shard_map/ppermute | solution.py:37
  72.7 9.0 %collective-permute-start.19 = (bf16[8,48,512]{2,1,0:T(8,128)(2,1)S(1)}, bf16[8,48,512]{2,1,0:T(8,128)(2,1)S(1)}, u32[]{:S(2)}, u32[]{:S(2)}) collective-permute-start(bf16[8,48,512]{2,1,0:T(8,128)(2,1)S(1)} %slice.160), channel_id=1, source_target_pairs={{0,96},{8,104},{16,112},{24,120},{1,97},{9,105},{17,113},{25,121},... | collective-permute-start | bytes 1179656 | tf_op jit(solution)/shard_map/ppermute | solution.py:37
  108.3 15.8 %collective-permute-start.37 = (bf16[4,2,48,512]{3,2,1,0:T(8,128)(2,1)S(1)}, bf16[4,2,48,512]{3,2,1,0:T(8,128)(2,1)S(1)}, u32[]{:S(2)}, u32[]{:S(2)}) collective-permute-start(bf16[4,2,48,512]{3,2,1,0:T(8,128)(2,1)S(1)} %get-tuple-element.79), channel_id=1, source_target_pairs={{0,96},{8,104},{16,112},{24,120},{1,97},{9,105},{17,113},{25,121},... | collective-permute-start | bytes 1179656 | tf_op jit(solution)/shard_map/ppermute | solution.py:37
  111.1 20.0 %collective-permute-start.30 = (bf16[4,4,32,512]{3,2,1,0:T(8,128)(2,1)S(1)}, bf16[4,4,32,512]{3,2,1,0:T(8,128)(2,1)S(1)}, u32[]{:S(2)}, u32[]{:S(2)}) collective-permute-start(bf16[4,4,32,512]{3,2,1,0:T(8,128)(2,1)S(1)} %get-tuple-element.75), channel_id=1, source_target_pairs={{0,6},{8,14},{16,22},{24,30},{1,7},{9,15},{17,23},{25,31},{2,4},{1... | collective-permute-start | bytes 1572872 | tf_op jit(solution)/shard_map/ppermute | solution.py:37
  121.1 9.9 %collective-permute-start.39 = (bf16[4,2,48,512]{3,2,1,0:T(8,128)(2,1)S(1)}, bf16[4,2,48,512]{3,2,1,0:T(8,128)(2,1)S(1)}, u32[]{:S(2)}, u32[]{:S(2)}) collective-permute-start(bf16[4,2,48,512]{3,2,1,0:T(8,128)(2,1)S(1)} %get-tuple-element.83), channel_id=1, source_target_pairs={{0,32},{8,40},{16,48},{24,56},{1,33},{9,41},{17,49},{25,57},{2,34}... | collective-permute-start | bytes 1179656 | tf_op jit(solution)/shard_map/ppermute | solution.py:37
  121.2 11.3 %collective-permute-start.24 = (bf16[2,4,48,512]{3,2,1,0:T(8,128)(2,1)S(1)}, bf16[2,4,48,512]{3,2,1,0:T(8,128)(2,1)S(1)}, u32[]{:S(2)}, u32[]{:S(2)}) collective-permute-start(bf16[2,4,48,512]{3,2,1,0:T(8,128)(2,1)S(1)} %get-tuple-element.67), channel_id=1, source_target_pairs={{0,17},{8,25},{16,1},{24,9},{1,16},{9,24},{17,0},{25,8},{2,19},{10... | collective-permute-start | bytes 1179656 | tf_op jit(solution)/shard_map/ppermute | solution.py:37
  121.9 11.3 %collective-permute-start.26 = (bf16[2,4,48,512]{3,2,1,0:T(8,128)(2,1)S(1)}, bf16[2,4,48,512]{3,2,1,0:T(8,128)(2,1)S(1)}, u32[]{:S(2)}, u32[]{:S(2)}) collective-permute-start(bf16[2,4,48,512]{3,2,1,0:T(8,128)(2,1)S(1)} %get-tuple-element.71), channel_id=1, source_target_pairs={{0,16},{8,24},{16,0},{24,8},{1,17},{9,25},{17,1},{25,9},{2,18},{10... | collective-permute-start | bytes 1179656 | tf_op jit(solution)/shard_map/ppermute | solution.py:37
  124.1 11.6 %collective-permute-start.32 = (bf16[4,4,32,512]{3,2,1,0:T(8,128)(2,1)S(1)}, bf16[4,4,32,512]{3,2,1,0:T(8,128)(2,1)S(1)}, u32[]{:S(2)}, u32[]{:S(2)}) collective-permute-start(bf16[4,4,32,512]{3,2,1,0:T(8,128)(2,1)S(1)} %get-tuple-element.76), channel_id=1, source_target_pairs={{0,6},{8,14},{16,22},{24,30},{1,7},{9,15},{17,23},{25,31},{2,4},{1... | collective-permute-start | bytes 1572872 | tf_op jit(solution)/shard_map/ppermute | solution.py:37
  131.0 14.8 %collective-permute-start.38 = (bf16[8,2,48,512]{3,2,1,0:T(8,128)(2,1)S(1)}, bf16[8,2,48,512]{3,2,1,0:T(8,128)(2,1)S(1)}, u32[]{:S(2)}, u32[]{:S(2)}) collective-permute-start(bf16[8,2,48,512]{3,2,1,0:T(8,128)(2,1)S(1)} %pad_maximum_fusion.4), channel_id=1, source_target_pairs={{0,32},{8,40},{16,48},{24,56},{1,33},{9,41},{17,49},{25,57},{2,34}... | collective-permute-start | bytes 2359304 | tf_op jit(solution)/shard_map/ppermute | solution.py:37
  132.3 9.3 %collective-permute-start.31 = (bf16[4,4,32,512]{3,2,1,0:T(8,128)(2,1)S(1)}, bf16[4,4,32,512]{3,2,1,0:T(8,128)(2,1)S(1)}, u32[]{:S(2)}, u32[]{:S(2)}) collective-permute-start(bf16[4,4,32,512]{3,2,1,0:T(8,128)(2,1)S(1)} %add.139), channel_id=1, source_target_pairs={{0,2},{8,10},{16,18},{24,26},{1,3},{9,11},{17,19},{25,27},{2,0},{1... | collective-permute-start | bytes 1572872 | tf_op jit(solution)/shard_map/ppermute | solution.py:37
  132.5 14.3 %collective-permute-start.40 = (bf16[8,2,48,512]{3,2,1,0:T(8,128)(2,1)S(1)}, bf16[8,2,48,512]{3,2,1,0:T(8,128)(2,1)S(1)}, u32[]{:S(2)}, u32[]{:S(2)}) collective-permute-start(bf16[8,2,48,512]{3,2,1,0:T(8,128)(2,1)S(1)} %pad_maximum_fusion.5), channel_id=1, source_target_pairs={{0,96},{8,104},{16,112},{24,120},{1,97},{9,105},{17,113},{25,121},... | collective-permute-start | bytes 2359304 | tf_op jit(solution)/shard_map/ppermute | solution.py:37
  133.3 25.1 %collective-permute-start.25 = (bf16[4,4,48,512]{3,2,1,0:T(8,128)(2,1)S(1)}, bf16[4,4,48,512]{3,2,1,0:T(8,128)(2,1)S(1)}, u32[]{:S(2)}, u32[]{:S(2)}) collective-permute-start(bf16[4,4,48,512]{3,2,1,0:T(8,128)(2,1)S(1)} %pad_maximum_fusion.2), channel_id=1, source_target_pairs={{0,16},{8,24},{16,0},{24,8},{1,17},{9,25},{17,1},{25,9},{2,18},{10... | collective-permute-start | bytes 2359304 | tf_op jit(solution)/shard_map/ppermute | solution.py:37
  135.7 22.6 %collective-permute-start.27 = (bf16[4,4,48,512]{3,2,1,0:T(8,128)(2,1)S(1)}, bf16[4,4,48,512]{3,2,1,0:T(8,128)(2,1)S(1)}, u32[]{:S(2)}, u32[]{:S(2)}) collective-permute-start(bf16[4,4,48,512]{3,2,1,0:T(8,128)(2,1)S(1)} %pad_maximum_fusion.3), channel_id=1, source_target_pairs={{0,17},{8,25},{16,1},{24,9},{1,16},{9,24},{17,0},{25,8},{2,19},{10... | collective-permute-start | bytes 2359304 | tf_op jit(solution)/shard_map/ppermute | solution.py:37
  141.8 14.6 %collective-permute-start.33 = (bf16[2,4,32,512]{3,2,1,0:T(8,128)(2,1)S(1)}, bf16[2,4,32,512]{3,2,1,0:T(8,128)(2,1)S(1)}, u32[]{:S(2)}, u32[]{:S(2)}) collective-permute-start(bf16[2,4,32,512]{3,2,1,0:T(8,128)(2,1)S(1)} %slice.169), channel_id=1, source_target_pairs={{0,17},{8,25},{16,1},{24,9},{1,16},{9,24},{17,0},{25,8},{2,19},{10... | collective-permute-start | bytes 786440 | tf_op jit(solution)/shard_map/ppermute | solution.py:37
  147.2 14.4 %collective-permute-start.41 = (bf16[2,4,48,512]{3,2,1,0:T(8,128)(2,1)S(1)}, bf16[2,4,48,512]{3,2,1,0:T(8,128)(2,1)S(1)}, u32[]{:S(2)}, u32[]{:S(2)}) collective-permute-start(bf16[2,4,48,512]{3,2,1,0:T(8,128)(2,1)S(1)} %pad_maximum_fusion.7), channel_id=1, source_target_pairs={{0,16},{8,24},{16,0},{24,8},{1,17},{9,25},{17,1},{25,9},{2,18},{10... | collective-permute-start | bytes 1179656 | tf_op jit(solution)/shard_map/ppermute | solution.py:37
  158.5 10.1 %collective-permute-start.28 = (bf16[2,4,48,512]{3,2,1,0:T(8,128)(2,1)S(1)}, bf16[2,4,48,512]{3,2,1,0:T(8,128)(2,1)S(1)}, u32[]{:S(2)}, u32[]{:S(2)}) collective-permute-start(bf16[2,4,48,512]{3,2,1,0:T(8,128)(2,1)S(1)} %add_convert_fusion.3), channel_id=1, source_target_pairs={{0,6},{8,14},{16,22},{24,30},{1,7},{9,15},{17,23},{25,31},{2,4},{1... | collective-permute-start | bytes 1179656 | tf_op jit(solution)/shard_map/ppermute | solution.py:37
  (16 other events, 120.5 us)
